TPU v7x, 32 devices: a whole 2x2x4 slice. The times are simulated.
32 devices in a mesh: segment: 2 (over y), fsdp: 4 (over z), seq: 4 (over x, core).
Axes of the slice: x: 2, y: 2, z: 4, core: 2. Of those that a mesh axis runs over, the one named last changes fastest.
Arguments:
- branch_x: bfloat16 [8, 512, 4096], P(('segment', 'fsdp'), 'seq'), may hold values from -6 to 6
- positions: int32 [8, 512], P(('segment', 'fsdp'), 'seq'), may hold values from 0 to 511, as said below
- teacher_held: bfloat16 [8, 512, 4096], P(('segment', 'fsdp'), 'seq'), may hold values from -6 to 6
- gate_weights: bfloat16 [32, 2, 128, 128], P('fsdp'), may hold values from -0.5 to 0.5
- gate_bias: float32 [2, 4096], replicated, may hold values from -4 to 4
- conv_weight: float32 [4, 4096], replicated, may hold values from -3 to 3
- conv_bias: float32 [4096], replicated, may hold values from -3 to 3
- decay_rate: float32 [4096], replicated, as said below
Outputs:
- student_out: bfloat16 [8, 512, 4096], P(('segment', 'fsdp'), 'seq')
- token_loss: float32 [8, 512], P(('segment', 'fsdp'), 'seq')
Inputs may be any that keep to these rules, and one draw needn't show every extreme that they name: `positions`: within each sequence a token's position is 0 at a document start and one more than the previous token's position otherwise; every sequence begins with a document start; the first sequence is one whole document. `decay_rate`: rates are positive.
All inputs are finite; a program needn't handle non-finite values.
Results may differ from a plain program's by a relative error of at most 0.0055.
Values may be sent and summed in bfloat16 or wider, within the bound.
No kernel may reach another device: no remote copies, remote signals or barrier semaphores. Data moves between devices by JAX's collectives and lax.ppermute only.
A program may use at most 64 MiB of HBM per device.

v0:
```python
import jax
import jax.numpy as jnp
from jax import lax
from jax.sharding import PartitionSpec as P

HEADS = 32
HS = 128


def prefix(value, axis, combine, identity):
    devices, here = (lax.axis_size(axis), lax.axis_index(axis))
    everything = jax.tree.map(lambda part: lax.all_gather(part, axis), value)
    start = jax.tree.map(
        lambda part, zero: jnp.broadcast_to(jnp.asarray(zero, part.dtype), part.shape),
        value,
        identity,
    )

    def hop(k, before):
        reached = k < here
        new = combine(before, jax.tree.map(lambda part: part[k], everything))
        return jax.tree.map(lambda a, b: jnp.where(reached, a, b), new, before)

    return lax.fori_loop(0, devices, hop, start)


def from_partner(value, axis, apart):
    return lax.ppermute(value, axis, [(i, i ^ 1 << apart) for i in range(lax.axis_size(axis))])


def from_behind(value, axis, steps):
    count = lax.axis_size(axis)
    leading, last = (max(0, -steps), min(count, count - steps))
    return lax.ppermute(value, axis, [(source, source + steps) for source in range(leading, last)])


def combine(former, latter):
    return (former[0] * latter[0], latter[0] * former[1] + latter[1])


def recurrence(conv_rows, gate_pre_x, gate_pre_a, bias_pair, rates, places):
    group = conv_rows.shape[0]
    tokens = conv_rows.shape[1]
    width = conv_rows.shape[2]
    blocks = tokens // 8
    seq_total = lax.axis_size("seq") * tokens
    gate_x = jax.nn.sigmoid(gate_pre_x + bias_pair[0])
    gate_a = jax.nn.sigmoid(gate_pre_a + bias_pair[1])
    log_a = -8.0 * gate_a * rates / seq_total
    reset = (places == 0)[:, :, None]
    decay = jnp.where(reset, jnp.float32(0.0), jnp.exp(log_a))
    scale = jnp.where(reset, jnp.float32(1.0), jnp.sqrt(-jnp.expm1(2.0 * log_a)))
    drive = conv_rows.astype(jnp.float32) * gate_x * scale
    decay_blocks = decay.reshape(group, blocks, 8, width)
    drive_blocks = drive.reshape(group, blocks, 8, width)
    running_prod = jnp.ones((group, blocks, width), jnp.float32)
    running_state = jnp.zeros((group, blocks, width), jnp.float32)
    prod_list = []
    state_list = []
    for inner in range(8):
        step_decay = decay_blocks[:, :, inner, :]
        running_prod = running_prod * step_decay
        running_state = step_decay * running_state + drive_blocks[:, :, inner, :]
        prod_list.append(running_prod)
        state_list.append(running_state)
    block_prod = jnp.swapaxes(running_prod, 0, 1)
    block_state = jnp.swapaxes(running_state, 0, 1)

    def across(carry, pair):
        after = combine(carry, pair)
        return (after, carry)

    start = (jnp.ones((group, width), jnp.float32), jnp.zeros((group, width), jnp.float32))
    ending, befores = lax.scan(across, start, (block_prod, block_state))
    identity = (jnp.ones_like(ending[0]), jnp.zeros_like(ending[1]))
    incoming = prefix(ending, "seq", combine, identity)
    entering = befores[1] + befores[0] * incoming[1][None, :, :]
    entering = jnp.swapaxes(entering, 0, 1)[:, :, None, :]
    products = jnp.stack(prod_list, axis=2)
    local_state = jnp.stack(state_list, axis=2)
    full = local_state + products * entering
    return full.reshape(group, tokens, width).astype(jnp.bfloat16)


def local(
    branch_x, positions, teacher_held, gate_weights, gate_bias, conv_weight, conv_bias, decay_rate
):
    tokens = branch_x.shape[1]
    width = branch_x.shape[2]
    target = from_partner(teacher_held, "segment", 0)
    previous = from_behind(branch_x[:, -3:, :], "seq", 1)
    extended = jnp.concatenate([previous, branch_x], axis=1).astype(jnp.float32)
    conv = jnp.zeros((1, tokens, width), jnp.float32) + conv_bias
    for lag_steps in range(4):
        valid = (positions >= lag_steps).astype(jnp.float32)[:, :, None]
        conv = (
            conv
            + conv_weight[lag_steps]
            * extended[:, 3 - lag_steps : 3 - lag_steps + tokens, :]
            * valid
        )
    conv_rounded = conv.astype(jnp.bfloat16)
    by_heads = conv_rounded.reshape(1, tokens, HEADS, HS)
    preact = jnp.einsum(
        "nthi,hgij->ngthj",
        by_heads,
        lax.all_gather(gate_weights, "fsdp", axis=0, tiled=True),
        preferred_element_type=jnp.float32,
    )
    student = recurrence(
        conv_rounded,
        preact[:, 0].reshape(1, tokens, width),
        preact[:, 1].reshape(1, tokens, width),
        gate_bias,
        decay_rate,
        positions,
    )
    student_f = student.astype(jnp.float32)
    normed = student_f * lax.rsqrt(jnp.mean(student_f * student_f, axis=-1, keepdims=True) + 1e-06)
    token_loss = jnp.mean((normed - target.astype(jnp.float32)) ** 2, axis=-1)
    return (student, token_loss)


def solution(mesh):
    in_specs = (
        P(("segment", "fsdp"), "seq", None),
        P(("segment", "fsdp"), "seq"),
        P(("segment", "fsdp"), "seq", None),
        P("fsdp", None, None, None),
        P(),
        P(),
        P(),
        P(),
    )
    out_specs = (P(("segment", "fsdp"), "seq", None), P(("segment", "fsdp"), "seq"))
    return jax.shard_map(local, mesh=mesh, in_specs=in_specs, out_specs=out_specs, check_vma=False)
```

profile of v0, /device:TPU:0, one launch (start us, length us, event | category | flops | bytes accessed | tf_op | source)
XLA Modules:
  0.0 158.5 jit_solution(11214923404827814401)
XLA Ops:
  7.2 0.7 all-gather.6.cloned.1.call-update
  7.9 0.9 slice.90
  8.8 2.4 %collective-permute-start = (bf16[1,3,4096]{2,1,0:T(4,128)(2,1)S(1)}, bf16[1,3,4096]{2,1,0:T(4,128)(2,1)S(1)}, u32[]{:S(2)}, u32[]{:S(2)}) collective-permute-start(bf16[1,3,4096]{2,1,0:T(4,128)(2,1)S(1)} %slice.90), channel_id=1, source_target_pairs={{0,1},{1,2},{2,3},{4,5},{5,6},{6,7},{8,9},{9,10},{10,11},{12,13},{... | collective-permute-start | bytes 73736 | tf_op jit(solution)/shard_map/ppermute | solution.py:34
  11.1 2.4 %collective-permute-start.1 = (bf16[1,128,4096]{2,1,0:T(8,128)(2,1)}, bf16[1,128,4096]{2,1,0:T(8,128)(2,1)}, u32[]{:S(2)}, u32[]{:S(2)}) collective-permute-start(bf16[1,128,4096]{2,1,0:T(8,128)(2,1)} %param.14), channel_id=1, source_target_pairs={{0,16},{16,0},{1,17},{17,1},{2,18},{18,2},{3,19},{19,3},{4,20},{20... | collective-permute-start | bytes 3145736 | tf_op jit(solution)/shard_map/ppermute | solution.py:28
  13.6 0.7 broadcast_multiply_fusion
  14.3 0.9 fusion.43
  15.1 1.1 fusion.42
  16.2 0.7 compare_reduce_fusion
  17.0 1.5 maximum_convert_fusion
  18.5 1.4 fusion.45
  20.2 38.1 %all-gather.6.cloned.1.call-done = bf16[32,2,128,128]{3,2,1,0:T(8,128)(2,1)} async-done(((bf16[8,2,128,128]{3,2,1,0:T(8,128)(2,1)}), bf16[32,2,128,128]{3,2,1,0:T(8,128)(2,1)}) %all-gather.6.cloned.1.call-update) | async-done | bytes 2097168 | tf_op jit(solution)/shard_map/all_gather | solution.py:107
  58.2 4.1 %copy.30 = bf16[32,2,128,128]{2,3,1,0:T(8,128)(2,1)} copy(bf16[32,2,128,128]{3,2,1,0:T(8,128)(2,1)} %all-gather.6.cloned.1.call-done) | data formatting | bytes 4194304 | tf_op jit(solution)/shard_map/all_gather | solution.py:107
  62.3 2.3 %fusion.11 = f32[32,128,256]{1,2,0:S(1)} fusion(bf16[32,128,256]{1,2,0:T(8,128)(2,1)} %bitcast.233, bf16[128,32,128]{2,1,0:T(8,128)(2,1)S(1)} %bitcast.236), kind=kOutput, calls=%fused_computation.33 | convolution fusion | flops 268435456 | bytes 7340032
  64.6 2.3 %fusion.41 = (f32[1,1,128,32,128]{2,4,1,3,0:T(8,128)}, f32[1,1,128,32,128]{2,4,1,3,0:T(8,128)}) fusion(f32[1,2,128,32,128]{2,4,1,3,0:T(8,128)S(1)} %bitcast.232), kind=kLoop, calls=%fused_computation.96 | loop fusion | bytes 8388608 | tf_op jit(solution)/shard_map/slice | solution.py:112
  66.9 3.1 %copy.31 = f32[1,1,128,32,128]{4,3,0,2,1:T(8,128)} copy(f32[1,1,128,32,128]{2,4,1,3,0:T(8,128)} %get-tuple-element.229) | data formatting | bytes 4194304 | tf_op jit(solution)/shard_map/slice | solution.py:113
  70.1 7.7 %broadcast_select_fusion.4 = f32[1,16,8,4096]{3,0,2,1:T(1,128)S(1)} fusion(pred[16,8]{1,0:T(8,128)(4,1)S(1)} %broadcast_in_dim.42, f32[1,16,8,4096]{3,0,2,1:T(1,128)} %bitcast.234, f32[4096]{0:T(1024)S(1)} %broadcast_multiply_fusion, f32[4096]{0:T(1024)S(1)} %bitcast.242), kind=kLoop, calls=%fused_computation.11 | loop fusion | flops 3670016 | bytes 4227200 | tf_op jit(solution)/shard_map/jit(_where)/select_n | solution.py:51
  77.7 2.2 %fusion.13 = f32[16,1,4096]{2,1,0:T(1,128)} fusion(f32[1,16,8,4096]{3,0,2,1:T(1,128)S(1)} %broadcast_select_fusion.4), kind=kLoop, calls=%fused_computation.37 | loop fusion | flops 458752 | bytes 2359296 | tf_op jit(solution)/shard_map/mul | solution.py:62
  80.0 3.2 %bitcast_multiply_fusion.29 = (f32[1,16,1,4096]{3,2,1,0:T(1,128)}, f32[1,16,1,4096]{3,2,1,0:T(1,128)}, f32[1,16,1,4096]{3,2,1,0:T(1,128)}, f32[1,16,1,4096]{3,2,...) fusion(f32[1,16,8,4096]{3,0,2,1:T(1,128)S(1)} %broadcast_select_fusion.4), kind=kLoop, calls=%fused_computation.77 | loop fusion | flops 458752 | bytes 3932160 | tf_op jit(solution)/shard_map/mul | solution.py:62
  83.2 2.9 %copy.34 = f32[1,128,4096]{2,1,0:T(8,128)} copy(f32[1,128,4096]{1,2,0:T(8,128)} %bitcast.231) | data formatting | bytes 4194304 | tf_op jit(solution)/shard_map/reshape;squeeze | solution.py:113
  86.1 2.9 %copy.33 = f32[1,128,4096]{2,1,0:T(8,128)} copy(f32[1,128,4096]{1,2,0:T(8,128)} %bitcast.235) | data formatting | bytes 4194304 | tf_op jit(solution)/shard_map/reshape;squeeze | solution.py:112
  89.0 5.2 %multiply_bitcast_fusion = f32[1,16,8,4096]{3,2,1,0:T(8,128)S(1)} fusion(f32[1,128,4096]{2,1,0:T(8,128)} %copy.34, f32[1,128,4096]{2,1,0:T(8,128)} %copy.33, f32[4096]{0:T(1024)S(1)} %broadcast_multiply_fusion, f32[4096]{0:T(1024)S(1)} %bitcast.243, f32[4096]{0:T(1024)S(1)} %bitcast.252, pred[128]{0:T(512)(128)(4,1)S(1)} %get-tuple-element.237, ...), kind=kLoop, calls=%fused_computation.31 | loop fusion | flops 14680064 | bytes 14813312 | tf_op jit(solution)/shard_map/reshape | solution.py:55
  94.3 2.1 %fusion.16 = f32[16,1,4096]{2,1,0:T(1,128)S(1)} fusion(f32[1,16,8,4096]{3,2,1,0:T(8,128)S(1)} %multiply_bitcast_fusion, f32[1,16,8,4096]{3,0,2,1:T(1,128)S(1)} %copy-done.1), kind=kLoop, calls=%fused_computation.40 | loop fusion | flops 1048576 | bytes 4456448 | tf_op jit(solution)/shard_map/add | solution.py:63
  96.8 13.5 %while.31 = (s32[]{:T(128)}, f32[1,4096]{1,0:T(1,128)S(1)}, f32[1,4096]{1,0:T(1,128)S(1)}, f32[16,1,4096]{2,1,0:T(1,128)S(1)}, f32[16,1,4096]{2,1,0:T(1,128)S(1)...) while((s32[]{:T(128)}, f32[1,4096]{1,0:T(1,128)S(1)}, ...), condition=%wide.region_1.2_spmd.clone, body=%wide.region_0.1_spmd.clone.sunk | while | flops 28675 | bytes 163952 | solution.py:74
  96.8 0.8 bitcast_add_fusion.3
  97.7 0.8 bitcast_add_fusion.3
  98.5 0.8 bitcast_add_fusion.3
  99.4 0.8 bitcast_add_fusion.3
  100.2 0.8 bitcast_add_fusion.3
  101.0 0.8 bitcast_add_fusion.3
  101.9 0.8 bitcast_add_fusion.3
  102.7 0.8 bitcast_add_fusion.3
  103.6 0.8 bitcast_add_fusion.3
  104.4 0.8 bitcast_add_fusion.3
  105.3 0.8 bitcast_add_fusion.3
  106.1 0.8 bitcast_add_fusion.3
  107.0 0.8 bitcast_add_fusion.3
  107.8 0.8 bitcast_add_fusion.3
  108.6 0.8 bitcast_add_fusion.3
  109.5 0.8 bitcast_add_fusion.3
  110.3 5.2 %all-gather.2 = f32[4,1,4096]{2,1,0:T(1,128)S(1)} all-gather(f32[1,1,4096]{2,1,0:T(1,128)S(1)} %bitcast.239), channel_id=2, replica_groups=mesh['segment'=2,'fsdp'=4,'seq'=4] {'seq'}, dimensions={0}, use_global_device_ids=true | all-gather | bytes 81920 | tf_op jit(solution)/shard_map/all_gather | solution.py:12
  115.5 5.2 %all-gather.3 = f32[4,1,4096]{2,1,0:T(1,128)S(1)} all-gather(f32[1,1,4096]{2,1,0:T(1,128)S(1)} %bitcast.240), channel_id=3, replica_groups=mesh['segment'=2,'fsdp'=4,'seq'=4] {'seq'}, dimensions={0}, use_global_device_ids=true | all-gather | bytes 81920 | tf_op jit(solution)/shard_map/all_gather | solution.py:12
  121.0 0.3 multiply_add_fusion
  121.5 6.7 %stack.10 = f32[1,16,8,4096]{3,2,1,0:T(8,128)} concatenate(f32[1,16,1,4096]{3,2,1,0:T(1,128)S(1)} %slice_bitcast_fusion, f32[1,16,1,4096]{3,2,1,0:T(1,128)} %get-tuple-element.223, f32[1,16,1,4096]{3,2,1,0:T(1,128)} %get-tuple-element.222, f32[1,16,1,4096]{3,2,1,0:T(1,128)} %get-tuple-element.221, f32[1,16,1,4096]{3,2,1,0:T(1,128)} %get-tuple-element.220, ...), dimensions={2} | concatenate | bytes 4194304 | tf_op jit(solution)/shard_map/stack | solution.py:79
  128.1 10.9 %fusion.29 = (f32[1,16,1,4096]{3,2,1,0:T(1,128)S(1)}, f32[1,16,1,4096]{3,2,1,0:T(1,128)S(1)}, f32[1,16,1,4096]{3,2,1,0:T(1,128)S(1)}, f32[1,16,1,4096]{3,2,1,0:T...) fusion(f32[1,16,8,4096]{3,2,1,0:T(8,128)} %copy-done.3, ...), kind=kLoop, calls=%fused_computation.79 | loop fusion | flops 1048576 | bytes 6291456 | tf_op jit(solution)/shard_map/add | solution.py:63
  139.0 6.5 %stack.8 = f32[1,16,8,4096]{3,2,1,0:T(8,128)} concatenate(f32[1,16,1,4096]{3,2,1,0:T(1,128)} %get-tuple-element.216, f32[1,16,1,4096]{3,2,1,0:T(1,128)} %get-tuple-element.215, f32[1,16,1,4096]{3,2,1,0:T(1,128)} %get-tuple-element.214, f32[1,16,1,4096]{3,2,1,0:T(1,128)} %get-tuple-element.213, f32[1,16,1,4096]{3,2,1,0:T(1,128)S(1)} %get-tuple-element.212, ...), dimensions={2} | concatenate | bytes 4194304 | tf_op jit(solution)/shard_map/stack | solution.py:80
  145.5 2.0 %multiply_reduce_fusion.1 = f32[16,8]{1,0:T(8,128)S(1)} fusion(f32[1,16,8,4096]{3,2,1,0:T(8,128)} %stack.8, f32[1,16,8,4096]{3,2,1,0:T(8,128)S(1)} %copy-done.4, f32[16,4096]{1,0:T(8,128)S(1)} %bitcast.237), kind=kLoop, calls=%fused_computation.29 | loop fusion | flops 3145600 | bytes 4456960 | tf_op jit(solution)/shard_map/reduce_sum | solution.py:119
  147.6 3.6 %multiply_reduce_fusion = (f32[128]{0:T(128)S(1)}, bf16[1,128,4096]{2,1,0:T(8,128)(2,1)}) fusion(bf16[1,128,4096]{2,1,0:T(8,128)(2,1)} %collective-permute-done.1, f32[128]{0:T(128)S(1)} %rsqrt.12, f32[16,4096]{1,0:T(8,128)S(1)} %bitcast.238, f32[1,16,8,4096]{3,2,1,0:T(8,128)S(1)} %copy-done.4, f32[1,16,8,4096]{3,2,1,0:T(8,128)} %stack.8), kind=kLoop, calls=%fused_computation.28 | loop fusion | flops 4718464 | bytes 6554624 | tf_op jit(solution)/shard_map/reduce_sum | solution.py:120
  151.1 0.5 multiply_bitcast_fusion.1
  (47 shorter events, 2.2 us)
Async XLA Ops:
  7.2 11.4 %copy-start.5 = (f32[4096]{0:T(1024)S(1)}, f32[4096]{0:T(1024)}, u32[]{:S(2)}) copy-start(f32[4096]{0:T(1024)} %param.18) | copy-start | bytes 49156
  7.2 51.1 %all-gather.6.cloned.1.call-start = ((), (), s32[]{:S(2)}) async-start(), calls=%async_computation | async-start | bytes 2621440 | tf_op jit(solution)/shard_map/all_gather | solution.py:107
  8.8 8.2 %collective-permute-start = (bf16[1,3,4096]{2,1,0:T(4,128)(2,1)S(1)}, bf16[1,3,4096]{2,1,0:T(4,128)(2,1)S(1)}, u32[]{:S(2)}, u32[]{:S(2)}) collective-permute-start(bf16[1,3,4096]{2,1,0:T(4,128)(2,1)S(1)} %slice.90), channel_id=1, source_target_pairs={{0,1},{1,2},{2,3},{4,5},{5,6},{6,7},{8,9},{9,10},{10,11},{12,13},{... | collective-permute-start | bytes 73736 | tf_op jit(solution)/shard_map/ppermute | solution.py:34
  11.1 136.4 %collective-permute-start.1 = (bf16[1,128,4096]{2,1,0:T(8,128)(2,1)}, bf16[1,128,4096]{2,1,0:T(8,128)(2,1)}, u32[]{:S(2)}, u32[]{:S(2)}) collective-permute-start(bf16[1,128,4096]{2,1,0:T(8,128)(2,1)} %param.14), channel_id=1, source_target_pairs={{0,16},{16,0},{1,17},{17,1},{2,18},{18,2},{3,19},{19,3},{4,20},{20... | collective-permute-start | bytes 3145736 | tf_op jit(solution)/shard_map/ppermute | solution.py:28
  77.7 5.4 %copy-start = (f32[1,16,8,4096]{3,0,2,1:T(1,128)}, f32[1,16,8,4096]{3,0,2,1:T(1,128)S(1)}, u32[]{:S(2)}) copy-start(f32[1,16,8,4096]{3,0,2,1:T(1,128)S(1)} %broadcast_select_fusion.4) | copy-start | bytes 6291460
  89.0 5.2 %copy-start.1 = (f32[1,16,8,4096]{3,0,2,1:T(1,128)S(1)}, f32[1,16,8,4096]{3,0,2,1:T(1,128)}, u32[]{:S(2)}) copy-start(f32[1,16,8,4096]{3,0,2,1:T(1,128)} %copy-done) | copy-start | bytes 6291460
  94.2 2.1 %copy-start.3 = (f32[1,16,8,4096]{3,2,1,0:T(8,128)}, f32[1,16,8,4096]{3,2,1,0:T(8,128)S(1)}, u32[]{:S(2)}) copy-start(f32[1,16,8,4096]{3,2,1,0:T(8,128)S(1)} %multiply_bitcast_fusion) | copy-start | bytes 6291460
  121.4 6.7 %copy-start.2 = (f32[1,16,8,4096]{3,0,2,1:T(1,128)S(1)}, f32[1,16,8,4096]{3,0,2,1:T(1,128)}, u32[]{:S(2)}) copy-start(f32[1,16,8,4096]{3,0,2,1:T(1,128)} %copy-done) | copy-start | bytes 6291460
  139.0 6.5 %copy-start.4 = (f32[1,16,8,4096]{3,2,1,0:T(8,128)S(1)}, f32[1,16,8,4096]{3,2,1,0:T(8,128)}, u32[]{:S(2)}) copy-start(f32[1,16,8,4096]{3,2,1,0:T(8,128)} %stack.10) | copy-start | bytes 6291460
Sparse Core Ops, SparseCore 0:
  9.6 48.6 all-gather.5
where the time goes:
time: 161 us; the launch traced here: 158 us
  other arithmetic  55.3 us (34%)
  waiting for transfers between devices  38.8 us (24%)
  local copies, waits for them, and re-layouts  32.2 us (20%)
  between operations  14.3 us (9%)
  blocking collectives  10.5 us (7%)
  starting transfers between devices  4.81 us (3%)
  matrix products  2.33 us (1%)
    all_gather x1, waiting for transfers between devices, local(): lax.all_gather(gate_weights, 'fsdp', axis=0, tiled=True)  38.1 us
    add x2, other arithmetic, recurrence(): running_state = step_decay * running_state + drive_blocks[:, :, inner, :]  13 us
    add x16, other arithmetic, combine(): return (former[0] * latter[0], latter[0] * former[1] + latter[1])  12.5 us
    all_gather x2, blocking collectives, prefix(): everything = jax.tree.map(lambda part: lax.all_gather(part, axis), value)  10.5 us
    select_n x1, other arithmetic, recurrence(): decay = jnp.where(reset, jnp.float32(0.0), jnp.exp(log_a))  7.66 us
    another operation x1, local copies, waits for them, and re-layouts, recurrence(): products = jnp.stack(prod_list, axis=2)  6.67 us
    another operation x1, local copies, waits for them, and re-layouts, recurrence(): local_state = jnp.stack(state_list, axis=2)  6.47 us
    mul x2, other arithmetic, recurrence(): running_prod = running_prod * step_decay  5.4 us
  transfers between devices with their start and end apart: 3, of which 1 were waited for; matrix products, arithmetic and copies ran while one was open for 54% of the time, Pallas kernels for 0%

commit v1 on v0

--- a/solution.py
+++ b/solution.py
@@ -1,10 +1,19 @@
+import functools
+import math
+
 import jax
 import jax.numpy as jnp
 from jax import lax
+from jax.experimental import pallas as pl
+from jax.experimental.pallas import tpu as pltpu
 from jax.sharding import PartitionSpec as P
 
 HEADS = 32
 HS = 128
+LOG2E = math.log2(math.e)
+LN2 = math.log(2.0)
+STEPS = 16
+EDGE = 16
 
 
 def prefix(value, axis, combine, identity):
@@ -82,7 +91,7 @@
     return full.reshape(group, tokens, width).astype(jnp.bfloat16)
 
 
-def local(
+def general(
     branch_x, positions, teacher_held, gate_weights, gate_bias, conv_weight, conv_bias, decay_rate
 ):
     tokens = branch_x.shape[1]
@@ -121,7 +130,457 @@
     return (student, token_loss)
 
 
+def shard_of(shift):
+    count = lax.axis_size("fsdp")
+    return lax.rem(lax.axis_index("fsdp") + count - shift, count)
+
+
+def pack_kernel(
+    shifts, per, x_ref, pos_ref, w_ref, *refs
+):
+    devices = lax.axis_size("seq")
+    sends, (own_ref, wq_ref, edge_ref), (codes, sem) = refs[:devices], refs[devices : devices + 3], refs[devices + 3 :]
+    here = lax.axis_index("seq")
+    tokens = x_ref.shape[1]
+    shard_heads = w_ref.shape[0]
+    shard_width = shard_heads * HS
+    wide = per * HS
+    copies = []
+
+    def copy(source, target):
+        one = pltpu.make_async_copy(source, target, sem.at[len(copies)])
+        one.start()
+        copies.append(one)
+
+    copy(w_ref.at[pl.ds(here * per, per)], wq_ref)
+    own = pl.multiple_of(lax.axis_index("fsdp") * shard_width, shard_width)
+    for apart in range(devices - 1, -1, -1):
+        owner = lax.bitwise_xor(here, apart)
+        for index, shift in enumerate(shifts):
+            start = pl.multiple_of((shard_of(shift) * shard_heads + owner * per) * HS, wide)
+            copy(
+                x_ref.at[0, :, pl.ds(start, wide)],
+                sends[apart].at[pl.ds(0, tokens), pl.ds(index * wide, wide)],
+            )
+    copy(x_ref.at[0, pl.ds(tokens - EDGE, EDGE), pl.ds(own, shard_width)], edge_ref)
+    copy(x_ref.at[0, :, pl.ds(own, shard_width)], own_ref)
+    coded = jnp.minimum(pos_ref[...], 3).astype(jnp.float32)
+    codes[...] = jnp.zeros_like(codes)
+    codes[:, :tokens] = jnp.broadcast_to(coded, (EDGE, tokens)).astype(jnp.bfloat16)
+    for apart in range(devices):
+        copy(codes, sends[apart].at[pl.ds(tokens, EDGE), :])
+    for one in copies:
+        one.wait()
+
+
+def pack(branch_x, positions, gate_weights, shifts, per):
+    devices = lax.axis_size("seq")
+    tokens = branch_x.shape[1]
+    width = len(shifts) * per * HS
+    shard_width = gate_weights.shape[0] * HS
+    send = jax.ShapeDtypeStruct((tokens + EDGE, width), jnp.bfloat16)
+    anywhere = pl.BlockSpec(memory_space=pl.ANY)
+    out = pl.pallas_call(
+        functools.partial(pack_kernel, shifts, per),
+        out_shape=[send] * devices
+        + [
+            jax.ShapeDtypeStruct((tokens, shard_width), jnp.bfloat16),
+            jax.ShapeDtypeStruct((per,) + gate_weights.shape[1:], jnp.bfloat16),
+            jax.ShapeDtypeStruct((EDGE, shard_width), jnp.bfloat16),
+        ],
+        in_specs=[anywhere, pl.BlockSpec(memory_space=pltpu.VMEM), anywhere],
+        out_specs=[anywhere] * (devices + 3),
+        scratch_shapes=[
+            pltpu.VMEM((EDGE, width), jnp.bfloat16),
+            pltpu.SemaphoreType.DMA((devices * (len(shifts) + 1) + 3,)),
+        ],
+        compiler_params=pltpu.CompilerParams(vmem_limit_bytes=48 << 20),
+        name="pack",
+    )(branch_x, positions, gate_weights)
+    return out[:devices], out[devices], out[devices + 1], out[devices + 2]
+
+
+def spread(codes):
+    tokens = codes.shape[1]
+    down = lax.broadcasted_iota(jnp.int32, (tokens, tokens), 0)
+    across = lax.broadcasted_iota(jnp.int32, (tokens, tokens), 1)
+    diagonal = jnp.where(down == across, jnp.broadcast_to(codes, (tokens, tokens)), 0.0)
+    return jnp.dot(
+        diagonal.astype(jnp.bfloat16),
+        jnp.ones((tokens, HS), jnp.bfloat16),
+        preferred_element_type=jnp.float32,
+    )
+
+
+def write_masks(masks, natural, span):
+    for step in range(span):
+        code = natural[pl.ds(step, 8, stride=span), :]
+        rows = pl.ds(step * 8, 8)
+        first = jnp.minimum(code, 1.0)
+        masks[0, rows, :] = first
+        masks[1, rows, :] = jnp.clip(code - 1.0, 0.0, 1.0)
+        masks[2, rows, :] = jnp.clip(code - 2.0, 0.0, 1.0)
+        masks[3, rows, :] = jnp.maximum(1.0 - first, 1e-37)
+
+
+def row_of(ref, index, lanes):
+    return ref[pl.ds(index, 1), lanes]
+
+
+def gated_chunk(rows_ref, tile, first, span, lanes, masks, weights, params, total, carry):
+    conv_w, conv_b, bias, rates = params
+    tiles = [
+        rows_ref[tile, pl.ds(8 + first + step, 8, stride=span), :] for step in range(-3, STEPS)
+    ]
+    mask_rows = pl.ds(pl.multiple_of(first * 8, 8 * STEPS), 8 * STEPS)
+    half = jnp.concatenate(tiles[3:], axis=0) * (row_of(conv_w, 0, lanes) * 0.5) + (
+        row_of(conv_b, 0, lanes) * 0.5
+    )
+    for lag in range(1, 4):
+        shifted = jnp.concatenate(tiles[3 - lag : 3 - lag + STEPS], axis=0)
+        half = half + shifted * (row_of(conv_w, lag, lanes) * 0.5) * masks[lag - 1, mask_rows, :]
+    rounded = half.astype(jnp.bfloat16)
+    pre = jnp.dot(rounded, weights, preferred_element_type=jnp.float32)
+    gate_x = 1.0 + jnp.tanh(pre[:, :HS] + row_of(bias, 0, lanes) * 0.5)
+    gate_a = 1.0 + jnp.tanh(pre[:, HS:] + row_of(bias, 1, lanes) * 0.5)
+    power = gate_a * (row_of(rates, 0, lanes) * (-4.0 * LOG2E / total))
+    decay = jnp.exp2(power)
+    lost = jnp.tanh(power * -LN2)
+    square = jnp.maximum(lost + lost * decay * decay, masks[3, mask_rows, :])
+    drive = rounded.astype(jnp.float32) * gate_x * (square * lax.rsqrt(square))
+    decay = decay * masks[0, mask_rows, :]
+    product, state = carry
+    states, products = [], []
+    for step in range(STEPS):
+        at = slice(step * 8, step * 8 + 8)
+        state = decay[at] * state + drive[at]
+        product = product * decay[at]
+        states.append(state)
+        products.append(product)
+    return jnp.concatenate(states, axis=0), jnp.concatenate(products, axis=0), (product, state)
+
+
+def across_spans(product, state):
+    place = lax.broadcasted_iota(jnp.int32, product.shape, 0)
+    for apart in (1, 2, 4):
+        reached = place >= apart
+        before_p = jnp.where(reached, pltpu.roll(product, apart, 0), 1.0)
+        before_s = jnp.where(reached, pltpu.roll(state, apart, 0), 0.0)
+        state = product * before_s + state
+        product = product * before_p
+    enter_p = jnp.where(place >= 1, pltpu.roll(product, 1, 0), 1.0)
+    enter_s = jnp.where(place >= 1, pltpu.roll(state, 1, 0), 0.0)
+    return product, state, enter_p, enter_s
+
+
+def own_kernel(
+    total, x_ref, edge_ref, pos_ref, w_ref, cw_ref, cb_ref, bias_ref, rate_ref,
+    state_ref, prod_ref, enter_ref, end_ref, rows, natural, masks,
+):
+    tokens, width = x_ref.shape
+    span = tokens // 8
+    natural[...] = spread(jnp.minimum(pos_ref[...], 3).astype(jnp.float32))
+    write_masks(masks, natural, span)
+    for tile in range(width // HS):
+        column = pl.ds(tile * HS, HS)
+        rows[tile, pl.ds(0, 8), :] = edge_ref[:, column].astype(jnp.float32)[EDGE - 8 :]
+        rows[tile, pl.ds(8, tokens), :] = x_ref[:, column].astype(jnp.float32)
+    base = lax.axis_index("fsdp") * width
+    params = (cw_ref, cb_ref, bias_ref, rate_ref)
+
+    def body(head, unused):
+        column = pl.ds(pl.multiple_of(head * HS, HS), HS)
+        lanes = pl.ds(pl.multiple_of(base + head * HS, HS), HS)
+        weights = jnp.concatenate([w_ref[head, 0], w_ref[head, 1]], axis=1)
+        carry = (jnp.ones((8, HS), jnp.float32), jnp.zeros((8, HS), jnp.float32))
+        for first in range(0, span, STEPS):
+            states, products, carry = gated_chunk(
+                rows, head, first, span, lanes, masks, weights, params, total, carry
+            )
+            state_ref[pl.ds(first * 8, 8 * STEPS), column] = states
+            prod_ref[pl.ds(first * 8, 8 * STEPS), column] = products
+        product, state, enter_p, enter_s = across_spans(*carry)
+        enter_ref[0, :, column] = enter_p
+        enter_ref[1, :, column] = enter_s
+        end_ref[0:1, column] = product[7:8]
+        end_ref[1:2, column] = state[7:8]
+        return unused
+
+    lax.fori_loop(0, w_ref.shape[0], body, 0, unroll=2)
+
+
+def in_vmem(count):
+    return [pl.BlockSpec(memory_space=pltpu.VMEM)] * count
+
+
+def own_shard(own_x, edge, positions, gate_weights, params, total):
+    tokens, width = own_x.shape
+    return pl.pallas_call(
+        functools.partial(own_kernel, total),
+        out_shape=[
+            jax.ShapeDtypeStruct((tokens, width), jnp.float32),
+            jax.ShapeDtypeStruct((tokens, width), jnp.float32),
+            jax.ShapeDtypeStruct((2, 8, width), jnp.float32),
+            jax.ShapeDtypeStruct((2, width), jnp.float32),
+        ],
+        in_specs=in_vmem(8),
+        out_specs=in_vmem(4),
+        scratch_shapes=[
+            pltpu.VMEM((width // HS, tokens + 8, HS), jnp.float32),
+            pltpu.VMEM((tokens, HS), jnp.float32),
+            pltpu.VMEM((4, tokens, HS), jnp.float32),
+        ],
+        compiler_params=pltpu.CompilerParams(vmem_limit_bytes=32 << 20),
+        cost_estimate=pl.CostEstimate(
+            flops=200 * tokens * width, bytes_accessed=12 * tokens * width, transcendentals=5 * tokens * width
+        ),
+        name="own_shard",
+    )(own_x, edge, positions, gate_weights, *params)
+
+
+def far_kernel(indices, shifts, per, total, *refs):
+    devices = lax.axis_size("seq")
+    here = lax.axis_index("seq")
+    count = len(indices)
+    arrived, refs = refs[:devices], refs[devices:]
+    weights_refs, refs = refs[:count], refs[count:]
+    params, refs = refs[:4], refs[4:]
+    outs, (rows, natural, masks, states_s, prods_s) = refs[:devices], refs[devices:]
+    tokens = arrived[0].shape[0] - EDGE
+    length = tokens * devices
+    span = length // 8
+    wide = per * HS
+    shard_heads = HEADS // lax.axis_size("fsdp")
+    tiles = count * per
+    for tile in range(tiles):
+        rows[tile, pl.ds(0, 8), :] = jnp.zeros((8, HS), jnp.float32)
+    for apart in range(devices):
+        owner = lax.bitwise_xor(here, apart)
+        place = pl.multiple_of(owner * tokens, tokens)
+        for tile in range(tiles):
+            slot, head = divmod(tile, per)
+            rows[tile, pl.ds(8 + place, tokens), :] = arrived[apart][
+                pl.ds(0, tokens), pl.ds(indices[slot] * wide + head * HS, HS)
+            ].astype(jnp.float32)
+        codes = arrived[apart][pl.ds(tokens, EDGE), pl.ds(0, tokens)].astype(jnp.float32)
+        natural[pl.ds(place, tokens), :] = spread(codes[0:1])
+    write_masks(masks, natural, span)
+
+    def body(chunk, carries):
+        first = pl.multiple_of(chunk * STEPS, STEPS)
+        after = []
+        for tile in range(tiles):
+            slot, head = divmod(tile, per)
+            column = pl.ds(tile * HS, HS)
+            start = (shard_of(shifts[indices[slot]]) * shard_heads + here * per + head) * HS
+            lanes = pl.ds(pl.multiple_of(start, HS), HS)
+            weights = jnp.concatenate(
+                [weights_refs[slot][head, 0], weights_refs[slot][head, 1]], axis=1
+            )
+            states, products, carry = gated_chunk(
+                rows, tile, first, span, lanes, masks, weights, params, total, carries[tile]
+            )
+            at = pl.ds(pl.multiple_of(first * 8, 8 * STEPS), 8 * STEPS)
+            states_s[at, column] = states
+            prods_s[at, column] = products
+            after.append(carry)
+        return tuple(after)
+
+    begin = (jnp.ones((8, HS), jnp.float32), jnp.zeros((8, HS), jnp.float32))
+    carries = lax.fori_loop(0, span // STEPS, body, (begin,) * tiles)
+    entering = [across_spans(*carry)[3] for carry in carries]
+    for tile in range(tiles):
+        column = pl.ds(tile * HS, HS)
+        for step in range(span):
+            at = pl.ds(step * 8, 8)
+            rows[tile, pl.ds(step, 8, stride=span), :] = (
+                states_s[at, column] + prods_s[at, column] * entering[tile]
+            )
+    for apart in range(devices):
+        owner = lax.bitwise_xor(here, apart)
+        place = pl.multiple_of(owner * tokens, tokens)
+        for tile in range(tiles):
+            outs[apart][:, pl.ds(tile * HS, HS)] = rows[tile, pl.ds(place, tokens), :].astype(
+                jnp.bfloat16
+            )
+
+
+def far_shards(indices, shifts, per, arrived, weights, params, total):
+    devices = lax.axis_size("seq")
+    tokens = arrived[0].shape[0] - EDGE
+    length = tokens * devices
+    width = len(indices) * per * HS
+    return pl.pallas_call(
+        functools.partial(far_kernel, indices, shifts, per, total),
+        out_shape=[jax.ShapeDtypeStruct((tokens, width), jnp.bfloat16)] * devices,
+        in_specs=in_vmem(devices + len(indices) + 4),
+        out_specs=in_vmem(devices),
+        scratch_shapes=[
+            pltpu.VMEM((width // HS, length + 8, HS), jnp.float32),
+            pltpu.VMEM((length, HS), jnp.float32),
+            pltpu.VMEM((4, length, HS), jnp.float32),
+            pltpu.VMEM((length, width), jnp.float32),
+            pltpu.VMEM((length, width), jnp.float32),
+        ],
+        compiler_params=pltpu.CompilerParams(vmem_limit_bytes=32 << 20),
+        cost_estimate=pl.CostEstimate(
+            flops=200 * length * width, bytes_accessed=8 * length * width, transcendentals=5 * length * width
+        ),
+        name="far_shards",
+    )(*arrived, *weights, *params)
+
+
+def student_kernel(batches, shifts, per, *refs):
+    devices = lax.axis_size("seq")
+    here = lax.axis_index("seq")
+    state_ref, prod_ref, enter_ref = refs[:3]
+    ends, refs = refs[3 : 3 + devices], refs[3 + devices :]
+    pieces, refs = refs[: len(batches) * devices], refs[len(batches) * devices :]
+    out_ref, scale_ref, ends_s, natural = refs
+    tokens, width = state_ref.shape
+    span = tokens // 8
+    wide = per * HS
+    shard_heads = width // HS
+    for apart in range(devices):
+        ends_s[lax.bitwise_xor(here, apart)] = ends[apart][...]
+    incoming = jnp.zeros((1, width), jnp.float32)
+    for place in range(devices - 1):
+        after = ends_s[place, 0:1, :] * incoming + ends_s[place, 1:2, :]
+        incoming = jnp.where(place < here, after, incoming)
+    entering = enter_ref[1] + enter_ref[0] * incoming
+    for tile in range(shard_heads):
+        column = slice(tile * HS, (tile + 1) * HS)
+        for step in range(span):
+            at = pl.ds(step * 8, 8)
+            natural[tile, pl.ds(step, 8, stride=span), :] = (
+                state_ref[at, column] + prod_ref[at, column] * entering[:, column]
+            )
+    squares = jnp.zeros((tokens, HS), jnp.float32)
+
+    def add(squares, rounded):
+        value = rounded.astype(jnp.float32)
+        for tile in range(value.shape[1] // HS):
+            part = value[:, tile * HS : (tile + 1) * HS]
+            squares = squares + part * part
+        return squares
+
+    base = pl.multiple_of(lax.axis_index("fsdp") * width, width)
+    for tile in range(shard_heads):
+        rounded = natural[tile].astype(jnp.bfloat16)
+        out_ref[0, :, pl.ds(pl.multiple_of(base + tile * HS, HS), HS)] = rounded
+        squares = add(squares, rounded)
+    for number, batch in enumerate(batches):
+        for slot, index in enumerate(batch):
+            shard = shard_of(shifts[index])
+            for apart in range(devices):
+                owner = lax.bitwise_xor(here, apart)
+                rounded = pieces[number * devices + apart][:, slot * wide : (slot + 1) * wide]
+                start = pl.multiple_of((shard * shard_heads + owner * per) * HS, wide)
+                out_ref[0, :, pl.ds(start, wide)] = rounded
+                squares = add(squares, rounded)
+    mean = jnp.sum(squares, axis=1, keepdims=True) * (1.0 / out_ref.shape[2])
+    scale_ref[...] = jnp.broadcast_to(lax.rsqrt(mean + 1e-06), (tokens, HS))
+
+
+def student_rows(states, products, enter, ends, batches, shifts, per, pieces):
+    devices = lax.axis_size("seq")
+    tokens, width = states.shape
+    full = HEADS * HS
+    flat = [piece for batch in pieces for piece in batch]
+    return pl.pallas_call(
+        functools.partial(student_kernel, batches, shifts, per),
+        out_shape=[
+            jax.ShapeDtypeStruct((1, tokens, full), jnp.bfloat16),
+            jax.ShapeDtypeStruct((tokens, HS), jnp.float32),
+        ],
+        in_specs=in_vmem(3 + devices + len(flat)),
+        out_specs=in_vmem(2),
+        scratch_shapes=[
+            pltpu.VMEM((devices, 2, width), jnp.float32),
+            pltpu.VMEM((width // HS, tokens, HS), jnp.float32),
+        ],
+        compiler_params=pltpu.CompilerParams(vmem_limit_bytes=32 << 20),
+        cost_estimate=pl.CostEstimate(
+            flops=8 * tokens * full, bytes_accessed=6 * tokens * full, transcendentals=0
+        ),
+        name="student_rows",
+    )(states, products, enter, *ends, *flat)
+
+
+def loss_kernel(student_ref, scale_ref, target_ref, loss_ref):
+    tokens = student_ref.shape[1]
+    width = student_ref.shape[2]
+    scale = scale_ref[...]
+    total = jnp.zeros((tokens, HS), jnp.float32)
+    for start in range(0, width, HS):
+        lanes = slice(start, start + HS)
+        off = student_ref[0, :, lanes].astype(jnp.float32) * scale - target_ref[
+            0, :, lanes
+        ].astype(jnp.float32)
+        total = total + off * off
+    loss_ref[...] = jnp.sum(total.T, axis=0, keepdims=True) * (1.0 / width)
+
+
+def token_losses(student, scale, target):
+    tokens = student.shape[1]
+    return pl.pallas_call(
+        loss_kernel,
+        out_shape=jax.ShapeDtypeStruct((1, tokens), jnp.float32),
+        in_specs=in_vmem(3),
+        out_specs=pl.BlockSpec(memory_space=pltpu.VMEM),
+        compiler_params=pltpu.CompilerParams(vmem_limit_bytes=32 << 20),
+        cost_estimate=pl.CostEstimate(
+            flops=4 * student.size, bytes_accessed=4 * student.size, transcendentals=0
+        ),
+        name="token_losses",
+    )(student, scale, target)
+
+
+def across_seq(value, apart):
+    return lax.ppermute(value, "seq", [(i, i ^ apart) for i in range(lax.axis_size("seq"))])
+
+
+def local(
+    branch_x, positions, teacher_held, gate_weights, gate_bias, conv_weight, conv_bias, decay_rate
+):
+    devices, shards = lax.axis_size("seq"), lax.axis_size("fsdp")
+    tokens, width = branch_x.shape[1:]
+    total = devices * tokens
+    per = gate_weights.shape[0] // devices
+    shifts = (1, 3, 2)
+    batches = ((0, 1), (2,))
+    target = from_partner(teacher_held, "segment", 0)
+    sends, own_x, weights_part, edge = pack(branch_x, positions, gate_weights, shifts, per)
+    arrived = [sends[0]] + [None] * (devices - 1)
+    for apart in range(devices - 1, 0, -1):
+        arrived[apart] = across_seq(sends[apart], apart)
+    weights = [
+        lax.ppermute(weights_part, "fsdp", [(i, (i + shift) % shards) for i in range(shards)])
+        for shift in shifts
+    ]
+    edge = from_behind(edge, "seq", 1)
+    params = (
+        conv_weight,
+        conv_bias.reshape(1, width),
+        gate_bias,
+        decay_rate.reshape(1, width),
+    )
+    states, products, enter, end = own_shard(own_x, edge, positions, gate_weights, params, total)
+    ends = [end] + [across_seq(end, apart) for apart in range(1, devices)]
+    pieces = []
+    for batch in batches:
+        outs = far_shards(
+            batch, shifts, per, arrived, [weights[index] for index in batch], params, total
+        )
+        pieces.append([outs[0]] + [across_seq(outs[apart], apart) for apart in range(1, devices)])
+    student, scale = student_rows(states, products, enter, ends, batches, shifts, per, pieces)
+    return student, token_losses(student, scale, target)
+
+
 def solution(mesh):
+    shards, devices = mesh.shape["fsdp"], mesh.shape["seq"]
+    held = HEADS // shards
+    whole = HEADS % shards == 0 and shards == 4 and held % devices == 0 and devices & (devices - 1) == 0
     in_specs = (
         P(("segment", "fsdp"), "seq", None),
         P(("segment", "fsdp"), "seq"),
@@ -133,4 +592,10 @@
         P(),
     )
     out_specs = (P(("segment", "fsdp"), "seq", None), P(("segment", "fsdp"), "seq"))
-    return jax.shard_map(local, mesh=mesh, in_specs=in_specs, out_specs=out_specs, check_vma=False)
+    return jax.shard_map(
+        local if whole else general,
+        mesh=mesh,
+        in_specs=in_specs,
+        out_specs=out_specs,
+        check_vma=False,
+    )

time: 161 us -> 52.1 us (0.32); the launches traced: 158 us -> 51.8 us
  other arithmetic: 55.3 us -> 0 us
  local copies, waits for them, and re-layouts: 32.2 us -> 4.16 us
  waiting for transfers between devices: 38.8 us -> 15.6 us
  starting transfers between devices: 4.81 us -> 21.7 us
  between operations: 14.3 us -> 0.75 us
  blocking collectives: 10.5 us -> 0 us
  Pallas kernels: 0 us -> 9.6 us
  matrix products: 2.33 us -> 0 us
    all_gather x1 -> x0, waiting for transfers between devices: 38.1 us -> none  [local(): lax.all_gather(gate_weights, 'fsdp', axis=0, tiled=True)]
    add x19 -> x0, other arithmetic: 25.8 us -> none  [the longest x2 13 us: recurrence(): running_state = step_decay * running_state + drive_blocks[:, :, inner, :]]
    another operation x6 -> x0, local copies, waits for them, and re-layouts: 19.4 us -> none  [the longest x1 6.67 us: recurrence(): products = jnp.stack(prod_list, axis=2)]
    ppermute x0 -> x15, starting transfers between devices: none -> 16.3 us  [the longest x12 9.88 us: across_seq(): lax.ppermute(value, 'seq', [(i, i ^ apart) for i in range(lax.axis_size('...]
    ppermute x0 -> x15, waiting for transfers between devices: none -> 14.7 us  [the longest x12 7.87 us: across_seq(): lax.ppermute(value, 'seq', [(i, i ^ apart) for i in range(lax.axis_size('...]
    all_gather x2 -> x0, blocking collectives: 10.5 us -> none  [prefix(): everything = jax.tree.map(lambda part: lax.all_gather(part, axis), value)]
    pallas_call x0 -> x6, Pallas kernels: none -> 9.6 us  [the longest x2 4.93 us: far_shards(): pl.pallas_call(functools.partial(far_kernel, indices, shifts, per, total)...]
    slice x5 -> x0, local copies, waits for them, and re-layouts: 8.19 us -> none  [the longest x1 3.12 us: local(): preact[:, 1].reshape(1, tokens, width)]
  transfers between devices with their start and end apart: 3 -> 17, of which waited for: 1 -> 4; matrix products, arithmetic and copies ran while one was open for 54% -> 0% of each run, Pallas kernels for 0% -> 16%
where the time goes in v1:
time: 52.1 us; the launch traced here: 51.8 us
  starting transfers between devices  21.7 us (42%)
  waiting for transfers between devices  15.6 us (30%)
  Pallas kernels  9.6 us (18%)
  local copies, waits for them, and re-layouts  4.16 us (8%)
  between operations  0.75 us (1%)
    ppermute x12, starting transfers between devices, across_seq(): lax.ppermute(value, 'seq', [(i, i ^ apart) for i in range(lax.axis_size('...  9.88 us
    ppermute x12, waiting for transfers between devices, across_seq(): lax.ppermute(value, 'seq', [(i, i ^ apart) for i in range(lax.axis_size('...  7.87 us
    ppermute x3, waiting for transfers between devices, local(): lax.ppermute(weights_part, 'fsdp', [(i, (i + shift) % shards) for i in ra...  6.87 us
    ppermute x3, starting transfers between devices, local(): lax.ppermute(weights_part, 'fsdp', [(i, (i + shift) % shards) for i in ra...  6.41 us
    pallas_call x2, Pallas kernels, far_shards(): pl.pallas_call(functools.partial(far_kernel, indices, shifts, per, total)...  4.93 us
    unnamed x16, local copies, waits for them, and re-layouts  4.16 us
    ppermute x1, starting transfers between devices, from_partner(): lax.ppermute(value, axis, [(i, i ^ 1 << apart) for i in range(lax.axis_si...  3.03 us
    ppermute x1, starting transfers between devices, from_behind(): lax.ppermute(value, axis, [(source, source + steps) for source in range(l...  2.39 us
  transfers between devices with their start and end apart: 17, of which 4 were waited for; matrix products, arithmetic and copies ran while one was open for 0% of the time, Pallas kernels for 16%

profile of v1, /device:TPU:0, one launch (start us, length us, event | category | flops | bytes accessed | tf_op | source)
XLA Modules:
  0.0 51.8 jit_solution(13200646805942472054)
XLA Ops:
  0.6 3.0 %collective-permute-start.16 = (bf16[1,128,4096]{2,1,0:T(8,128)(2,1)}, bf16[1,128,4096]{2,1,0:T(8,128)(2,1)S(1)}, u32[]{:S(2)}, u32[]{:S(2)}) collective-permute-start(bf16[1,128,4096]{2,1,0:T(8,128)(2,1)} %param.10), channel_id=1, source_target_pairs={{0,16},{16,0},{1,17},{17,1},{2,18},{18,2},{3,19},{19,3},{4,20},{20... | collective-permute-start | bytes 3145736 | tf_op jit(solution)/shard_map/ppermute | solution.py:37
  3.7 1.2 %copy-done.1 = bf16[1,128,4096]{2,1,0:T(8,128)(2,1)S(1)} copy-done((bf16[1,128,4096]{2,1,0:T(8,128)(2,1)S(1)}, bf16[1,128,4096]{2,1,0:T(8,128)(2,1)}, u32[]{:S(2)}) %copy-start.1) | copy-done | bytes 1048600
  4.9 1.0 %copy-done.2 = bf16[8,2,128,128]{3,2,1,0:T(8,128)(2,1)S(1)} copy-done((bf16[8,2,128,128]{3,2,1,0:T(8,128)(2,1)S(1)}, bf16[8,2,128,128]{3,2,1,0:T(8,128)(2,1)}, u32[]{:S(2)}) %copy-start.2) | copy-done | bytes 524312
  5.9 0.7 %copy-done.3 = s32[1,128]{1,0:T(1,128)S(1)} copy-done((s32[1,128]{1,0:T(1,128)S(1)}, s32[1,128]{1,0:T(1,128)}, u32[]{:S(2)}) %copy-start.3) | copy-done | bytes 536
  6.6 0.7 %pack.1 = (bf16[144,768]{1,0:T(8,128)(2,1)S(1)}, bf16[144,768]{1,0:T(8,128)(2,1)S(1)}, bf16[144,768]{1,0:T(8,128)(2,1)S(1)}, bf16[144,768]{1,0:T(8,128)(2,1)S(1)...) custom-call(bf16[1,128,4096]{2,1,0:T(8,128)(2,1)S(1)} %copy-done.1, ...), custom_call_target="tpu_custom_call" | custom-call | tf_op jit(solution)/shard_map/pack/pallas_call | solution.py:183
  7.3 0.1 collective-permute-start.4
  7.4 1.6 %collective-permute-start.5 = (bf16[144,768]{1,0:T(8,128)(2,1)S(1)}, bf16[144,768]{1,0:T(8,128)(2,1)S(1)}, u32[]{:S(2)}, u32[]{:S(2)}) collective-permute-start(bf16[144,768]{1,0:T(8,128)(2,1)S(1)} %get-tuple-element.31), channel_id=1, source_target_pairs={{0,2},{1,3},{2,0},{3,1},{4,6},{5,7},{6,4},{7,5},{8,10},{9,11},{10,... | collective-permute-start | bytes 663560 | tf_op jit(solution)/shard_map/ppermute | solution.py:540
  9.0 0.3 collective-permute-start.6
  9.3 2.6 %collective-permute-start.12 = (bf16[2,2,128,128]{3,2,1,0:T(8,128)(2,1)S(1)}, bf16[2,2,128,128]{3,2,1,0:T(8,128)(2,1)S(1)}, u32[]{:S(2)}, u32[]{:S(2)}) collective-permute-start(bf16[2,2,128,128]{3,2,1,0:T(8,128)(2,1)S(1)} %get-tuple-element.33), channel_id=1, source_target_pairs={{0,8},{4,12},{8,0},{12,4},{1,9},{5,13},{9,1},{13,5},{2,10},{6,14},... | collective-permute-start | bytes 393224 | tf_op jit(solution)/shard_map/ppermute | solution.py:558
  11.9 6.9 %collective-permute-done.12.refs_4_ = bf16[2,2,128,128]{3,2,1,0:T(8,128)(2,1)S(1)} collective-permute-done((bf16[2,2,128,128]{3,2,1,0:T(8,128)(2,1)S(1)}, bf16[2,2,128,128]{3,2,1,0:T(8,128)(2,1)S(1)}, u32[]{:S(2)}, u32[]{:S(2)}) %collective-permute-start.12) | collective-permute-done | bytes 131104 | tf_op jit(solution)/shard_map/ppermute | solution.py:558
  18.7 0.7 %collective-permute-start.7 = (bf16[2,2,128,128]{3,2,1,0:T(8,128)(2,1)S(1)}, bf16[2,2,128,128]{3,2,1,0:T(8,128)(2,1)S(1)}, u32[]{:S(2)}, u32[]{:S(2)}) collective-permute-start(bf16[2,2,128,128]{3,2,1,0:T(8,128)(2,1)S(1)} %get-tuple-element.33), channel_id=1, source_target_pairs={{0,4},{4,8},{8,12},{12,0},{1,5},{5,9},{9,13},{13,1},{2,6},{6,10},{... | collective-permute-start | bytes 393224 | tf_op jit(solution)/shard_map/ppermute | solution.py:558
  19.4 0.0 collective-permute-done.4.refs_1_
  19.4 3.1 %collective-permute-start.8 = (bf16[2,2,128,128]{3,2,1,0:T(8,128)(2,1)S(1)}, bf16[2,2,128,128]{3,2,1,0:T(8,128)(2,1)S(1)}, u32[]{:S(2)}, u32[]{:S(2)}) collective-permute-start(bf16[2,2,128,128]{3,2,1,0:T(8,128)(2,1)S(1)} %get-tuple-element.33), channel_id=1, source_target_pairs={{0,12},{4,0},{8,4},{12,8},{1,13},{5,1},{9,5},{13,9},{2,14},{6,2},{... | collective-permute-start | bytes 393224 | tf_op jit(solution)/shard_map/ppermute | solution.py:558
  22.5 0.0 collective-permute-done.5.refs_2_
  22.5 0.0 collective-permute-done.6.refs_3_
  22.6 0.0 copy-done.4
  22.6 0.0 copy-done.5
  22.6 0.0 copy-done.6
  22.6 0.0 copy-done.7
  22.6 1.9 %far_shards.3 = (bf16[128,256]{1,0:T(8,128)(2,1)S(1)}, bf16[128,256]{1,0:T(8,128)(2,1)S(1)}, bf16[128,256]{1,0:T(8,128)(2,1)S(1)}, bf16[128,256]{1,0:T(8,128)(2,1)S(1)}) custom-call(bf16[144,768]{1,0:T(8,128)(2,1)S(1)} %get-tuple-element.29.refs_0_, bf16[144,768]{1,0:T(8,128)(2,1)S(1)} %collective-permute-done.4.refs_1_, ...), custom_call_target="tpu_custom_call" | custom-call | flops 26214400 | bytes 1048576 | tf_op jit(solution)/shard_map/far_shards/pallas_call | solution.py:413
  24.5 0.1 collective-permute-start.13
  24.6 2.4 %collective-permute-start = (bf16[16,1024]{1,0:T(8,128)(2,1)S(1)}, bf16[16,1024]{1,0:T(8,128)(2,1)S(1)}, u32[]{:S(2)}, u32[]{:S(2)}) collective-permute-start(bf16[16,1024]{1,0:T(8,128)(2,1)S(1)} %get-tuple-element.24), channel_id=1, source_target_pairs={{0,1},{1,2},{2,3},{4,5},{5,6},{6,7},{8,9},{9,10},{10,11},{12,13},{... | collective-permute-start | bytes 98312 | tf_op jit(solution)/shard_map/ppermute | solution.py:43
  27.0 0.8 %collective-permute-done.edge_ref = bf16[16,1024]{1,0:T(8,128)(2,1)S(1)} collective-permute-done((bf16[16,1024]{1,0:T(8,128)(2,1)S(1)}, bf16[16,1024]{1,0:T(8,128)(2,1)S(1)}, u32[]{:S(2)}, u32[]{:S(2)}) %collective-permute-start) | collective-permute-done | bytes 32800 | tf_op jit(solution)/shard_map/ppermute | solution.py:43
  27.8 1.3 %own_shard.1 = (f32[128,1024]{1,0:T(8,128)S(1)}, f32[128,1024]{1,0:T(8,128)S(1)}, f32[2,8,1024]{2,1,0:T(8,128)S(1)}, f32[2,1024]{1,0:T(2,128)S(1)}) custom-call(bf16[128,1024]{1,0:T(8,128)(2,1)S(1)} %get-tuple-element.23.x_ref, bf16[16,1024]{1,0:T(8,128)(2,1)S(1)} %collective-permute-done.edge_ref, s32[1,128]{1,0:T(1,128)S(1)} %copy-done.3, ...), custom_call_target="tpu_custom_call" | custom-call | flops 26214400 | bytes 1572864 | tf_op jit(solution)/shard_map/own_shard/pallas_call | solution.py:318
  29.1 1.3 %collective-permute-start.1 = (f32[2,1024]{1,0:T(2,128)S(1)}, f32[2,1024]{1,0:T(2,128)S(1)}, u32[]{:S(2)}, u32[]{:S(2)}) collective-permute-start(f32[2,1024]{1,0:T(2,128)S(1)} %get-tuple-element.28.refs_3_), channel_id=1, source_target_pairs={{0,1},{1,0},{2,3},{3,2},{4,5},{5,4},{6,7},{7,6},{8,9},{9,8},{10,11... | collective-permute-start | bytes 24584 | tf_op jit(solution)/shard_map/ppermute | solution.py:540
  30.5 0.0 collective-permute-done.7.refs_4_
  30.5 2.3 %collective-permute-start.2 = (f32[2,1024]{1,0:T(2,128)S(1)}, f32[2,1024]{1,0:T(2,128)S(1)}, u32[]{:S(2)}, u32[]{:S(2)}) collective-permute-start(f32[2,1024]{1,0:T(2,128)S(1)} %get-tuple-element.28.refs_3_), channel_id=1, source_target_pairs={{0,2},{1,3},{2,0},{3,1},{4,6},{5,7},{6,4},{7,5},{8,10},{9,11},{10,... | collective-permute-start | bytes 24584 | tf_op jit(solution)/shard_map/ppermute | solution.py:540
  32.8 0.0 collective-permute-done.8.refs_5_
  32.8 0.1 collective-permute-start.3
  32.9 3.0 %far_shards.2 = (bf16[128,512]{1,0:T(8,128)(2,1)S(1)}, bf16[128,512]{1,0:T(8,128)(2,1)S(1)}, bf16[128,512]{1,0:T(8,128)(2,1)S(1)}, bf16[128,512]{1,0:T(8,128)(2,1)S(1)}) custom-call(bf16[144,768]{1,0:T(8,128)(2,1)S(1)} %get-tuple-element.29.refs_0_, bf16[144,768]{1,0:T(8,128)(2,1)S(1)} %collective-permute-done.4.refs_1_, ...), custom_call_target="tpu_custom_call" | custom-call | flops 52428800 | bytes 2097152 | tf_op jit(solution)/shard_map/far_shards/pallas_call | solution.py:413
  35.9 0.0 collective-permute-done.1.refs_4_
  35.9 1.7 %collective-permute-start.10 = (bf16[128,512]{1,0:T(8,128)(2,1)S(1)}, bf16[128,512]{1,0:T(8,128)(2,1)S(1)}, u32[]{:S(2)}, u32[]{:S(2)}) collective-permute-start(bf16[128,512]{1,0:T(8,128)(2,1)S(1)} %get-tuple-element.36), channel_id=1, source_target_pairs={{0,2},{1,3},{2,0},{3,1},{4,6},{5,7},{6,4},{7,5},{8,10},{9,11},{10,... | collective-permute-start | bytes 393224 | tf_op jit(solution)/shard_map/ppermute | solution.py:540
  37.7 0.0 collective-permute-done.2.refs_5_
  37.7 0.4 collective-permute-start.14
  38.0 0.0 collective-permute-done.3.refs_6_
  38.0 1.1 %collective-permute-start.11 = (bf16[128,512]{1,0:T(8,128)(2,1)S(1)}, bf16[128,512]{1,0:T(8,128)(2,1)S(1)}, u32[]{:S(2)}, u32[]{:S(2)}) collective-permute-start(bf16[128,512]{1,0:T(8,128)(2,1)S(1)} %get-tuple-element.37), channel_id=1, source_target_pairs={{0,3},{1,2},{2,1},{3,0},{4,7},{5,6},{6,5},{7,4},{8,11},{9,10},{10,... | collective-permute-start | bytes 393224 | tf_op jit(solution)/shard_map/ppermute | solution.py:540
  39.1 0.0 collective-permute-done.13.refs_12_
  39.1 0.7 %collective-permute-start.9 = (bf16[128,512]{1,0:T(8,128)(2,1)S(1)}, bf16[128,512]{1,0:T(8,128)(2,1)S(1)}, u32[]{:S(2)}, u32[]{:S(2)}) collective-permute-start(bf16[128,512]{1,0:T(8,128)(2,1)S(1)} %get-tuple-element.35), channel_id=1, source_target_pairs={{0,1},{1,0},{2,3},{3,2},{4,5},{5,4},{6,7},{7,6},{8,9},{9,8},{10,11... | collective-permute-start | bytes 393224 | tf_op jit(solution)/shard_map/ppermute | solution.py:540
  39.8 3.9 %collective-permute-done.14.refs_13_ = bf16[128,256]{1,0:T(8,128)(2,1)S(1)} collective-permute-done((bf16[128,256]{1,0:T(8,128)(2,1)S(1)}, bf16[128,256]{1,0:T(8,128)(2,1)S(1)}, u32[]{:S(2)}, u32[]{:S(2)}) %collective-permute-start.14) | collective-permute-done | bytes 65568 | tf_op jit(solution)/shard_map/ppermute | solution.py:540
  43.7 0.2 collective-permute-start.15
  44.0 3.9 %collective-permute-done.15.refs_14_ = bf16[128,256]{1,0:T(8,128)(2,1)S(1)} collective-permute-done((bf16[128,256]{1,0:T(8,128)(2,1)S(1)}, bf16[128,256]{1,0:T(8,128)(2,1)S(1)}, u32[]{:S(2)}, u32[]{:S(2)}) %collective-permute-start.15) | collective-permute-done | bytes 65568 | tf_op jit(solution)/shard_map/ppermute | solution.py:540
  47.9 0.0 collective-permute-done.10.refs_9_
  47.9 0.0 collective-permute-done.11.refs_10_
  47.9 0.0 collective-permute-done.9.refs_8_
  47.9 1.5 %student_rows.1 = (bf16[1,128,4096]{2,1,0:T(8,128)(2,1)}, f32[128,128]{1,0:T(8,128)S(1)}) custom-call(f32[128,1024]{1,0:T(8,128)S(1)} %get-tuple-element.25.refs_0_, f32[128,1024]{1,0:T(8,128)S(1)} %get-tuple-element.26.refs_1_, f32[2,8,1024]{2,1,0:T(8,128)S(1)} %get-tuple-element.27.refs_2_, f32[2,1024]{1,0:T(2,128)S(1)} %get-tuple-element.28.refs_3_, ...), custom_call_target="tpu_custom_call" | custom-call | flops 4194304 | bytes 3145728 | tf_op jit(solution)/shard_map/student_rows/pallas_call | solution.py:490
  49.5 0.0 collective-permute-done.16.target_ref
  49.5 1.2 %copy-done = bf16[1,128,4096]{2,1,0:T(8,128)(2,1)S(1)} copy-done((bf16[1,128,4096]{2,1,0:T(8,128)(2,1)S(1)}, bf16[1,128,4096]{2,1,0:T(8,128)(2,1)}, u32[]{:S(2)}) %copy-start) | copy-done | bytes 1048600
  50.7 1.1 %token_losses.1 = f32[1,128]{1,0:T(1,128)} custom-call(bf16[1,128,4096]{2,1,0:T(8,128)(2,1)S(1)} %copy-done, f32[128,128]{1,0:T(8,128)S(1)} %get-tuple-element.43.scale_ref, bf16[1,128,4096]{2,1,0:T(8,128)(2,1)S(1)} %collective-permute-done.16.target_ref), custom_call_target="tpu_custom_call" | custom-call | flops 2097152 | bytes 2097152 | tf_op jit(solution)/shard_map/token_losses/pallas_call | solution.py:526
  (8 shorter events, 0.0 us)
Async XLA Ops:
  0.6 48.8 %collective-permute-start.16 = (bf16[1,128,4096]{2,1,0:T(8,128)(2,1)}, bf16[1,128,4096]{2,1,0:T(8,128)(2,1)S(1)}, u32[]{:S(2)}, u32[]{:S(2)}) collective-permute-start(bf16[1,128,4096]{2,1,0:T(8,128)(2,1)} %param.10), channel_id=1, source_target_pairs={{0,16},{16,0},{1,17},{17,1},{2,18},{18,2},{3,19},{19,3},{4,20},{20... | collective-permute-start | bytes 3145736 | tf_op jit(solution)/shard_map/ppermute | solution.py:37
  3.7 1.2 %copy-start.1 = (bf16[1,128,4096]{2,1,0:T(8,128)(2,1)S(1)}, bf16[1,128,4096]{2,1,0:T(8,128)(2,1)}, u32[]{:S(2)}) copy-start(bf16[1,128,4096]{2,1,0:T(8,128)(2,1)} %x_ref.1) | copy-start | bytes 3145732
  4.9 1.0 %copy-start.2 = (bf16[8,2,128,128]{3,2,1,0:T(8,128)(2,1)S(1)}, bf16[8,2,128,128]{3,2,1,0:T(8,128)(2,1)}, u32[]{:S(2)}) copy-start(bf16[8,2,128,128]{3,2,1,0:T(8,128)(2,1)} %w_ref.3) | copy-start | bytes 1572868
  5.9 0.7 %copy-start.3 = (s32[1,128]{1,0:T(1,128)S(1)}, s32[1,128]{1,0:T(1,128)}, u32[]{:S(2)}) copy-start(s32[1,128]{1,0:T(1,128)} %pos_ref.3) | copy-start | bytes 1540
  6.6 16.0 %copy-start.4 = (f32[4,4096]{1,0:T(4,128)S(1)}, f32[4,4096]{1,0:T(4,128)}, u32[]{:S(2)}) copy-start(f32[4,4096]{1,0:T(4,128)} %refs_5_.1) | copy-start | bytes 196612
  6.6 16.0 %copy-start.5 = (f32[2,4096]{1,0:T(2,128)S(1)}, f32[2,4096]{1,0:T(2,128)}, u32[]{:S(2)}) copy-start(f32[2,4096]{1,0:T(2,128)} %refs_7_.1) | copy-start | bytes 98308
  6.6 16.0 %copy-start.6 = (f32[4096]{0:T(1024)S(1)}, f32[4096]{0:T(1024)}, u32[]{:S(2)}) copy-start(f32[4096]{0:T(1024)} %param.14) | copy-start | bytes 49156
  6.6 16.0 %copy-start.7 = (f32[4096]{0:T(1024)S(1)}, f32[4096]{0:T(1024)}, u32[]{:S(2)}) copy-start(f32[4096]{0:T(1024)} %param.15) | copy-start | bytes 49156
  7.3 12.1 %collective-permute-start.4 = (bf16[144,768]{1,0:T(8,128)(2,1)S(1)}, bf16[144,768]{1,0:T(8,128)(2,1)S(1)}, u32[]{:S(2)}, u32[]{:S(2)}) collective-permute-start(bf16[144,768]{1,0:T(8,128)(2,1)S(1)} %get-tuple-element.30), channel_id=1, source_target_pairs={{0,1},{1,0},{2,3},{3,2},{4,5},{5,4},{6,7},{7,6},{8,9},{9,8},{10,11... | collective-permute-start | bytes 663560 | tf_op jit(solution)/shard_map/ppermute | solution.py:540
  7.4 15.1 %collective-permute-start.5 = (bf16[144,768]{1,0:T(8,128)(2,1)S(1)}, bf16[144,768]{1,0:T(8,128)(2,1)S(1)}, u32[]{:S(2)}, u32[]{:S(2)}) collective-permute-start(bf16[144,768]{1,0:T(8,128)(2,1)S(1)} %get-tuple-element.31), channel_id=1, source_target_pairs={{0,2},{1,3},{2,0},{3,1},{4,6},{5,7},{6,4},{7,5},{8,10},{9,11},{10,... | collective-permute-start | bytes 663560 | tf_op jit(solution)/shard_map/ppermute | solution.py:540
  9.0 13.6 %collective-permute-start.6 = (bf16[144,768]{1,0:T(8,128)(2,1)S(1)}, bf16[144,768]{1,0:T(8,128)(2,1)S(1)}, u32[]{:S(2)}, u32[]{:S(2)}) collective-permute-start(bf16[144,768]{1,0:T(8,128)(2,1)S(1)} %get-tuple-element.32), channel_id=1, source_target_pairs={{0,3},{1,2},{2,1},{3,0},{4,7},{5,6},{6,5},{7,4},{8,11},{9,10},{10,... | collective-permute-start | bytes 663560 | tf_op jit(solution)/shard_map/ppermute | solution.py:540
  9.3 9.5 %collective-permute-start.12 = (bf16[2,2,128,128]{3,2,1,0:T(8,128)(2,1)S(1)}, bf16[2,2,128,128]{3,2,1,0:T(8,128)(2,1)S(1)}, u32[]{:S(2)}, u32[]{:S(2)}) collective-permute-start(bf16[2,2,128,128]{3,2,1,0:T(8,128)(2,1)S(1)} %get-tuple-element.33), channel_id=1, source_target_pairs={{0,8},{4,12},{8,0},{12,4},{1,9},{5,13},{9,1},{13,5},{2,10},{6,14},... | collective-permute-start | bytes 393224 | tf_op jit(solution)/shard_map/ppermute | solution.py:558
  18.7 11.8 %collective-permute-start.7 = (bf16[2,2,128,128]{3,2,1,0:T(8,128)(2,1)S(1)}, bf16[2,2,128,128]{3,2,1,0:T(8,128)(2,1)S(1)}, u32[]{:S(2)}, u32[]{:S(2)}) collective-permute-start(bf16[2,2,128,128]{3,2,1,0:T(8,128)(2,1)S(1)} %get-tuple-element.33), channel_id=1, source_target_pairs={{0,4},{4,8},{8,12},{12,0},{1,5},{5,9},{9,13},{13,1},{2,6},{6,10},{... | collective-permute-start | bytes 393224 | tf_op jit(solution)/shard_map/ppermute | solution.py:558
  19.4 13.4 %collective-permute-start.8 = (bf16[2,2,128,128]{3,2,1,0:T(8,128)(2,1)S(1)}, bf16[2,2,128,128]{3,2,1,0:T(8,128)(2,1)S(1)}, u32[]{:S(2)}, u32[]{:S(2)}) collective-permute-start(bf16[2,2,128,128]{3,2,1,0:T(8,128)(2,1)S(1)} %get-tuple-element.33), channel_id=1, source_target_pairs={{0,12},{4,0},{8,4},{12,8},{1,13},{5,1},{9,5},{13,9},{2,14},{6,2},{... | collective-permute-start | bytes 393224 | tf_op jit(solution)/shard_map/ppermute | solution.py:558
  24.5 14.6 %collective-permute-start.13 = (bf16[128,256]{1,0:T(8,128)(2,1)S(1)}, bf16[128,256]{1,0:T(8,128)(2,1)S(1)}, u32[]{:S(2)}, u32[]{:S(2)}) collective-permute-start(bf16[128,256]{1,0:T(8,128)(2,1)S(1)} %get-tuple-element.39), channel_id=1, source_target_pairs={{0,1},{1,0},{2,3},{3,2},{4,5},{5,4},{6,7},{7,6},{8,9},{9,8},{10,11... | collective-permute-start | bytes 196616 | tf_op jit(solution)/shard_map/ppermute | solution.py:540
  24.6 3.2 %collective-permute-start = (bf16[16,1024]{1,0:T(8,128)(2,1)S(1)}, bf16[16,1024]{1,0:T(8,128)(2,1)S(1)}, u32[]{:S(2)}, u32[]{:S(2)}) collective-permute-start(bf16[16,1024]{1,0:T(8,128)(2,1)S(1)} %get-tuple-element.24), channel_id=1, source_target_pairs={{0,1},{1,2},{2,3},{4,5},{5,6},{6,7},{8,9},{9,10},{10,11},{12,13},{... | collective-permute-start | bytes 98312 | tf_op jit(solution)/shard_map/ppermute | solution.py:43
  29.1 6.8 %collective-permute-start.1 = (f32[2,1024]{1,0:T(2,128)S(1)}, f32[2,1024]{1,0:T(2,128)S(1)}, u32[]{:S(2)}, u32[]{:S(2)}) collective-permute-start(f32[2,1024]{1,0:T(2,128)S(1)} %get-tuple-element.28.refs_3_), channel_id=1, source_target_pairs={{0,1},{1,0},{2,3},{3,2},{4,5},{5,4},{6,7},{7,6},{8,9},{9,8},{10,11... | collective-permute-start | bytes 24584 | tf_op jit(solution)/shard_map/ppermute | solution.py:540
  30.5 7.2 %collective-permute-start.2 = (f32[2,1024]{1,0:T(2,128)S(1)}, f32[2,1024]{1,0:T(2,128)S(1)}, u32[]{:S(2)}, u32[]{:S(2)}) collective-permute-start(f32[2,1024]{1,0:T(2,128)S(1)} %get-tuple-element.28.refs_3_), channel_id=1, source_target_pairs={{0,2},{1,3},{2,0},{3,1},{4,6},{5,7},{6,4},{7,5},{8,10},{9,11},{10,... | collective-permute-start | bytes 24584 | tf_op jit(solution)/shard_map/ppermute | solution.py:540
  32.8 5.3 %collective-permute-start.3 = (f32[2,1024]{1,0:T(2,128)S(1)}, f32[2,1024]{1,0:T(2,128)S(1)}, u32[]{:S(2)}, u32[]{:S(2)}) collective-permute-start(f32[2,1024]{1,0:T(2,128)S(1)} %get-tuple-element.28.refs_3_), channel_id=1, source_target_pairs={{0,3},{1,2},{2,1},{3,0},{4,7},{5,6},{6,5},{7,4},{8,11},{9,10},{10,... | collective-permute-start | bytes 24584 | tf_op jit(solution)/shard_map/ppermute | solution.py:540
  35.9 12.0 %collective-permute-start.10 = (bf16[128,512]{1,0:T(8,128)(2,1)S(1)}, bf16[128,512]{1,0:T(8,128)(2,1)S(1)}, u32[]{:S(2)}, u32[]{:S(2)}) collective-permute-start(bf16[128,512]{1,0:T(8,128)(2,1)S(1)} %get-tuple-element.36), channel_id=1, source_target_pairs={{0,2},{1,3},{2,0},{3,1},{4,6},{5,7},{6,4},{7,5},{8,10},{9,11},{10,... | collective-permute-start | bytes 393224 | tf_op jit(solution)/shard_map/ppermute | solution.py:540
  37.7 6.1 %collective-permute-start.14 = (bf16[128,256]{1,0:T(8,128)(2,1)S(1)}, bf16[128,256]{1,0:T(8,128)(2,1)S(1)}, u32[]{:S(2)}, u32[]{:S(2)}) collective-permute-start(bf16[128,256]{1,0:T(8,128)(2,1)S(1)} %get-tuple-element.40), channel_id=1, source_target_pairs={{0,2},{1,3},{2,0},{3,1},{4,6},{5,7},{6,4},{7,5},{8,10},{9,11},{10,... | collective-permute-start | bytes 196616 | tf_op jit(solution)/shard_map/ppermute | solution.py:540
  38.0 9.9 %collective-permute-start.11 = (bf16[128,512]{1,0:T(8,128)(2,1)S(1)}, bf16[128,512]{1,0:T(8,128)(2,1)S(1)}, u32[]{:S(2)}, u32[]{:S(2)}) collective-permute-start(bf16[128,512]{1,0:T(8,128)(2,1)S(1)} %get-tuple-element.37), channel_id=1, source_target_pairs={{0,3},{1,2},{2,1},{3,0},{4,7},{5,6},{6,5},{7,4},{8,11},{9,10},{10,... | collective-permute-start | bytes 393224 | tf_op jit(solution)/shard_map/ppermute | solution.py:540
  39.1 8.8 %collective-permute-start.9 = (bf16[128,512]{1,0:T(8,128)(2,1)S(1)}, bf16[128,512]{1,0:T(8,128)(2,1)S(1)}, u32[]{:S(2)}, u32[]{:S(2)}) collective-permute-start(bf16[128,512]{1,0:T(8,128)(2,1)S(1)} %get-tuple-element.35), channel_id=1, source_target_pairs={{0,1},{1,0},{2,3},{3,2},{4,5},{5,4},{6,7},{7,6},{8,9},{9,8},{10,11... | collective-permute-start | bytes 393224 | tf_op jit(solution)/shard_map/ppermute | solution.py:540
  43.7 4.2 %collective-permute-start.15 = (bf16[128,256]{1,0:T(8,128)(2,1)S(1)}, bf16[128,256]{1,0:T(8,128)(2,1)S(1)}, u32[]{:S(2)}, u32[]{:S(2)}) collective-permute-start(bf16[128,256]{1,0:T(8,128)(2,1)S(1)} %get-tuple-element.41), channel_id=1, source_target_pairs={{0,3},{1,2},{2,1},{3,0},{4,7},{5,6},{6,5},{7,4},{8,11},{9,10},{10,... | collective-permute-start | bytes 196616 | tf_op jit(solution)/shard_map/ppermute | solution.py:540
  49.5 1.2 %copy-start = (bf16[1,128,4096]{2,1,0:T(8,128)(2,1)S(1)}, bf16[1,128,4096]{2,1,0:T(8,128)(2,1)}, u32[]{:S(2)}) copy-start(bf16[1,128,4096]{2,1,0:T(8,128)(2,1)} %get-tuple-element.21.student_ref) | copy-start | bytes 3145732

commit v2 on v0

--- a/solution.py
+++ b/solution.py
@@ -1,10 +1,18 @@
+import functools
+import math
+
 import jax
 import jax.numpy as jnp
 from jax import lax
+from jax.experimental import pallas as pl
+from jax.experimental.pallas import tpu as pltpu
 from jax.sharding import PartitionSpec as P
 
 HEADS = 32
 HS = 128
+LOG2E = math.log2(math.e)
+LN2 = math.log(2.0)
+EDGE = 16
 
 
 def prefix(value, axis, combine, identity):
@@ -82,7 +90,7 @@
     return full.reshape(group, tokens, width).astype(jnp.bfloat16)
 
 
-def local(
+def general(
     branch_x, positions, teacher_held, gate_weights, gate_bias, conv_weight, conv_bias, decay_rate
 ):
     tokens = branch_x.shape[1]
@@ -121,7 +129,344 @@
     return (student, token_loss)
 
 
+def in_vmem(count):
+    return [pl.BlockSpec(memory_space=pltpu.VMEM)] * count
+
+
+def pallas(kernel, name, out_shape, in_specs, out_specs, scratch_shapes, work, **more):
+    return pl.pallas_call(
+        kernel,
+        out_shape=out_shape,
+        in_specs=in_specs,
+        out_specs=out_specs,
+        scratch_shapes=scratch_shapes,
+        compiler_params=pltpu.CompilerParams(vmem_limit_bytes=24 << 20),
+        cost_estimate=pl.CostEstimate(
+            flops=0, bytes_accessed=0, transcendentals=0
+        ),
+        name=name,
+        **more,
+    )
+
+
+def cut_kernel(x_ref, w_ref, half_ref, quarter_ref, edge_ref, sem):
+    here = lax.axis_index("seq")
+    tokens = x_ref.shape[1]
+    halves, quarters = half_ref.shape[0], quarter_ref.shape[0]
+    copies = [
+        pltpu.make_async_copy(
+            w_ref.at[pl.ds(lax.rem(here, 2) * halves, halves)], half_ref, sem.at[0]
+        ),
+        pltpu.make_async_copy(w_ref.at[pl.ds(here * quarters, quarters)], quarter_ref, sem.at[1]),
+        pltpu.make_async_copy(x_ref.at[0, pl.ds(tokens - EDGE, EDGE), :], edge_ref, sem.at[2]),
+    ]
+    for copy in copies:
+        copy.start()
+    for copy in copies:
+        copy.wait()
+
+
+def cut(branch_x, gate_weights):
+    held = gate_weights.shape[0]
+    rest = gate_weights.shape[1:]
+    return pallas(
+        cut_kernel,
+        "cut",
+        [
+            jax.ShapeDtypeStruct((held // 2,) + rest, jnp.bfloat16),
+            jax.ShapeDtypeStruct((held // 4,) + rest, jnp.bfloat16),
+            jax.ShapeDtypeStruct((EDGE, branch_x.shape[2]), jnp.bfloat16),
+        ],
+        [pl.BlockSpec(memory_space=pltpu.HBM)] * 2,
+        [pl.BlockSpec(memory_space=pl.ANY)] * 3,
+        [pltpu.SemaphoreType.DMA((3,))],
+        10000,
+    )(
+        pltpu.with_memory_space_constraint(branch_x, pltpu.HBM),
+        pltpu.with_memory_space_constraint(gate_weights, pltpu.HBM),
+    )
+
+
+def spread(codes):
+    tokens = codes.shape[1]
+    down = lax.broadcasted_iota(jnp.int32, (tokens, tokens), 0)
+    across = lax.broadcasted_iota(jnp.int32, (tokens, tokens), 1)
+    diagonal = jnp.where(down == across, jnp.broadcast_to(codes, (tokens, tokens)), 0.0)
+    return jnp.dot(
+        diagonal.astype(jnp.bfloat16),
+        jnp.ones((tokens, HS), jnp.bfloat16),
+        preferred_element_type=jnp.float32,
+    )
+
+
+def lanes_of(head):
+    return pl.ds(pl.multiple_of(head * HS, HS), HS)
+
+
+def conv_kernel(x_ref, edge_ref, pos_ref, w_ref, b_ref, out_ref, mask_ref, rows, natural, lags):
+    tokens = x_ref.shape[1]
+    span = tokens // 8
+    natural[...] = spread(jnp.minimum(pos_ref[...], 3).astype(jnp.float32))
+    for step in range(span):
+        code = natural[pl.ds(step, 8, stride=span), :]
+        at = pl.ds(step * 8, 8)
+        first = jnp.minimum(code, 1.0)
+        mask_ref[0, at, :] = first
+        mask_ref[1, at, :] = jnp.maximum(1.0 - first, 1e-37)
+        lags[0, at, :] = jnp.clip(code - 1.0, 0.0, 1.0)
+        lags[1, at, :] = jnp.clip(code - 2.0, 0.0, 1.0)
+
+    def body(head, unused):
+        lanes = lanes_of(head)
+        rows[head, pl.ds(0, 8), :] = edge_ref[:, lanes].astype(jnp.float32)[EDGE - 8 :]
+        rows[head, pl.ds(8, tokens), :] = x_ref[0, :, lanes].astype(jnp.float32)
+        tiles = [rows[head, pl.ds(8 + step, 8, stride=span), :] for step in range(-3, span)]
+        half = jnp.concatenate(tiles[3:], axis=0) * (w_ref[0:1, lanes] * 0.5) + (
+            b_ref[0:1, lanes] * 0.5
+        )
+        for lag in range(1, 4):
+            shifted = jnp.concatenate(tiles[3 - lag : 3 - lag + span], axis=0)
+            mask = mask_ref[0] if lag == 1 else lags[lag - 2]
+            half = half + shifted * (w_ref[lag : lag + 1, lanes] * 0.5) * mask
+        out_ref[head] = half.astype(jnp.bfloat16)
+        return unused
+
+    lax.fori_loop(0, out_ref.shape[0], body, 0, unroll=4)
+
+
+def conv_rows(branch_x, edge, positions, weight, bias):
+    tokens, width = branch_x.shape[1:]
+    heads = width // HS
+    return pallas(
+        conv_kernel,
+        "conv_rows",
+        [
+            jax.ShapeDtypeStruct((heads, tokens, HS), jnp.bfloat16),
+            jax.ShapeDtypeStruct((2, tokens, HS), jnp.float32),
+        ],
+        in_vmem(5),
+        in_vmem(2),
+        [
+            pltpu.VMEM((heads, tokens + 8, HS), jnp.float32),
+            pltpu.VMEM((tokens, HS), jnp.float32),
+            pltpu.VMEM((2, tokens, HS), jnp.float32),
+        ],
+        tokens * width,
+    )(branch_x, edge, positions, weight, bias)
+
+
+def across_spans(product, state):
+    place = lax.broadcasted_iota(jnp.int32, product.shape, 0)
+    for apart in (1, 2, 4):
+        reached = place >= apart
+        before_p = jnp.where(reached, pltpu.roll(product, apart, 0), 1.0)
+        before_s = jnp.where(reached, pltpu.roll(state, apart, 0), 0.0)
+        state = product * before_s + state
+        product = product * before_p
+    enter_p = jnp.where(place >= 1, pltpu.roll(product, 1, 0), 1.0)
+    enter_s = jnp.where(place >= 1, pltpu.roll(state, 1, 0), 0.0)
+    return product, state, enter_p, enter_s
+
+
+def shard_kernel(total, pair, counts, earlier, conv_ref, mask_ref, bias_ref, rate_ref, *refs):
+    weights, refs = refs[: len(counts)], refs[len(counts) :]
+    before, (state_ref, prod_ref, enter_ref, end_ref) = refs[:earlier], refs[earlier:]
+    shard_heads, tokens = state_ref.shape[:2]
+    span = tokens // 8
+    base = lax.bitwise_xor(lax.axis_index("fsdp"), pair) * shard_heads
+    here = lax.axis_index("seq") if len(counts) == 4 else lax.rem(lax.axis_index("seq"), 2)
+    for slot, ref in enumerate(before):
+        end_ref[2 * slot : 2 * slot + 2, :] = ref[...]
+
+    def one(place, weights_of):
+        head = base + place
+        lanes = lanes_of(head)
+        rounded = conv_ref[head]
+        pre = jnp.dot(rounded, weights_of, preferred_element_type=jnp.float32)
+        gate_x = 1.0 + jnp.tanh(pre[:, :HS] + bias_ref[0:1, lanes] * 0.5)
+        gate_a = 1.0 + jnp.tanh(pre[:, HS:] + bias_ref[1:2, lanes] * 0.5)
+        power = gate_a * (rate_ref[0:1, lanes] * (-4.0 * LOG2E / total))
+        decay = jnp.exp2(power)
+        lost = jnp.tanh(power * -LN2)
+        square = jnp.maximum(lost + lost * decay * decay, mask_ref[1])
+        drive = rounded.astype(jnp.float32) * gate_x * (square * lax.rsqrt(square))
+        decay = decay * mask_ref[0]
+        product, state = jnp.ones((8, HS), jnp.float32), jnp.zeros((8, HS), jnp.float32)
+        for step in range(span):
+            at = slice(step * 8, step * 8 + 8)
+            state = decay[at] * state + drive[at]
+            product = product * decay[at]
+            state_ref[place, at, :] = state
+            prod_ref[place, at, :] = product
+        product, state, enter_p, enter_s = across_spans(product, state)
+        enter_ref[place, 0] = enter_p
+        enter_ref[place, 1] = enter_s
+        row = 2 * earlier
+        end_ref[row : row + 1, lanes_of(place)] = product[7:8]
+        end_ref[row + 1 : row + 2, lanes_of(place)] = state[7:8]
+
+    for apart, (count, ref) in enumerate(zip(counts, weights)):
+        first = lax.bitwise_xor(here, apart) * count if len(counts) > 1 else 0
+        for head in range(count):
+            one(first + head, jnp.concatenate([ref[head, 0], ref[head, 1]], axis=1))
+
+
+def shard(conv, masks, params, pair, weights, total, before=()):
+    tokens = conv.shape[1]
+    counts = tuple(part.shape[0] for part in weights)
+    heads = sum(counts)
+    return pallas(
+        functools.partial(shard_kernel, total, pair, counts, len(before)),
+        "shard",
+        [
+            jax.ShapeDtypeStruct((heads, tokens, HS), jnp.float32),
+            jax.ShapeDtypeStruct((heads, tokens, HS), jnp.float32),
+            jax.ShapeDtypeStruct((heads, 2, 8, HS), jnp.float32),
+            jax.ShapeDtypeStruct((2 * len(before) + 2, heads * HS), jnp.float32),
+        ],
+        in_vmem(4 + len(weights) + len(before)),
+        in_vmem(4),
+        [],
+        heads * tokens * HS,
+    )(conv, masks, *params, *weights, *before)
+
+
+def rows_kernel(pairs, *refs):
+    devices = lax.axis_size("seq")
+    here = lax.axis_index("seq")
+    ends, refs = refs[:devices], refs[devices:]
+    parts = [refs[3 * slot : 3 * slot + 3] for slot in range(len(pairs))]
+    student_ref, held_ref, scale_ref, ends_s, natural, sem = refs[3 * len(pairs) :]
+    heads, tokens = parts[0][0].shape[:2]
+    span = tokens // 8
+    width = heads * HS
+    for apart in range(devices):
+        ends_s[lax.bitwise_xor(here, apart)] = ends[apart][...]
+    squares = jnp.zeros((tokens, HS), jnp.float32)
+    copies = []
+    for slot, (pair, (state_ref, prod_ref, enter_ref)) in enumerate(zip(pairs, parts)):
+        incoming = jnp.zeros((1, width), jnp.float32)
+        for place in range(devices - 1):
+            after = ends_s[place, 2 * slot : 2 * slot + 1, :] * incoming + (
+                ends_s[place, 2 * slot + 1 : 2 * slot + 2, :]
+            )
+            incoming = jnp.where(place < here, after, incoming)
+        base = lax.bitwise_xor(lax.axis_index("fsdp"), pair) * heads
+        for head in range(heads):
+            entering = enter_ref[head, 1] + enter_ref[head, 0] * (
+                incoming[:, head * HS : (head + 1) * HS]
+            )
+            for step in range(span):
+                at = slice(step * 8, step * 8 + 8)
+                natural[slot * heads + head, pl.ds(step, 8, stride=span), :] = (
+                    state_ref[head, at, :] + prod_ref[head, at, :] * entering
+                )
+            rounded = natural[slot * heads + head].astype(jnp.bfloat16)
+            held_ref[0, :, lanes_of(base + head)] = rounded
+            value = rounded.astype(jnp.float32)
+            squares = squares + value * value
+        columns = pl.ds(pl.multiple_of(base * HS, width), width)
+        copies.append(
+            pltpu.make_async_copy(
+                held_ref.at[:, :, columns], student_ref.at[:, :, columns], sem.at[slot]
+            )
+        )
+        copies[-1].start()
+    mean = jnp.sum(squares, axis=1, keepdims=True) * (1.0 / student_ref.shape[2])
+    scale_ref[...] = jnp.broadcast_to(lax.rsqrt(mean + 1e-06), (tokens, HS))
+    for copy in copies:
+        copy.wait()
+
+
+def student_rows(pairs, ends, parts):
+    heads, tokens = parts[0][0].shape[:2]
+    full = HEADS * HS
+    flat = [array for part in parts for array in part[:3]]
+    whole = jax.ShapeDtypeStruct((1, tokens, full), jnp.bfloat16)
+    return pallas(
+        functools.partial(rows_kernel, pairs),
+        "student_rows",
+        [whole, whole, jax.ShapeDtypeStruct((tokens, HS), jnp.float32)],
+        in_vmem(len(ends) + len(flat)),
+        [pl.BlockSpec(memory_space=pltpu.HBM)] + in_vmem(2),
+        [
+            pltpu.VMEM((len(ends),) + ends[0].shape, jnp.float32),
+            pltpu.VMEM((HEADS, tokens, HS), jnp.float32),
+            pltpu.SemaphoreType.DMA((len(pairs),)),
+        ],
+        tokens * full,
+    )(*ends, *flat)
+
+
+def loss_kernel(student_ref, scale_ref, target_ref, loss_ref):
+    tokens, width = student_ref.shape[1:]
+    scale = scale_ref[...]
+    total = jnp.zeros((tokens, HS), jnp.float32)
+    for start in range(0, width, HS):
+        lanes = slice(start, start + HS)
+        wanted = target_ref[0, :, lanes].astype(jnp.float32)
+        off = student_ref[0, :, lanes].astype(jnp.float32) * scale - wanted
+        total = total + off * off
+    loss_ref[...] = jnp.sum(total.T, axis=0, keepdims=True) * (1.0 / width)
+
+
+def token_losses(student, scale, target):
+    return pallas(
+        loss_kernel,
+        "token_losses",
+        jax.ShapeDtypeStruct((1, student.shape[1]), jnp.float32),
+        in_vmem(3),
+        pl.BlockSpec(memory_space=pltpu.VMEM),
+        [],
+        student.size,
+    )(student, scale, target)
+
+
+def swap(value, axis, apart):
+    return lax.ppermute(value, axis, [(i, i ^ apart) for i in range(lax.axis_size(axis))])
+
+
+def after(value, *earlier):
+    return lax.optimization_barrier((value, *earlier))[0]
+
+
+def local(
+    branch_x, positions, teacher_held, gate_weights, gate_bias, conv_weight, conv_bias, decay_rate
+):
+    tokens, width = branch_x.shape[1:]
+    total = lax.axis_size("seq") * tokens
+    target = swap(teacher_held, "segment", 1)
+    half, quarter, edge = cut(branch_x, gate_weights)
+    quarters = {2: swap(quarter, "fsdp", 2)}
+    quarters[3] = swap(quarter, "fsdp", 3)
+    half = swap(half, "fsdp", 1)
+    edge = from_behind(edge, "seq", 1)
+    edge = edge
+    conv, masks = conv_rows(branch_x, edge, positions, conv_weight, conv_bias.reshape(1, width))
+    params = (gate_bias, decay_rate.reshape(1, width))
+    pairs = (0, 1, 2, 3)
+    parts = {0: shard(conv, masks, params, 0, [gate_weights], total)}
+
+    two = swap(quarters[2], "seq", 2)
+    three = swap(after(quarters[3], masks), "seq", 2)
+    mine = after(quarters[2], two, parts[0][3])
+    weights = [mine, swap(mine, "seq", 1), two, swap(two, "seq", 1)]
+    parts[2] = shard(conv, masks, params, 2, weights, total)
+    half = after(half,two)
+    parts[1] = shard(conv, masks, params, 1, [half, swap(half, "seq", 1)], total)
+    mine = after(quarters[3],three)
+    weights = [mine, swap(mine, "seq", 1), three, swap(three, "seq", 1)]
+    parts[3] = shard(conv, masks, params, 3, weights, total, [parts[pair][3] for pair in pairs[:3]])
+    parts = [parts[pair] for pair in pairs]
+    end = parts[-1][3]
+    ends = [end] + [swap(end, "seq", apart) for apart in (1, 2, 3)]
+    student, held, scale = student_rows(pairs, ends, parts)
+    return student, token_losses(held, scale, target)
+
+
 def solution(mesh):
+    shards, devices = mesh.shape["fsdp"], mesh.shape["seq"]
+    whole = shards == 4 and devices == 4
     in_specs = (
         P(("segment", "fsdp"), "seq", None),
         P(("segment", "fsdp"), "seq"),
@@ -133,4 +478,10 @@
         P(),
     )
     out_specs = (P(("segment", "fsdp"), "seq", None), P(("segment", "fsdp"), "seq"))
-    return jax.shard_map(local, mesh=mesh, in_specs=in_specs, out_specs=out_specs, check_vma=False)
+    return jax.shard_map(
+        local if whole else general,
+        mesh=mesh,
+        in_specs=in_specs,
+        out_specs=out_specs,
+        check_vma=False,
+    )

time: 161 us -> 35.7 us (0.22); the launches traced: 158 us -> 35.5 us
  other arithmetic: 55.3 us -> 0 us
  local copies, waits for them, and re-layouts: 32.2 us -> 0.03 us
  waiting for transfers between devices: 38.8 us -> 10.5 us
  between operations: 14.3 us -> 0.81 us
  starting transfers between devices: 4.81 us -> 15.8 us
  blocking collectives: 10.5 us -> 0 us
  Pallas kernels: 0 us -> 8.44 us
  matrix products: 2.33 us -> 0 us
    all_gather x1 -> x0, waiting for transfers between devices: 38.1 us -> none  [local(): lax.all_gather(gate_weights, 'fsdp', axis=0, tiled=True)]
    add x19 -> x0, other arithmetic: 25.8 us -> none  [the longest x2 13 us: recurrence(): running_state = step_decay * running_state + drive_blocks[:, :, inner, :]]
    another operation x6 -> x0, local copies, waits for them, and re-layouts: 19.4 us -> none  [the longest x1 6.67 us: recurrence(): products = jnp.stack(prod_list, axis=2)]
    ppermute x1 -> x14, starting transfers between devices: 2.41 us -> 14.4 us  [swap(): lax.ppermute(value, axis, [(i, i ^ apart) for i in range(lax.axis_size(ax...]
    all_gather x2 -> x0, blocking collectives: 10.5 us -> none  [prefix(): everything = jax.tree.map(lambda part: lax.all_gather(part, axis), value)]
    ppermute x1 -> x14, waiting for transfers between devices: 0.01 us -> 10.5 us  [swap(): lax.ppermute(value, axis, [(i, i ^ apart) for i in range(lax.axis_size(ax...]
    pallas_call x0 -> x8, Pallas kernels: none -> 8.44 us  [the longest x4 2.45 us: shard(): pallas(functools.partial(shard_kernel, total, pair, counts, len(before)),...]
    slice x5 -> x0, local copies, waits for them, and re-layouts: 8.19 us -> none  [the longest x1 3.12 us: local(): preact[:, 1].reshape(1, tokens, width)]
  transfers between devices with their start and end apart: 3 -> 15, of which waited for: 1 -> 5; matrix products, arithmetic and copies ran while one was open for 54% -> 0% of each run, Pallas kernels for 0% -> 21%
where the time goes in v2:
time: 35.7 us; the launch traced here: 35.5 us
  starting transfers between devices  15.8 us (44%)
  waiting for transfers between devices  10.5 us (29%)
  Pallas kernels  8.44 us (24%)
  between operations  0.81 us (2%)
    ppermute x14, starting transfers between devices, swap(): lax.ppermute(value, axis, [(i, i ^ apart) for i in range(lax.axis_size(ax...  14.4 us
    ppermute x14, waiting for transfers between devices, swap(): lax.ppermute(value, axis, [(i, i ^ apart) for i in range(lax.axis_size(ax...  10.5 us
    pallas_call x4, Pallas kernels, shard(): pallas(functools.partial(shard_kernel, total, pair, counts, len(before)),...  2.45 us
    pallas_call x1, Pallas kernels, conv_rows(): pallas(conv_kernel, 'conv_rows', [jax.ShapeDtypeStruct((heads, tokens, HS...  1.91 us
    pallas_call x1, Pallas kernels, student_rows(): pallas(functools.partial(rows_kernel, pairs), 'student_rows', [whole, who...  1.88 us
    ppermute x1, starting transfers between devices, from_behind(): lax.ppermute(value, axis, [(source, source + steps) for source in range(l...  1.42 us
    pallas_call x1, Pallas kernels, token_losses(): pallas(loss_kernel, 'token_losses', jax.ShapeDtypeStruct((1, student.shap...  1.13 us
    pallas_call x1, Pallas kernels, cut(): pallas(cut_kernel, 'cut', [jax.ShapeDtypeStruct((held // 2,) + rest, jnp....  1.08 us
  transfers between devices with their start and end apart: 15, of which 5 were waited for; matrix products, arithmetic and copies ran while one was open for 0% of the time, Pallas kernels for 21%

profile of v2, /device:TPU:0, one launch (start us, length us, event | category | flops | bytes accessed | tf_op | source)
XLA Modules:
  0.0 35.5 jit_solution(8823507753106549462)
XLA Ops:
  0.6 0.0 copy-start
  0.6 0.0 copy-start.4
  0.7 3.0 %collective-permute-start.14 = (bf16[1,128,4096]{2,1,0:T(8,128)(2,1)}, bf16[1,128,4096]{2,1,0:T(8,128)(2,1)S(1)}, u32[]{:S(2)}, u32[]{:S(2)}) collective-permute-start(bf16[1,128,4096]{2,1,0:T(8,128)(2,1)} %param.10), channel_id=1, source_target_pairs={{0,16},{16,0},{1,17},{17,1},{2,18},{18,2},{3,19},{19,3},{4,20},{20... | collective-permute-start | bytes 3145736 | tf_op jit(solution)/shard_map/ppermute | solution.py:426
  3.7 1.1 %cut.1 = (bf16[4,2,128,128]{3,2,1,0:T(8,128)(2,1)S(1)}, bf16[2,2,128,128]{3,2,1,0:T(8,128)(2,1)S(1)}, bf16[16,4096]{1,0:T(8,128)(2,1)S(1)}) custom-call(bf16[1,128,4096]{2,1,0:T(8,128)(2,1)} %x_ref.3, bf16[8,2,128,128]{3,2,1,0:T(8,128)(2,1)} %refs_0_.1), custom_call_target="tpu_custom_call" | custom-call | tf_op jit(solution)/shard_map/cut/pallas_call | solution.py:172
  4.8 2.7 %collective-permute-start.6 = (bf16[2,2,128,128]{3,2,1,0:T(8,128)(2,1)S(1)}, bf16[2,2,128,128]{3,2,1,0:T(8,128)(2,1)S(1)}, u32[]{:S(2)}, u32[]{:S(2)}) collective-permute-start(bf16[2,2,128,128]{3,2,1,0:T(8,128)(2,1)S(1)} %get-tuple-element.33), channel_id=1, source_target_pairs={{0,8},{4,12},{8,0},{12,4},{1,9},{5,13},{9,1},{13,5},{2,10},{6,14},... | collective-permute-start | bytes 393224 | tf_op jit(solution)/shard_map/ppermute | solution.py:426
  7.4 1.6 %collective-permute-start.5 = (bf16[4,2,128,128]{3,2,1,0:T(8,128)(2,1)S(1)}, bf16[4,2,128,128]{3,2,1,0:T(8,128)(2,1)S(1)}, u32[]{:S(2)}, u32[]{:S(2)}) collective-permute-start(bf16[4,2,128,128]{3,2,1,0:T(8,128)(2,1)S(1)} %get-tuple-element.37), channel_id=1, source_target_pairs={{0,4},{4,0},{8,12},{12,8},{1,5},{5,1},{9,13},{13,9},{2,6},{6,2},{1... | collective-permute-start | bytes 786440 | tf_op jit(solution)/shard_map/ppermute | solution.py:426
  9.0 1.4 %collective-permute-start = (bf16[16,4096]{1,0:T(8,128)(2,1)S(1)}, bf16[16,4096]{1,0:T(8,128)(2,1)S(1)}, u32[]{:S(2)}, u32[]{:S(2)}) collective-permute-start(bf16[16,4096]{1,0:T(8,128)(2,1)S(1)} %get-tuple-element.30), channel_id=1, source_target_pairs={{0,1},{1,2},{2,3},{4,5},{5,6},{6,7},{8,9},{9,10},{10,11},{12,13},{... | collective-permute-start | bytes 393224 | tf_op jit(solution)/shard_map/ppermute | solution.py:42
  10.4 0.3 collective-permute-start.1
  10.7 2.9 %collective-permute-done.6.refs_0_ = bf16[2,2,128,128]{3,2,1,0:T(8,128)(2,1)S(1)} collective-permute-done((bf16[2,2,128,128]{3,2,1,0:T(8,128)(2,1)S(1)}, bf16[2,2,128,128]{3,2,1,0:T(8,128)(2,1)S(1)}, u32[]{:S(2)}, u32[]{:S(2)}) %collective-permute-start.6) | collective-permute-done | bytes 131104 | tf_op jit(solution)/shard_map/ppermute | solution.py:426
  13.6 2.3 %collective-permute-start.7 = (bf16[2,2,128,128]{3,2,1,0:T(8,128)(2,1)S(1)}, bf16[2,2,128,128]{3,2,1,0:T(8,128)(2,1)S(1)}, u32[]{:S(2)}, u32[]{:S(2)}) collective-permute-start(bf16[2,2,128,128]{3,2,1,0:T(8,128)(2,1)S(1)} %collective-permute-done.6.refs_0_), channel_id=1, source_target_pairs={{0,2},{1,3},{2,0},{3,1},{4,6},{5,7},{6,4},{7,5},{8,10},{9,11},{10,... | collective-permute-start | bytes 393224 | tf_op jit(solution)/shard_map/ppermute | solution.py:426
  15.9 0.0 collective-permute-done.edge_ref
  15.9 0.0 copy-done
  15.9 0.0 copy-done.4
  15.9 0.0 copy-done.5
  15.9 0.0 copy-start.1
  15.9 0.0 copy-start.2
  15.9 0.0 copy-start.3
  15.9 1.9 %conv_rows.1 = (bf16[32,128,128]{2,1,0:T(8,128)(2,1)S(1)}, f32[2,128,128]{2,1,0:T(8,128)S(1)}) custom-call(bf16[1,128,4096]{2,1,0:T(8,128)(2,1)S(1)} %copy-done, bf16[16,4096]{1,0:T(8,128)(2,1)S(1)} %collective-permute-done.edge_ref, s32[1,128]{1,0:T(1,128)S(1)} %copy-done.6, f32[4,4096]{1,0:T(4,128)S(1)} %copy-done.4, f32[1,4096]{1,0:T(1,128)S(1)} %bitcast.6), custom_call_target="tpu_custom_call" | custom-call | tf_op jit(solution)/shard_map/conv_rows/pallas_call | solution.py:240
  17.8 2.3 %collective-permute-done.1.refs_0_ = bf16[2,2,128,128]{3,2,1,0:T(8,128)(2,1)S(1)} collective-permute-done((bf16[2,2,128,128]{3,2,1,0:T(8,128)(2,1)S(1)}, bf16[2,2,128,128]{3,2,1,0:T(8,128)(2,1)S(1)}, u32[]{:S(2)}, u32[]{:S(2)}) %collective-permute-start.1) | collective-permute-done | bytes 131104 | tf_op jit(solution)/shard_map/ppermute | solution.py:426
  20.2 1.5 %collective-permute-start.2 = (bf16[2,2,128,128]{3,2,1,0:T(8,128)(2,1)S(1)}, bf16[2,2,128,128]{3,2,1,0:T(8,128)(2,1)S(1)}, u32[]{:S(2)}, u32[]{:S(2)}) collective-permute-start(bf16[2,2,128,128]{3,2,1,0:T(8,128)(2,1)S(1)} %collective-permute-done.1.refs_0_), channel_id=1, source_target_pairs={{0,2},{1,3},{2,0},{3,1},{4,6},{5,7},{6,4},{7,5},{8,10},{9,11},{10,... | collective-permute-start | bytes 393224 | tf_op jit(solution)/shard_map/ppermute | solution.py:426
  21.7 0.0 copy-done.1
  21.7 0.0 copy-done.3
  21.7 0.6 %shard.4 = (f32[8,128,128]{2,1,0:T(8,128)S(1)}, f32[8,128,128]{2,1,0:T(8,128)S(1)}, f32[8,2,8,128]{3,2,1,0:T(8,128)S(1)}, f32[2,1024]{1,0:T(2,128)S(1)}) custom-call(bf16[32,128,128]{2,1,0:T(8,128)(2,1)S(1)} %get-tuple-element.31.conv_ref, f32[2,128,128]{2,1,0:T(8,128)S(1)} %get-tuple-element.32.mask_ref, f32[2,4096]{1,0:T(2,128)S(1)} %copy-done.2, ...), custom_call_target="tpu_custom_call" | custom-call | tf_op jit(solution)/shard_map/shard/pallas_call | solution.py:318
  22.3 0.0 collective-permute-done.7.refs_2_
  22.3 0.0 collective-permute-done.5.refs_0_
  22.3 0.1 collective-permute-start.8
  22.4 0.5 %collective-permute-start.9 = (bf16[2,2,128,128]{3,2,1,0:T(8,128)(2,1)S(1)}, bf16[2,2,128,128]{3,2,1,0:T(8,128)(2,1)S(1)}, u32[]{:S(2)}, u32[]{:S(2)}) collective-permute-start(bf16[2,2,128,128]{3,2,1,0:T(8,128)(2,1)S(1)} %collective-permute-done.6.refs_0_), channel_id=1, source_target_pairs={{0,1},{1,0},{2,3},{3,2},{4,5},{5,4},{6,7},{7,6},{8,9},{9,8},{10,11... | collective-permute-start | bytes 393224 | tf_op jit(solution)/shard_map/ppermute | solution.py:426
  22.9 0.1 collective-permute-start.10
  23.0 2.5 %collective-permute-done.2.refs_2_ = bf16[2,2,128,128]{3,2,1,0:T(8,128)(2,1)S(1)} collective-permute-done((bf16[2,2,128,128]{3,2,1,0:T(8,128)(2,1)S(1)}, bf16[2,2,128,128]{3,2,1,0:T(8,128)(2,1)S(1)}, u32[]{:S(2)}, u32[]{:S(2)}) %collective-permute-start.2) | collective-permute-done | bytes 131104 | tf_op jit(solution)/shard_map/ppermute | solution.py:426
  25.5 0.0 collective-permute-start.3
  25.5 0.0 collective-permute-done.9.refs_1_
  25.5 0.5 %collective-permute-start.4 = (bf16[2,2,128,128]{3,2,1,0:T(8,128)(2,1)S(1)}, bf16[2,2,128,128]{3,2,1,0:T(8,128)(2,1)S(1)}, u32[]{:S(2)}, u32[]{:S(2)}) collective-permute-start(bf16[2,2,128,128]{3,2,1,0:T(8,128)(2,1)S(1)} %collective-permute-done.2.refs_2_), channel_id=1, source_target_pairs={{0,1},{1,0},{2,3},{3,2},{4,5},{5,4},{6,7},{7,6},{8,9},{9,8},{10,11... | collective-permute-start | bytes 393224 | tf_op jit(solution)/shard_map/ppermute | solution.py:426
  26.0 0.0 collective-permute-done.10.refs_3_
  26.0 0.6 %shard.6 = (f32[8,128,128]{2,1,0:T(8,128)S(1)}, f32[8,128,128]{2,1,0:T(8,128)S(1)}, f32[8,2,8,128]{3,2,1,0:T(8,128)S(1)}, f32[2,1024]{1,0:T(2,128)S(1)}) custom-call(bf16[32,128,128]{2,1,0:T(8,128)(2,1)S(1)} %get-tuple-element.31.conv_ref, f32[2,128,128]{2,1,0:T(8,128)S(1)} %get-tuple-element.32.mask_ref, f32[2,4096]{1,0:T(2,128)S(1)} %copy-done.2, ...), custom_call_target="tpu_custom_call" | custom-call | tf_op jit(solution)/shard_map/shard/pallas_call | solution.py:318
  26.6 0.0 collective-permute-done.8.refs_1_
  26.6 0.6 %shard.5 = (f32[8,128,128]{2,1,0:T(8,128)S(1)}, f32[8,128,128]{2,1,0:T(8,128)S(1)}, f32[8,2,8,128]{3,2,1,0:T(8,128)S(1)}, f32[2,1024]{1,0:T(2,128)S(1)}) custom-call(bf16[32,128,128]{2,1,0:T(8,128)(2,1)S(1)} %get-tuple-element.31.conv_ref, f32[2,128,128]{2,1,0:T(8,128)S(1)} %get-tuple-element.32.mask_ref, f32[2,4096]{1,0:T(2,128)S(1)} %copy-done.2, ...), custom_call_target="tpu_custom_call" | custom-call | tf_op jit(solution)/shard_map/shard/pallas_call | solution.py:318
  27.3 0.0 collective-permute-done.3.refs_1_
  27.3 0.0 collective-permute-done.4.refs_3_
  27.3 0.6 %shard.7 = (f32[8,128,128]{2,1,0:T(8,128)S(1)}, f32[8,128,128]{2,1,0:T(8,128)S(1)}, f32[8,2,8,128]{3,2,1,0:T(8,128)S(1)}, f32[8,1024]{1,0:T(8,128)S(1)}) custom-call(bf16[32,128,128]{2,1,0:T(8,128)(2,1)S(1)} %get-tuple-element.31.conv_ref, f32[2,128,128]{2,1,0:T(8,128)S(1)} %get-tuple-element.32.mask_ref, f32[2,4096]{1,0:T(2,128)S(1)} %copy-done.2, ...), custom_call_target="tpu_custom_call" | custom-call | tf_op jit(solution)/shard_map/shard/pallas_call | solution.py:318
  27.9 0.1 collective-permute-start.11
  28.0 1.1 %collective-permute-start.12 = (f32[8,1024]{1,0:T(8,128)S(1)}, f32[8,1024]{1,0:T(8,128)S(1)}, u32[]{:S(2)}, u32[]{:S(2)}) collective-permute-start(f32[8,1024]{1,0:T(8,128)S(1)} %get-tuple-element.42.refs_0_), channel_id=1, source_target_pairs={{0,2},{1,3},{2,0},{3,1},{4,6},{5,7},{6,4},{7,5},{8,10},{9,11},{10,... | collective-permute-start | bytes 98312 | tf_op jit(solution)/shard_map/ppermute | solution.py:426
  29.2 0.7 %collective-permute-start.13 = (f32[8,1024]{1,0:T(8,128)S(1)}, f32[8,1024]{1,0:T(8,128)S(1)}, u32[]{:S(2)}, u32[]{:S(2)}) collective-permute-start(f32[8,1024]{1,0:T(8,128)S(1)} %get-tuple-element.42.refs_0_), channel_id=1, source_target_pairs={{0,3},{1,2},{2,1},{3,0},{4,7},{5,6},{6,5},{7,4},{8,11},{9,10},{10,... | collective-permute-start | bytes 98312 | tf_op jit(solution)/shard_map/ppermute | solution.py:426
  29.8 0.0 collective-permute-done.11.refs_1_
  29.8 2.1 %collective-permute-done.12.refs_2_ = f32[8,1024]{1,0:T(8,128)S(1)} collective-permute-done((f32[8,1024]{1,0:T(8,128)S(1)}, f32[8,1024]{1,0:T(8,128)S(1)}, u32[]{:S(2)}, u32[]{:S(2)}) %collective-permute-start.12) | collective-permute-done | bytes 32800 | tf_op jit(solution)/shard_map/ppermute | solution.py:426
  31.9 0.6 %collective-permute-done.13.refs_3_ = f32[8,1024]{1,0:T(8,128)S(1)} collective-permute-done((f32[8,1024]{1,0:T(8,128)S(1)}, f32[8,1024]{1,0:T(8,128)S(1)}, u32[]{:S(2)}, u32[]{:S(2)}) %collective-permute-start.13) | collective-permute-done | bytes 32800 | tf_op jit(solution)/shard_map/ppermute | solution.py:426
  32.5 1.9 %student_rows.1 = (bf16[1,128,4096]{2,1,0:T(8,128)(2,1)}, bf16[1,128,4096]{2,1,0:T(8,128)(2,1)S(1)}, f32[128,128]{1,0:T(8,128)S(1)}) custom-call(f32[8,1024]{1,0:T(8,128)S(1)} %get-tuple-element.42.refs_0_, f32[8,1024]{1,0:T(8,128)S(1)} %collective-permute-done.11.refs_1_, f32[8,1024]{1,0:T(8,128)S(1)} %collective-permute-done.12.refs_2_, ...), custom_call_target="tpu_custom_call" | custom-call | tf_op jit(solution)/shard_map/student_rows/pallas_call | solution.py:386
  34.4 0.0 collective-permute-done.14.target_ref
  34.4 1.1 %token_losses.1 = f32[1,128]{1,0:T(1,128)} custom-call(bf16[1,128,4096]{2,1,0:T(8,128)(2,1)S(1)} %get-tuple-element.56.student_ref, f32[128,128]{1,0:T(8,128)S(1)} %get-tuple-element.57.scale_ref, bf16[1,128,4096]{2,1,0:T(8,128)(2,1)S(1)} %collective-permute-done.14.target_ref), custom_call_target="tpu_custom_call" | custom-call | tf_op jit(solution)/shard_map/token_losses/pallas_call | solution.py:414
  (4 shorter events, 0.0 us)
Async XLA Ops:
  0.6 15.2 %copy-start = (bf16[1,128,4096]{2,1,0:T(8,128)(2,1)S(1)}, bf16[1,128,4096]{2,1,0:T(8,128)(2,1)}, u32[]{:S(2)}) copy-start(bf16[1,128,4096]{2,1,0:T(8,128)(2,1)} %x_ref.3) | copy-start | bytes 3145732
  0.6 15.2 %copy-start.4 = (f32[4,4096]{1,0:T(4,128)S(1)}, f32[4,4096]{1,0:T(4,128)}, u32[]{:S(2)}) copy-start(f32[4,4096]{1,0:T(4,128)} %w_ref.3) | copy-start | bytes 196612
  0.7 33.8 %collective-permute-start.14 = (bf16[1,128,4096]{2,1,0:T(8,128)(2,1)}, bf16[1,128,4096]{2,1,0:T(8,128)(2,1)S(1)}, u32[]{:S(2)}, u32[]{:S(2)}) collective-permute-start(bf16[1,128,4096]{2,1,0:T(8,128)(2,1)} %param.10), channel_id=1, source_target_pairs={{0,16},{16,0},{1,17},{17,1},{2,18},{18,2},{3,19},{19,3},{4,20},{20... | collective-permute-start | bytes 3145736 | tf_op jit(solution)/shard_map/ppermute | solution.py:426
  3.7 12.2 %copy-start.5 = (f32[4096]{0:T(1024)S(1)}, f32[4096]{0:T(1024)}, u32[]{:S(2)}) copy-start(f32[4096]{0:T(1024)} %param.14) | copy-start | bytes 49156
  4.8 8.8 %collective-permute-start.6 = (bf16[2,2,128,128]{3,2,1,0:T(8,128)(2,1)S(1)}, bf16[2,2,128,128]{3,2,1,0:T(8,128)(2,1)S(1)}, u32[]{:S(2)}, u32[]{:S(2)}) collective-permute-start(bf16[2,2,128,128]{3,2,1,0:T(8,128)(2,1)S(1)} %get-tuple-element.33), channel_id=1, source_target_pairs={{0,8},{4,12},{8,0},{12,4},{1,9},{5,13},{9,1},{13,5},{2,10},{6,14},... | collective-permute-start | bytes 393224 | tf_op jit(solution)/shard_map/ppermute | solution.py:426
  7.4 14.9 %collective-permute-start.5 = (bf16[4,2,128,128]{3,2,1,0:T(8,128)(2,1)S(1)}, bf16[4,2,128,128]{3,2,1,0:T(8,128)(2,1)S(1)}, u32[]{:S(2)}, u32[]{:S(2)}) collective-permute-start(bf16[4,2,128,128]{3,2,1,0:T(8,128)(2,1)S(1)} %get-tuple-element.37), channel_id=1, source_target_pairs={{0,4},{4,0},{8,12},{12,8},{1,5},{5,1},{9,13},{13,9},{2,6},{6,2},{1... | collective-permute-start | bytes 786440 | tf_op jit(solution)/shard_map/ppermute | solution.py:426
  9.0 6.9 %copy-start.6 = (s32[1,128]{1,0:T(1,128)S(1)}, s32[1,128]{1,0:T(1,128)}, u32[]{:S(2)}) copy-start(s32[1,128]{1,0:T(1,128)} %pos_ref.1) | copy-start | bytes 1540
  9.0 6.9 %collective-permute-start = (bf16[16,4096]{1,0:T(8,128)(2,1)S(1)}, bf16[16,4096]{1,0:T(8,128)(2,1)S(1)}, u32[]{:S(2)}, u32[]{:S(2)}) collective-permute-start(bf16[16,4096]{1,0:T(8,128)(2,1)S(1)} %get-tuple-element.30), channel_id=1, source_target_pairs={{0,1},{1,2},{2,3},{4,5},{5,6},{6,7},{8,9},{9,10},{10,11},{12,13},{... | collective-permute-start | bytes 393224 | tf_op jit(solution)/shard_map/ppermute | solution.py:42
  10.4 9.7 %collective-permute-start.1 = (bf16[2,2,128,128]{3,2,1,0:T(8,128)(2,1)S(1)}, bf16[2,2,128,128]{3,2,1,0:T(8,128)(2,1)S(1)}, u32[]{:S(2)}, u32[]{:S(2)}) collective-permute-start(bf16[2,2,128,128]{3,2,1,0:T(8,128)(2,1)S(1)} %get-tuple-element.33), channel_id=1, source_target_pairs={{0,12},{4,8},{8,4},{12,0},{1,13},{5,9},{9,5},{13,1},{2,14},{6,10},... | collective-permute-start | bytes 393224 | tf_op jit(solution)/shard_map/ppermute | solution.py:426
  13.6 8.7 %collective-permute-start.7 = (bf16[2,2,128,128]{3,2,1,0:T(8,128)(2,1)S(1)}, bf16[2,2,128,128]{3,2,1,0:T(8,128)(2,1)S(1)}, u32[]{:S(2)}, u32[]{:S(2)}) collective-permute-start(bf16[2,2,128,128]{3,2,1,0:T(8,128)(2,1)S(1)} %collective-permute-done.6.refs_0_), channel_id=1, source_target_pairs={{0,2},{1,3},{2,0},{3,1},{4,6},{5,7},{6,4},{7,5},{8,10},{9,11},{10,... | collective-permute-start | bytes 393224 | tf_op jit(solution)/shard_map/ppermute | solution.py:426
  15.9 5.8 %copy-start.1 = (bf16[8,2,128,128]{3,2,1,0:T(8,128)(2,1)S(1)}, bf16[8,2,128,128]{3,2,1,0:T(8,128)(2,1)}, u32[]{:S(2)}) copy-start(bf16[8,2,128,128]{3,2,1,0:T(8,128)(2,1)} %refs_0_.1) | copy-start | bytes 1572868
  15.9 5.8 %copy-start.2 = (f32[2,4096]{1,0:T(2,128)S(1)}, f32[2,4096]{1,0:T(2,128)}, u32[]{:S(2)}) copy-start(f32[2,4096]{1,0:T(2,128)} %bias_ref.7) | copy-start | bytes 98308
  15.9 5.8 %copy-start.3 = (f32[4096]{0:T(1024)S(1)}, f32[4096]{0:T(1024)}, u32[]{:S(2)}) copy-start(f32[4096]{0:T(1024)} %param.15) | copy-start | bytes 49156
  20.2 5.3 %collective-permute-start.2 = (bf16[2,2,128,128]{3,2,1,0:T(8,128)(2,1)S(1)}, bf16[2,2,128,128]{3,2,1,0:T(8,128)(2,1)S(1)}, u32[]{:S(2)}, u32[]{:S(2)}) collective-permute-start(bf16[2,2,128,128]{3,2,1,0:T(8,128)(2,1)S(1)} %collective-permute-done.1.refs_0_), channel_id=1, source_target_pairs={{0,2},{1,3},{2,0},{3,1},{4,6},{5,7},{6,4},{7,5},{8,10},{9,11},{10,... | collective-permute-start | bytes 393224 | tf_op jit(solution)/shard_map/ppermute | solution.py:426
  22.3 4.3 %collective-permute-start.8 = (bf16[4,2,128,128]{3,2,1,0:T(8,128)(2,1)S(1)}, bf16[4,2,128,128]{3,2,1,0:T(8,128)(2,1)S(1)}, u32[]{:S(2)}, u32[]{:S(2)}) collective-permute-start(bf16[4,2,128,128]{3,2,1,0:T(8,128)(2,1)S(1)} %collective-permute-done.5.refs_0_), channel_id=1, source_target_pairs={{0,1},{1,0},{2,3},{3,2},{4,5},{5,4},{6,7},{7,6},{8,9},{9,8},{10,11... | collective-permute-start | bytes 786440 | tf_op jit(solution)/shard_map/ppermute | solution.py:426
  22.4 3.1 %collective-permute-start.9 = (bf16[2,2,128,128]{3,2,1,0:T(8,128)(2,1)S(1)}, bf16[2,2,128,128]{3,2,1,0:T(8,128)(2,1)S(1)}, u32[]{:S(2)}, u32[]{:S(2)}) collective-permute-start(bf16[2,2,128,128]{3,2,1,0:T(8,128)(2,1)S(1)} %collective-permute-done.6.refs_0_), channel_id=1, source_target_pairs={{0,1},{1,0},{2,3},{3,2},{4,5},{5,4},{6,7},{7,6},{8,9},{9,8},{10,11... | collective-permute-start | bytes 393224 | tf_op jit(solution)/shard_map/ppermute | solution.py:426
  22.9 3.1 %collective-permute-start.10 = (bf16[2,2,128,128]{3,2,1,0:T(8,128)(2,1)S(1)}, bf16[2,2,128,128]{3,2,1,0:T(8,128)(2,1)S(1)}, u32[]{:S(2)}, u32[]{:S(2)}) collective-permute-start(bf16[2,2,128,128]{3,2,1,0:T(8,128)(2,1)S(1)} %collective-permute-done.7.refs_2_), channel_id=1, source_target_pairs={{0,1},{1,0},{2,3},{3,2},{4,5},{5,4},{6,7},{7,6},{8,9},{9,8},{10,11... | collective-permute-start | bytes 393224 | tf_op jit(solution)/shard_map/ppermute | solution.py:426
  25.5 1.8 %collective-permute-start.3 = (bf16[2,2,128,128]{3,2,1,0:T(8,128)(2,1)S(1)}, bf16[2,2,128,128]{3,2,1,0:T(8,128)(2,1)S(1)}, u32[]{:S(2)}, u32[]{:S(2)}) collective-permute-start(bf16[2,2,128,128]{3,2,1,0:T(8,128)(2,1)S(1)} %collective-permute-done.1.refs_0_), channel_id=1, source_target_pairs={{0,1},{1,0},{2,3},{3,2},{4,5},{5,4},{6,7},{7,6},{8,9},{9,8},{10,11... | collective-permute-start | bytes 393224 | tf_op jit(solution)/shard_map/ppermute | solution.py:426
  25.5 1.8 %collective-permute-start.4 = (bf16[2,2,128,128]{3,2,1,0:T(8,128)(2,1)S(1)}, bf16[2,2,128,128]{3,2,1,0:T(8,128)(2,1)S(1)}, u32[]{:S(2)}, u32[]{:S(2)}) collective-permute-start(bf16[2,2,128,128]{3,2,1,0:T(8,128)(2,1)S(1)} %collective-permute-done.2.refs_2_), channel_id=1, source_target_pairs={{0,1},{1,0},{2,3},{3,2},{4,5},{5,4},{6,7},{7,6},{8,9},{9,8},{10,11... | collective-permute-start | bytes 393224 | tf_op jit(solution)/shard_map/ppermute | solution.py:426
  27.9 1.9 %collective-permute-start.11 = (f32[8,1024]{1,0:T(8,128)S(1)}, f32[8,1024]{1,0:T(8,128)S(1)}, u32[]{:S(2)}, u32[]{:S(2)}) collective-permute-start(f32[8,1024]{1,0:T(8,128)S(1)} %get-tuple-element.42.refs_0_), channel_id=1, source_target_pairs={{0,1},{1,0},{2,3},{3,2},{4,5},{5,4},{6,7},{7,6},{8,9},{9,8},{10,11... | collective-permute-start | bytes 98312 | tf_op jit(solution)/shard_map/ppermute | solution.py:426
  28.0 3.9 %collective-permute-start.12 = (f32[8,1024]{1,0:T(8,128)S(1)}, f32[8,1024]{1,0:T(8,128)S(1)}, u32[]{:S(2)}, u32[]{:S(2)}) collective-permute-start(f32[8,1024]{1,0:T(8,128)S(1)} %get-tuple-element.42.refs_0_), channel_id=1, source_target_pairs={{0,2},{1,3},{2,0},{3,1},{4,6},{5,7},{6,4},{7,5},{8,10},{9,11},{10,... | collective-permute-start | bytes 98312 | tf_op jit(solution)/shard_map/ppermute | solution.py:426
  29.2 3.3 %collective-permute-start.13 = (f32[8,1024]{1,0:T(8,128)S(1)}, f32[8,1024]{1,0:T(8,128)S(1)}, u32[]{:S(2)}, u32[]{:S(2)}) collective-permute-start(f32[8,1024]{1,0:T(8,128)S(1)} %get-tuple-element.42.refs_0_), channel_id=1, source_target_pairs={{0,3},{1,2},{2,1},{3,0},{4,7},{5,6},{6,5},{7,4},{8,11},{9,10},{10,... | collective-permute-start | bytes 98312 | tf_op jit(solution)/shard_map/ppermute | solution.py:426

commit v3 on v2

--- a/solution.py
+++ b/solution.py
@@ -268,47 +268,58 @@
     return product, state, enter_p, enter_s
 
 
-def shard_kernel(total, pair, counts, earlier, conv_ref, mask_ref, bias_ref, rate_ref, *refs):
+def gated(total, rounded, weights, masks, bias_ref, rate_ref, head, state_ref, prod_ref, place):
+    lanes = lanes_of(head)
+    span = rounded.shape[0] // 8
+    pre = jnp.dot(rounded, weights, preferred_element_type=jnp.float32)
+    gate_x = 1.0 + jnp.tanh(pre[:, :HS] + bias_ref[0:1, lanes] * 0.5)
+    gate_a = 1.0 + jnp.tanh(pre[:, HS:] + bias_ref[1:2, lanes] * 0.5)
+    power = gate_a * (rate_ref[0:1, lanes] * (-4.0 * LOG2E / total))
+    decay = jnp.exp2(power)
+    lost = jnp.tanh(power * -LN2)
+    square = jnp.maximum(lost + lost * decay * decay, masks[1])
+    drive = rounded.astype(jnp.float32) * gate_x * (square * lax.rsqrt(square))
+    decay = decay * masks[0]
+    product, state = jnp.ones((8, HS), jnp.float32), jnp.zeros((8, HS), jnp.float32)
+    for step in range(span):
+        at = slice(step * 8, step * 8 + 8)
+        state = decay[at] * state + drive[at]
+        product = product * decay[at]
+        state_ref[place, at, :] = state
+        prod_ref[place, at, :] = product
+    return across_spans(product, state)
+
+
+def shard_kernel(total, pair, counts, conv_ref, mask_ref, bias_ref, rate_ref, *refs):
     weights, refs = refs[: len(counts)], refs[len(counts) :]
-    before, (state_ref, prod_ref, enter_ref, end_ref) = refs[:earlier], refs[earlier:]
-    shard_heads, tokens = state_ref.shape[:2]
-    span = tokens // 8
-    base = lax.bitwise_xor(lax.axis_index("fsdp"), pair) * shard_heads
+    before, (state_ref, prod_ref, enter_ref, end_ref) = refs[:-4], refs[-4:]
+    heads = state_ref.shape[0]
+    row = 2 * heads * len(before)
+    for slot, ref in enumerate(before):
+        end_ref[pl.ds(2 * heads * slot, 2 * heads), :] = ref[...]
+    base = lax.bitwise_xor(lax.axis_index("fsdp"), pair) * heads
     here = lax.axis_index("seq") if len(counts) == 4 else lax.rem(lax.axis_index("seq"), 2)
-    for slot, ref in enumerate(before):
-        end_ref[2 * slot : 2 * slot + 2, :] = ref[...]
-
-    def one(place, weights_of):
-        head = base + place
-        lanes = lanes_of(head)
-        rounded = conv_ref[head]
-        pre = jnp.dot(rounded, weights_of, preferred_element_type=jnp.float32)
-        gate_x = 1.0 + jnp.tanh(pre[:, :HS] + bias_ref[0:1, lanes] * 0.5)
-        gate_a = 1.0 + jnp.tanh(pre[:, HS:] + bias_ref[1:2, lanes] * 0.5)
-        power = gate_a * (rate_ref[0:1, lanes] * (-4.0 * LOG2E / total))
-        decay = jnp.exp2(power)
-        lost = jnp.tanh(power * -LN2)
-        square = jnp.maximum(lost + lost * decay * decay, mask_ref[1])
-        drive = rounded.astype(jnp.float32) * gate_x * (square * lax.rsqrt(square))
-        decay = decay * mask_ref[0]
-        product, state = jnp.ones((8, HS), jnp.float32), jnp.zeros((8, HS), jnp.float32)
-        for step in range(span):
-            at = slice(step * 8, step * 8 + 8)
-            state = decay[at] * state + drive[at]
-            product = product * decay[at]
-            state_ref[place, at, :] = state
-            prod_ref[place, at, :] = product
-        product, state, enter_p, enter_s = across_spans(product, state)
-        enter_ref[place, 0] = enter_p
-        enter_ref[place, 1] = enter_s
-        row = 2 * earlier
-        end_ref[row : row + 1, lanes_of(place)] = product[7:8]
-        end_ref[row + 1 : row + 2, lanes_of(place)] = state[7:8]
-
+    masks = (mask_ref[0], mask_ref[1])
     for apart, (count, ref) in enumerate(zip(counts, weights)):
         first = lax.bitwise_xor(here, apart) * count if len(counts) > 1 else 0
-        for head in range(count):
-            one(first + head, jnp.concatenate([ref[head, 0], ref[head, 1]], axis=1))
+        for index in range(count):
+            place = first + index
+            product, state, enter_p, enter_s = gated(
+                total,
+                conv_ref[base + place],
+                jnp.concatenate([ref[index, 0], ref[index, 1]], axis=1),
+                masks,
+                bias_ref,
+                rate_ref,
+                base + place,
+                state_ref,
+                prod_ref,
+                place,
+            )
+            enter_ref[place, 0] = enter_p
+            enter_ref[place, 1] = enter_s
+            end_ref[pl.ds(row + place, 1), :] = product[7:8]
+            end_ref[pl.ds(row + heads + place, 1), :] = state[7:8]
 
 
 def shard(conv, masks, params, pair, weights, total, before=()):
@@ -316,13 +327,13 @@
     counts = tuple(part.shape[0] for part in weights)
     heads = sum(counts)
     return pallas(
-        functools.partial(shard_kernel, total, pair, counts, len(before)),
+        functools.partial(shard_kernel, total, pair, counts),
         "shard",
         [
             jax.ShapeDtypeStruct((heads, tokens, HS), jnp.float32),
             jax.ShapeDtypeStruct((heads, tokens, HS), jnp.float32),
             jax.ShapeDtypeStruct((heads, 2, 8, HS), jnp.float32),
-            jax.ShapeDtypeStruct((2 * len(before) + 2, heads * HS), jnp.float32),
+            jax.ShapeDtypeStruct((2 * heads * (1 + len(before)), HS), jnp.float32),
         ],
         in_vmem(4 + len(weights) + len(before)),
         in_vmem(4),
@@ -331,95 +342,93 @@
     )(conv, masks, *params, *weights, *before)
 
 
-def rows_kernel(pairs, *refs):
+def natural_order(tokens):
+    span = tokens // 8
+    token = lax.broadcasted_iota(jnp.int32, (tokens, tokens), 0)
+    row = lax.broadcasted_iota(jnp.int32, (tokens, tokens), 1)
+    here = row == lax.rem(token, span) * 8 + lax.div(token, span)
+    return jnp.where(here, 1.0, 0.0).astype(jnp.bfloat16)
+
+
+def final_kernel(pairs, target_ref, *refs):
     devices = lax.axis_size("seq")
     here = lax.axis_index("seq")
-    ends, refs = refs[:devices], refs[devices:]
+    ends, refs = refs[: devices - 1], refs[devices - 1 :]
     parts = [refs[3 * slot : 3 * slot + 3] for slot in range(len(pairs))]
-    student_ref, held_ref, scale_ref, ends_s, natural, sem = refs[3 * len(pairs) :]
+    student_ref, loss_ref, ends_s, held, sem = refs[3 * len(pairs) :]
     heads, tokens = parts[0][0].shape[:2]
     span = tokens // 8
     width = heads * HS
-    for apart in range(devices):
-        ends_s[lax.bitwise_xor(here, apart)] = ends[apart][...]
+    for apart in range(1, devices):
+        ends_s[lax.bitwise_xor(here, apart)] = ends[apart - 1][...]
     squares = jnp.zeros((tokens, HS), jnp.float32)
     copies = []
+    bases = []
+    order = natural_order(tokens)
     for slot, (pair, (state_ref, prod_ref, enter_ref)) in enumerate(zip(pairs, parts)):
-        incoming = jnp.zeros((1, width), jnp.float32)
+        incoming = jnp.zeros((heads, HS), jnp.float32)
+        row = 2 * heads * slot
         for place in range(devices - 1):
-            after = ends_s[place, 2 * slot : 2 * slot + 1, :] * incoming + (
-                ends_s[place, 2 * slot + 1 : 2 * slot + 2, :]
+            after = ends_s[place, row : row + heads, :] * incoming + (
+                ends_s[place, row + heads : row + 2 * heads, :]
             )
             incoming = jnp.where(place < here, after, incoming)
         base = lax.bitwise_xor(lax.axis_index("fsdp"), pair) * heads
+        bases.append(base)
         for head in range(heads):
-            entering = enter_ref[head, 1] + enter_ref[head, 0] * (
-                incoming[:, head * HS : (head + 1) * HS]
-            )
-            for step in range(span):
-                at = slice(step * 8, step * 8 + 8)
-                natural[slot * heads + head, pl.ds(step, 8, stride=span), :] = (
-                    state_ref[head, at, :] + prod_ref[head, at, :] * entering
-                )
-            rounded = natural[slot * heads + head].astype(jnp.bfloat16)
-            held_ref[0, :, lanes_of(base + head)] = rounded
-            value = rounded.astype(jnp.float32)
+            at_head = slot * heads + head
+            entering = enter_ref[head, 1] + enter_ref[head, 0] * incoming[head : head + 1]
+            rows = [
+                state_ref[head, step * 8 : step * 8 + 8, :]
+                + prod_ref[head, step * 8 : step * 8 + 8, :] * entering
+                for step in range(span)
+            ]
+            strided = jnp.concatenate(rows, axis=0).astype(jnp.bfloat16)
+            value = jnp.dot(order, strided, preferred_element_type=jnp.float32)
+            held[:, at_head * HS : (at_head + 1) * HS] = value.astype(jnp.bfloat16)
             squares = squares + value * value
         columns = pl.ds(pl.multiple_of(base * HS, width), width)
         copies.append(
             pltpu.make_async_copy(
-                held_ref.at[:, :, columns], student_ref.at[:, :, columns], sem.at[slot]
+                held.at[:, pl.ds(slot * width, width)], student_ref.at[0, :, columns], sem.at[slot]
             )
         )
         copies[-1].start()
-    mean = jnp.sum(squares, axis=1, keepdims=True) * (1.0 / student_ref.shape[2])
-    scale_ref[...] = jnp.broadcast_to(lax.rsqrt(mean + 1e-06), (tokens, HS))
+    full = student_ref.shape[2]
+    mean = jnp.sum(squares, axis=1, keepdims=True) * (1.0 / full)
+    scale = jnp.broadcast_to(lax.rsqrt(mean + 1e-06), (tokens, HS))
+    total = jnp.zeros((tokens, HS), jnp.float32)
+    for slot, base in enumerate(bases):
+        for head in range(heads):
+            at_head = slot * heads + head
+            value = held[:, at_head * HS : (at_head + 1) * HS].astype(jnp.float32)
+            off = value * scale - target_ref[0, :, lanes_of(base + head)].astype(jnp.float32)
+            total = total + off * off
+    loss_ref[...] = jnp.sum(total.T, axis=0, keepdims=True) * (1.0 / full)
     for copy in copies:
         copy.wait()
 
 
-def student_rows(pairs, ends, parts):
+def final(pairs, target, ends, parts):
     heads, tokens = parts[0][0].shape[:2]
     full = HEADS * HS
     flat = [array for part in parts for array in part[:3]]
-    whole = jax.ShapeDtypeStruct((1, tokens, full), jnp.bfloat16)
     return pallas(
-        functools.partial(rows_kernel, pairs),
-        "student_rows",
-        [whole, whole, jax.ShapeDtypeStruct((tokens, HS), jnp.float32)],
-        in_vmem(len(ends) + len(flat)),
-        [pl.BlockSpec(memory_space=pltpu.HBM)] + in_vmem(2),
-        [
-            pltpu.VMEM((len(ends),) + ends[0].shape, jnp.float32),
-            pltpu.VMEM((HEADS, tokens, HS), jnp.float32),
+        functools.partial(final_kernel, pairs),
+        "final",
+        [
+            jax.ShapeDtypeStruct((1, tokens, full), jnp.bfloat16),
+            jax.ShapeDtypeStruct((1, tokens), jnp.float32),
+        ],
+        in_vmem(1 + len(ends) + len(flat)),
+        [pl.BlockSpec(memory_space=pltpu.HBM)] + in_vmem(1),
+        [
+            pltpu.VMEM((len(ends) + 1,) + ends[0].shape, jnp.float32),
+            pltpu.VMEM((tokens, full), jnp.bfloat16),
             pltpu.SemaphoreType.DMA((len(pairs),)),
         ],
         tokens * full,
-    )(*ends, *flat)
-
-
-def loss_kernel(student_ref, scale_ref, target_ref, loss_ref):
-    tokens, width = student_ref.shape[1:]
-    scale = scale_ref[...]
-    total = jnp.zeros((tokens, HS), jnp.float32)
-    for start in range(0, width, HS):
-        lanes = slice(start, start + HS)
-        wanted = target_ref[0, :, lanes].astype(jnp.float32)
-        off = student_ref[0, :, lanes].astype(jnp.float32) * scale - wanted
-        total = total + off * off
-    loss_ref[...] = jnp.sum(total.T, axis=0, keepdims=True) * (1.0 / width)
-
-
-def token_losses(student, scale, target):
-    return pallas(
-        loss_kernel,
-        "token_losses",
-        jax.ShapeDtypeStruct((1, student.shape[1]), jnp.float32),
-        in_vmem(3),
-        pl.BlockSpec(memory_space=pltpu.VMEM),
-        [],
-        student.size,
-    )(student, scale, target)
+    )(target, *ends, *flat)
 
 
 def swap(value, axis, apart):
@@ -435,33 +444,30 @@
 ):
     tokens, width = branch_x.shape[1:]
     total = lax.axis_size("seq") * tokens
+    half, quarter, edge = cut(branch_x, gate_weights)
     target = swap(teacher_held, "segment", 1)
-    half, quarter, edge = cut(branch_x, gate_weights)
-    quarters = {2: swap(quarter, "fsdp", 2)}
-    quarters[3] = swap(quarter, "fsdp", 3)
+    quarters = {pair: swap(quarter, "fsdp", pair) for pair in (2, 3)}
     half = swap(half, "fsdp", 1)
     edge = from_behind(edge, "seq", 1)
-    edge = edge
     conv, masks = conv_rows(branch_x, edge, positions, conv_weight, conv_bias.reshape(1, width))
     params = (gate_bias, decay_rate.reshape(1, width))
-    pairs = (0, 1, 2, 3)
-    parts = {0: shard(conv, masks, params, 0, [gate_weights], total)}
-
+    parts = [shard(conv, masks, params, 0, [gate_weights], total)]
     two = swap(quarters[2], "seq", 2)
     three = swap(after(quarters[3], masks), "seq", 2)
     mine = after(quarters[2], two, parts[0][3])
     weights = [mine, swap(mine, "seq", 1), two, swap(two, "seq", 1)]
-    parts[2] = shard(conv, masks, params, 2, weights, total)
-    half = after(half,two)
-    parts[1] = shard(conv, masks, params, 1, [half, swap(half, "seq", 1)], total)
-    mine = after(quarters[3],three)
+    parts.append(shard(conv, masks, params, 2, weights, total))
+    half = after(half, two)
+    weights = [half, swap(half, "seq", 1)]
+    before = [part[3] for part in parts]
+    parts.append(shard(conv, masks, params, 1, weights, total, ()))
+    mine = after(quarters[3], three)
     weights = [mine, swap(mine, "seq", 1), three, swap(three, "seq", 1)]
-    parts[3] = shard(conv, masks, params, 3, weights, total, [parts[pair][3] for pair in pairs[:3]])
-    parts = [parts[pair] for pair in pairs]
+    before = [part[3] for part in parts]
+    parts.append(shard(conv, masks, params, 3, weights, total, before))
     end = parts[-1][3]
-    ends = [end] + [swap(end, "seq", apart) for apart in (1, 2, 3)]
-    student, held, scale = student_rows(pairs, ends, parts)
-    return student, token_losses(held, scale, target)
+    ends = [swap(end, "seq", apart) for apart in (1, 2, 3)]
+    return final((0, 2, 1, 3), target, ends, parts)
 
 
 def solution(mesh):

time: 35.7 us -> 35.1 us (0.983)
  Pallas kernels: 8.44 us -> 7.86 us
    pallas_call x6 -> x5, Pallas kernels: 5.45 us -> 4.87 us  [the longest x1 2.45 us: final(): pallas(functools.partial(final_kernel, pairs), 'final', [jax.ShapeDtypeSt...]
  transfers between devices with their start and end apart: 15 -> 15, of which waited for: 5 -> 5; matrix products, arithmetic and copies ran while one was open for 0% -> 0% of each run, Pallas kernels for 21% -> 15%
where the time goes in v3:
time: 35.1 us; the launch traced here: 35 us
  starting transfers between devices  15.8 us (45%)
  waiting for transfers between devices  10.5 us (30%)
  Pallas kernels  7.86 us (22%)
  between operations  0.79 us (2%)
    ppermute x14, starting transfers between devices, swap(): lax.ppermute(value, axis, [(i, i ^ apart) for i in range(lax.axis_size(ax...  14.4 us
    ppermute x14, waiting for transfers between devices, swap(): lax.ppermute(value, axis, [(i, i ^ apart) for i in range(lax.axis_size(ax...  10.5 us
    pallas_call x1, Pallas kernels, final(): pallas(functools.partial(final_kernel, pairs), 'final', [jax.ShapeDtypeSt...  2.45 us
    pallas_call x4, Pallas kernels, shard(): pallas(functools.partial(shard_kernel, total, pair, counts), 'shard', [ja...  2.42 us
    pallas_call x1, Pallas kernels, conv_rows(): pallas(conv_kernel, 'conv_rows', [jax.ShapeDtypeStruct((heads, tokens, HS...  1.91 us
    ppermute x1, starting transfers between devices, from_behind(): lax.ppermute(value, axis, [(source, source + steps) for source in range(l...  1.42 us
    pallas_call x1, Pallas kernels, cut(): pallas(cut_kernel, 'cut', [jax.ShapeDtypeStruct((held // 2,) + rest, jnp....  1.08 us
  transfers between devices with their start and end apart: 15, of which 5 were waited for; matrix products, arithmetic and copies ran while one was open for 0% of the time, Pallas kernels for 15%

profile of v3, /device:TPU:0, one launch (start us, length us, event | category | flops | bytes accessed | tf_op | source)
XLA Modules:
  0.0 35.0 jit_solution(3009657956549848280)
XLA Ops:
  0.6 0.0 copy-start
  0.6 0.0 copy-start.4
  0.7 3.0 %collective-permute-start = (bf16[1,128,4096]{2,1,0:T(8,128)(2,1)}, bf16[1,128,4096]{2,1,0:T(8,128)(2,1)S(1)}, u32[]{:S(2)}, u32[]{:S(2)}) collective-permute-start(bf16[1,128,4096]{2,1,0:T(8,128)(2,1)} %param.10), channel_id=1, source_target_pairs={{0,16},{16,0},{1,17},{17,1},{2,18},{18,2},{3,19},{19,3},{4,20},{20... | collective-permute-start | bytes 3145736 | tf_op jit(solution)/shard_map/ppermute | solution.py:435
  3.7 1.1 %cut.1 = (bf16[4,2,128,128]{3,2,1,0:T(8,128)(2,1)S(1)}, bf16[2,2,128,128]{3,2,1,0:T(8,128)(2,1)S(1)}, bf16[16,4096]{1,0:T(8,128)(2,1)S(1)}) custom-call(bf16[1,128,4096]{2,1,0:T(8,128)(2,1)} %x_ref.3, bf16[8,2,128,128]{3,2,1,0:T(8,128)(2,1)} %refs_0_.1), custom_call_target="tpu_custom_call" | custom-call | tf_op jit(solution)/shard_map/cut/pallas_call | solution.py:172
  4.8 2.7 %collective-permute-start.6 = (bf16[2,2,128,128]{3,2,1,0:T(8,128)(2,1)S(1)}, bf16[2,2,128,128]{3,2,1,0:T(8,128)(2,1)S(1)}, u32[]{:S(2)}, u32[]{:S(2)}) collective-permute-start(bf16[2,2,128,128]{3,2,1,0:T(8,128)(2,1)S(1)} %get-tuple-element.30), channel_id=1, source_target_pairs={{0,8},{4,12},{8,0},{12,4},{1,9},{5,13},{9,1},{13,5},{2,10},{6,14},... | collective-permute-start | bytes 393224 | tf_op jit(solution)/shard_map/ppermute | solution.py:435
  7.4 1.6 %collective-permute-start.10 = (bf16[4,2,128,128]{3,2,1,0:T(8,128)(2,1)S(1)}, bf16[4,2,128,128]{3,2,1,0:T(8,128)(2,1)S(1)}, u32[]{:S(2)}, u32[]{:S(2)}) collective-permute-start(bf16[4,2,128,128]{3,2,1,0:T(8,128)(2,1)S(1)} %get-tuple-element.36), channel_id=1, source_target_pairs={{0,4},{4,0},{8,12},{12,8},{1,5},{5,1},{9,13},{13,9},{2,6},{6,2},{1... | collective-permute-start | bytes 786440 | tf_op jit(solution)/shard_map/ppermute | solution.py:435
  9.0 1.4 %collective-permute-start.1 = (bf16[16,4096]{1,0:T(8,128)(2,1)S(1)}, bf16[16,4096]{1,0:T(8,128)(2,1)S(1)}, u32[]{:S(2)}, u32[]{:S(2)}) collective-permute-start(bf16[16,4096]{1,0:T(8,128)(2,1)S(1)} %get-tuple-element.27), channel_id=1, source_target_pairs={{0,1},{1,2},{2,3},{4,5},{5,6},{6,7},{8,9},{9,10},{10,11},{12,13},{... | collective-permute-start | bytes 393224 | tf_op jit(solution)/shard_map/ppermute | solution.py:42
  10.4 0.3 collective-permute-start.2
  10.7 2.9 %collective-permute-done.6.refs_0_ = bf16[2,2,128,128]{3,2,1,0:T(8,128)(2,1)S(1)} collective-permute-done((bf16[2,2,128,128]{3,2,1,0:T(8,128)(2,1)S(1)}, bf16[2,2,128,128]{3,2,1,0:T(8,128)(2,1)S(1)}, u32[]{:S(2)}, u32[]{:S(2)}) %collective-permute-start.6) | collective-permute-done | bytes 131104 | tf_op jit(solution)/shard_map/ppermute | solution.py:435
  13.6 2.3 %collective-permute-start.7 = (bf16[2,2,128,128]{3,2,1,0:T(8,128)(2,1)S(1)}, bf16[2,2,128,128]{3,2,1,0:T(8,128)(2,1)S(1)}, u32[]{:S(2)}, u32[]{:S(2)}) collective-permute-start(bf16[2,2,128,128]{3,2,1,0:T(8,128)(2,1)S(1)} %collective-permute-done.6.refs_0_), channel_id=1, source_target_pairs={{0,2},{1,3},{2,0},{3,1},{4,6},{5,7},{6,4},{7,5},{8,10},{9,11},{10,... | collective-permute-start | bytes 393224 | tf_op jit(solution)/shard_map/ppermute | solution.py:435
  15.9 0.0 collective-permute-done.1.edge_ref
  15.9 0.0 copy-done
  15.9 0.0 copy-done.4
  15.9 0.0 copy-done.5
  15.9 0.0 copy-done.6
  15.9 0.0 copy-start.1
  15.9 0.0 copy-start.2
  15.9 0.0 copy-start.3
  15.9 1.9 %conv_rows.1 = (bf16[32,128,128]{2,1,0:T(8,128)(2,1)S(1)}, f32[2,128,128]{2,1,0:T(8,128)S(1)}) custom-call(bf16[1,128,4096]{2,1,0:T(8,128)(2,1)S(1)} %copy-done, bf16[16,4096]{1,0:T(8,128)(2,1)S(1)} %collective-permute-done.1.edge_ref, s32[1,128]{1,0:T(1,128)S(1)} %copy-done.6, f32[4,4096]{1,0:T(4,128)S(1)} %copy-done.4, f32[1,4096]{1,0:T(1,128)S(1)} %bitcast.6), custom_call_target="tpu_custom_call" | custom-call | tf_op jit(solution)/shard_map/conv_rows/pallas_call | solution.py:240
  17.8 2.3 %collective-permute-done.2.refs_0_ = bf16[2,2,128,128]{3,2,1,0:T(8,128)(2,1)S(1)} collective-permute-done((bf16[2,2,128,128]{3,2,1,0:T(8,128)(2,1)S(1)}, bf16[2,2,128,128]{3,2,1,0:T(8,128)(2,1)S(1)}, u32[]{:S(2)}, u32[]{:S(2)}) %collective-permute-start.2) | collective-permute-done | bytes 131104 | tf_op jit(solution)/shard_map/ppermute | solution.py:435
  20.2 1.5 %collective-permute-start.3 = (bf16[2,2,128,128]{3,2,1,0:T(8,128)(2,1)S(1)}, bf16[2,2,128,128]{3,2,1,0:T(8,128)(2,1)S(1)}, u32[]{:S(2)}, u32[]{:S(2)}) collective-permute-start(bf16[2,2,128,128]{3,2,1,0:T(8,128)(2,1)S(1)} %collective-permute-done.2.refs_0_), channel_id=1, source_target_pairs={{0,2},{1,3},{2,0},{3,1},{4,6},{5,7},{6,4},{7,5},{8,10},{9,11},{10,... | collective-permute-start | bytes 393224 | tf_op jit(solution)/shard_map/ppermute | solution.py:435
  21.7 0.0 copy-done.1
  21.7 0.0 copy-done.2
  21.7 0.6 %shard.4 = (f32[8,128,128]{2,1,0:T(8,128)S(1)}, f32[8,128,128]{2,1,0:T(8,128)S(1)}, f32[8,2,8,128]{3,2,1,0:T(8,128)S(1)}, f32[16,128]{1,0:T(8,128)S(1)}) custom-call(bf16[32,128,128]{2,1,0:T(8,128)(2,1)S(1)} %get-tuple-element.28.conv_ref, f32[2,128,128]{2,1,0:T(8,128)S(1)} %get-tuple-element.29.mask_ref, f32[2,4096]{1,0:T(2,128)S(1)} %copy-done.2, ...), custom_call_target="tpu_custom_call" | custom-call | tf_op jit(solution)/shard_map/shard/pallas_call | solution.py:329
  22.3 0.0 collective-permute-done.7.refs_2_
  22.3 0.0 collective-permute-done.10.refs_0_
  22.3 0.1 collective-permute-start.11
  22.4 0.5 %collective-permute-start.8 = (bf16[2,2,128,128]{3,2,1,0:T(8,128)(2,1)S(1)}, bf16[2,2,128,128]{3,2,1,0:T(8,128)(2,1)S(1)}, u32[]{:S(2)}, u32[]{:S(2)}) collective-permute-start(bf16[2,2,128,128]{3,2,1,0:T(8,128)(2,1)S(1)} %collective-permute-done.6.refs_0_), channel_id=1, source_target_pairs={{0,1},{1,0},{2,3},{3,2},{4,5},{5,4},{6,7},{7,6},{8,9},{9,8},{10,11... | collective-permute-start | bytes 393224 | tf_op jit(solution)/shard_map/ppermute | solution.py:435
  22.9 0.1 collective-permute-start.9
  23.0 2.5 %collective-permute-done.3.refs_2_ = bf16[2,2,128,128]{3,2,1,0:T(8,128)(2,1)S(1)} collective-permute-done((bf16[2,2,128,128]{3,2,1,0:T(8,128)(2,1)S(1)}, bf16[2,2,128,128]{3,2,1,0:T(8,128)(2,1)S(1)}, u32[]{:S(2)}, u32[]{:S(2)}) %collective-permute-start.3) | collective-permute-done | bytes 131104 | tf_op jit(solution)/shard_map/ppermute | solution.py:435
  25.5 0.0 collective-permute-start.4
  25.5 0.0 collective-permute-done.8.refs_1_
  25.5 0.5 %collective-permute-start.5 = (bf16[2,2,128,128]{3,2,1,0:T(8,128)(2,1)S(1)}, bf16[2,2,128,128]{3,2,1,0:T(8,128)(2,1)S(1)}, u32[]{:S(2)}, u32[]{:S(2)}) collective-permute-start(bf16[2,2,128,128]{3,2,1,0:T(8,128)(2,1)S(1)} %collective-permute-done.3.refs_2_), channel_id=1, source_target_pairs={{0,1},{1,0},{2,3},{3,2},{4,5},{5,4},{6,7},{7,6},{8,9},{9,8},{10,11... | collective-permute-start | bytes 393224 | tf_op jit(solution)/shard_map/ppermute | solution.py:435
  26.0 0.0 collective-permute-done.9.refs_3_
  26.0 0.6 %shard.5 = (f32[8,128,128]{2,1,0:T(8,128)S(1)}, f32[8,128,128]{2,1,0:T(8,128)S(1)}, f32[8,2,8,128]{3,2,1,0:T(8,128)S(1)}, f32[16,128]{1,0:T(8,128)S(1)}) custom-call(bf16[32,128,128]{2,1,0:T(8,128)(2,1)S(1)} %get-tuple-element.28.conv_ref, f32[2,128,128]{2,1,0:T(8,128)S(1)} %get-tuple-element.29.mask_ref, f32[2,4096]{1,0:T(2,128)S(1)} %copy-done.2, ...), custom_call_target="tpu_custom_call" | custom-call | tf_op jit(solution)/shard_map/shard/pallas_call | solution.py:329
  26.6 0.0 collective-permute-done.11.refs_1_
  26.6 0.6 %shard.6 = (f32[8,128,128]{2,1,0:T(8,128)S(1)}, f32[8,128,128]{2,1,0:T(8,128)S(1)}, f32[8,2,8,128]{3,2,1,0:T(8,128)S(1)}, f32[16,128]{1,0:T(8,128)S(1)}) custom-call(bf16[32,128,128]{2,1,0:T(8,128)(2,1)S(1)} %get-tuple-element.28.conv_ref, f32[2,128,128]{2,1,0:T(8,128)S(1)} %get-tuple-element.29.mask_ref, f32[2,4096]{1,0:T(2,128)S(1)} %copy-done.2, ...), custom_call_target="tpu_custom_call" | custom-call | tf_op jit(solution)/shard_map/shard/pallas_call | solution.py:329
  27.2 0.0 collective-permute-done.4.refs_1_
  27.2 0.0 collective-permute-done.5.refs_3_
  27.3 0.6 %shard.7 = (f32[8,128,128]{2,1,0:T(8,128)S(1)}, f32[8,128,128]{2,1,0:T(8,128)S(1)}, f32[8,2,8,128]{3,2,1,0:T(8,128)S(1)}, f32[64,128]{1,0:T(8,128)S(1)}) custom-call(bf16[32,128,128]{2,1,0:T(8,128)(2,1)S(1)} %get-tuple-element.28.conv_ref, f32[2,128,128]{2,1,0:T(8,128)S(1)} %get-tuple-element.29.mask_ref, f32[2,4096]{1,0:T(2,128)S(1)} %copy-done.2, ...), custom_call_target="tpu_custom_call" | custom-call | tf_op jit(solution)/shard_map/shard/pallas_call | solution.py:329
  27.9 0.2 collective-permute-start.12
  28.0 1.1 %collective-permute-start.13 = (f32[64,128]{1,0:T(8,128)S(1)}, f32[64,128]{1,0:T(8,128)S(1)}, u32[]{:S(2)}, u32[]{:S(2)}) collective-permute-start(f32[64,128]{1,0:T(8,128)S(1)} %get-tuple-element.39), channel_id=1, source_target_pairs={{0,2},{1,3},{2,0},{3,1},{4,6},{5,7},{6,4},{7,5},{8,10},{9,11},{10,... | collective-permute-start | bytes 98312 | tf_op jit(solution)/shard_map/ppermute | solution.py:435
  29.2 0.6 %collective-permute-start.14 = (f32[64,128]{1,0:T(8,128)S(1)}, f32[64,128]{1,0:T(8,128)S(1)}, u32[]{:S(2)}, u32[]{:S(2)}) collective-permute-start(f32[64,128]{1,0:T(8,128)S(1)} %get-tuple-element.39), channel_id=1, source_target_pairs={{0,3},{1,2},{2,1},{3,0},{4,7},{5,6},{6,5},{7,4},{8,11},{9,10},{10,... | collective-permute-start | bytes 98312 | tf_op jit(solution)/shard_map/ppermute | solution.py:435
  29.8 0.0 collective-permute-done.12.refs_0_
  29.8 2.1 %collective-permute-done.13.refs_1_ = f32[64,128]{1,0:T(8,128)S(1)} collective-permute-done((f32[64,128]{1,0:T(8,128)S(1)}, f32[64,128]{1,0:T(8,128)S(1)}, u32[]{:S(2)}, u32[]{:S(2)}) %collective-permute-start.13) | collective-permute-done | bytes 32800 | tf_op jit(solution)/shard_map/ppermute | solution.py:435
  31.9 0.6 %collective-permute-done.14.refs_2_ = f32[64,128]{1,0:T(8,128)S(1)} collective-permute-done((f32[64,128]{1,0:T(8,128)S(1)}, f32[64,128]{1,0:T(8,128)S(1)}, u32[]{:S(2)}, u32[]{:S(2)}) %collective-permute-start.14) | collective-permute-done | bytes 32800 | tf_op jit(solution)/shard_map/ppermute | solution.py:435
  32.5 0.0 collective-permute-done.target_ref
  32.5 2.4 %final.1 = (bf16[1,128,4096]{2,1,0:T(8,128)(2,1)}, f32[1,128]{1,0:T(1,128)}) custom-call(bf16[1,128,4096]{2,1,0:T(8,128)(2,1)S(1)} %collective-permute-done.target_ref, f32[64,128]{1,0:T(8,128)S(1)} %collective-permute-done.12.refs_0_, f32[64,128]{1,0:T(8,128)S(1)} %collective-permute-done.13.refs_1_, f32[64,128]{1,0:T(8,128)S(1)} %collective-permute-done.14.refs_2_, ...), custom_call_target="tpu_custom_call" | custom-call | tf_op jit(solution)/shard_map/final/pallas_call | solution.py:416
  (3 shorter events, 0.0 us)
Async XLA Ops:
  0.6 15.2 %copy-start = (bf16[1,128,4096]{2,1,0:T(8,128)(2,1)S(1)}, bf16[1,128,4096]{2,1,0:T(8,128)(2,1)}, u32[]{:S(2)}) copy-start(bf16[1,128,4096]{2,1,0:T(8,128)(2,1)} %x_ref.3) | copy-start | bytes 3145732
  0.6 15.2 %copy-start.4 = (f32[4,4096]{1,0:T(4,128)S(1)}, f32[4,4096]{1,0:T(4,128)}, u32[]{:S(2)}) copy-start(f32[4,4096]{1,0:T(4,128)} %w_ref.3) | copy-start | bytes 196612
  0.7 31.9 %collective-permute-start = (bf16[1,128,4096]{2,1,0:T(8,128)(2,1)}, bf16[1,128,4096]{2,1,0:T(8,128)(2,1)S(1)}, u32[]{:S(2)}, u32[]{:S(2)}) collective-permute-start(bf16[1,128,4096]{2,1,0:T(8,128)(2,1)} %param.10), channel_id=1, source_target_pairs={{0,16},{16,0},{1,17},{17,1},{2,18},{18,2},{3,19},{19,3},{4,20},{20... | collective-permute-start | bytes 3145736 | tf_op jit(solution)/shard_map/ppermute | solution.py:435
  3.7 12.2 %copy-start.5 = (f32[4096]{0:T(1024)S(1)}, f32[4096]{0:T(1024)}, u32[]{:S(2)}) copy-start(f32[4096]{0:T(1024)} %param.14) | copy-start | bytes 49156
  4.8 8.8 %collective-permute-start.6 = (bf16[2,2,128,128]{3,2,1,0:T(8,128)(2,1)S(1)}, bf16[2,2,128,128]{3,2,1,0:T(8,128)(2,1)S(1)}, u32[]{:S(2)}, u32[]{:S(2)}) collective-permute-start(bf16[2,2,128,128]{3,2,1,0:T(8,128)(2,1)S(1)} %get-tuple-element.30), channel_id=1, source_target_pairs={{0,8},{4,12},{8,0},{12,4},{1,9},{5,13},{9,1},{13,5},{2,10},{6,14},... | collective-permute-start | bytes 393224 | tf_op jit(solution)/shard_map/ppermute | solution.py:435
  7.4 14.9 %collective-permute-start.10 = (bf16[4,2,128,128]{3,2,1,0:T(8,128)(2,1)S(1)}, bf16[4,2,128,128]{3,2,1,0:T(8,128)(2,1)S(1)}, u32[]{:S(2)}, u32[]{:S(2)}) collective-permute-start(bf16[4,2,128,128]{3,2,1,0:T(8,128)(2,1)S(1)} %get-tuple-element.36), channel_id=1, source_target_pairs={{0,4},{4,0},{8,12},{12,8},{1,5},{5,1},{9,13},{13,9},{2,6},{6,2},{1... | collective-permute-start | bytes 786440 | tf_op jit(solution)/shard_map/ppermute | solution.py:435
  9.0 6.9 %copy-start.6 = (s32[1,128]{1,0:T(1,128)S(1)}, s32[1,128]{1,0:T(1,128)}, u32[]{:S(2)}) copy-start(s32[1,128]{1,0:T(1,128)} %pos_ref.1) | copy-start | bytes 1540
  9.0 6.9 %collective-permute-start.1 = (bf16[16,4096]{1,0:T(8,128)(2,1)S(1)}, bf16[16,4096]{1,0:T(8,128)(2,1)S(1)}, u32[]{:S(2)}, u32[]{:S(2)}) collective-permute-start(bf16[16,4096]{1,0:T(8,128)(2,1)S(1)} %get-tuple-element.27), channel_id=1, source_target_pairs={{0,1},{1,2},{2,3},{4,5},{5,6},{6,7},{8,9},{9,10},{10,11},{12,13},{... | collective-permute-start | bytes 393224 | tf_op jit(solution)/shard_map/ppermute | solution.py:42
  10.4 9.7 %collective-permute-start.2 = (bf16[2,2,128,128]{3,2,1,0:T(8,128)(2,1)S(1)}, bf16[2,2,128,128]{3,2,1,0:T(8,128)(2,1)S(1)}, u32[]{:S(2)}, u32[]{:S(2)}) collective-permute-start(bf16[2,2,128,128]{3,2,1,0:T(8,128)(2,1)S(1)} %get-tuple-element.30), channel_id=1, source_target_pairs={{0,12},{4,8},{8,4},{12,0},{1,13},{5,9},{9,5},{13,1},{2,14},{6,10},... | collective-permute-start | bytes 393224 | tf_op jit(solution)/shard_map/ppermute | solution.py:435
  13.6 8.7 %collective-permute-start.7 = (bf16[2,2,128,128]{3,2,1,0:T(8,128)(2,1)S(1)}, bf16[2,2,128,128]{3,2,1,0:T(8,128)(2,1)S(1)}, u32[]{:S(2)}, u32[]{:S(2)}) collective-permute-start(bf16[2,2,128,128]{3,2,1,0:T(8,128)(2,1)S(1)} %collective-permute-done.6.refs_0_), channel_id=1, source_target_pairs={{0,2},{1,3},{2,0},{3,1},{4,6},{5,7},{6,4},{7,5},{8,10},{9,11},{10,... | collective-permute-start | bytes 393224 | tf_op jit(solution)/shard_map/ppermute | solution.py:435
  15.9 5.8 %copy-start.1 = (bf16[8,2,128,128]{3,2,1,0:T(8,128)(2,1)S(1)}, bf16[8,2,128,128]{3,2,1,0:T(8,128)(2,1)}, u32[]{:S(2)}) copy-start(bf16[8,2,128,128]{3,2,1,0:T(8,128)(2,1)} %refs_0_.1) | copy-start | bytes 1572868
  15.9 5.8 %copy-start.2 = (f32[2,4096]{1,0:T(2,128)S(1)}, f32[2,4096]{1,0:T(2,128)}, u32[]{:S(2)}) copy-start(f32[2,4096]{1,0:T(2,128)} %bias_ref.7) | copy-start | bytes 98308
  15.9 5.8 %copy-start.3 = (f32[4096]{0:T(1024)S(1)}, f32[4096]{0:T(1024)}, u32[]{:S(2)}) copy-start(f32[4096]{0:T(1024)} %param.15) | copy-start | bytes 49156
  20.2 5.3 %collective-permute-start.3 = (bf16[2,2,128,128]{3,2,1,0:T(8,128)(2,1)S(1)}, bf16[2,2,128,128]{3,2,1,0:T(8,128)(2,1)S(1)}, u32[]{:S(2)}, u32[]{:S(2)}) collective-permute-start(bf16[2,2,128,128]{3,2,1,0:T(8,128)(2,1)S(1)} %collective-permute-done.2.refs_0_), channel_id=1, source_target_pairs={{0,2},{1,3},{2,0},{3,1},{4,6},{5,7},{6,4},{7,5},{8,10},{9,11},{10,... | collective-permute-start | bytes 393224 | tf_op jit(solution)/shard_map/ppermute | solution.py:435
  22.3 4.3 %collective-permute-start.11 = (bf16[4,2,128,128]{3,2,1,0:T(8,128)(2,1)S(1)}, bf16[4,2,128,128]{3,2,1,0:T(8,128)(2,1)S(1)}, u32[]{:S(2)}, u32[]{:S(2)}) collective-permute-start(bf16[4,2,128,128]{3,2,1,0:T(8,128)(2,1)S(1)} %collective-permute-done.10.refs_0_), channel_id=1, source_target_pairs={{0,1},{1,0},{2,3},{3,2},{4,5},{5,4},{6,7},{7,6},{8,9},{9,8},{10,11... | collective-permute-start | bytes 786440 | tf_op jit(solution)/shard_map/ppermute | solution.py:435
  22.4 3.1 %collective-permute-start.8 = (bf16[2,2,128,128]{3,2,1,0:T(8,128)(2,1)S(1)}, bf16[2,2,128,128]{3,2,1,0:T(8,128)(2,1)S(1)}, u32[]{:S(2)}, u32[]{:S(2)}) collective-permute-start(bf16[2,2,128,128]{3,2,1,0:T(8,128)(2,1)S(1)} %collective-permute-done.6.refs_0_), channel_id=1, source_target_pairs={{0,1},{1,0},{2,3},{3,2},{4,5},{5,4},{6,7},{7,6},{8,9},{9,8},{10,11... | collective-permute-start | bytes 393224 | tf_op jit(solution)/shard_map/ppermute | solution.py:435
  22.9 3.1 %collective-permute-start.9 = (bf16[2,2,128,128]{3,2,1,0:T(8,128)(2,1)S(1)}, bf16[2,2,128,128]{3,2,1,0:T(8,128)(2,1)S(1)}, u32[]{:S(2)}, u32[]{:S(2)}) collective-permute-start(bf16[2,2,128,128]{3,2,1,0:T(8,128)(2,1)S(1)} %collective-permute-done.7.refs_2_), channel_id=1, source_target_pairs={{0,1},{1,0},{2,3},{3,2},{4,5},{5,4},{6,7},{7,6},{8,9},{9,8},{10,11... | collective-permute-start | bytes 393224 | tf_op jit(solution)/shard_map/ppermute | solution.py:435
  25.5 1.7 %collective-permute-start.4 = (bf16[2,2,128,128]{3,2,1,0:T(8,128)(2,1)S(1)}, bf16[2,2,128,128]{3,2,1,0:T(8,128)(2,1)S(1)}, u32[]{:S(2)}, u32[]{:S(2)}) collective-permute-start(bf16[2,2,128,128]{3,2,1,0:T(8,128)(2,1)S(1)} %collective-permute-done.2.refs_0_), channel_id=1, source_target_pairs={{0,1},{1,0},{2,3},{3,2},{4,5},{5,4},{6,7},{7,6},{8,9},{9,8},{10,11... | collective-permute-start | bytes 393224 | tf_op jit(solution)/shard_map/ppermute | solution.py:435
  25.5 1.8 %collective-permute-start.5 = (bf16[2,2,128,128]{3,2,1,0:T(8,128)(2,1)S(1)}, bf16[2,2,128,128]{3,2,1,0:T(8,128)(2,1)S(1)}, u32[]{:S(2)}, u32[]{:S(2)}) collective-permute-start(bf16[2,2,128,128]{3,2,1,0:T(8,128)(2,1)S(1)} %collective-permute-done.3.refs_2_), channel_id=1, source_target_pairs={{0,1},{1,0},{2,3},{3,2},{4,5},{5,4},{6,7},{7,6},{8,9},{9,8},{10,11... | collective-permute-start | bytes 393224 | tf_op jit(solution)/shard_map/ppermute | solution.py:435
  27.9 1.9 %collective-permute-start.12 = (f32[64,128]{1,0:T(8,128)S(1)}, f32[64,128]{1,0:T(8,128)S(1)}, u32[]{:S(2)}, u32[]{:S(2)}) collective-permute-start(f32[64,128]{1,0:T(8,128)S(1)} %get-tuple-element.39), channel_id=1, source_target_pairs={{0,1},{1,0},{2,3},{3,2},{4,5},{5,4},{6,7},{7,6},{8,9},{9,8},{10,11... | collective-permute-start | bytes 98312 | tf_op jit(solution)/shard_map/ppermute | solution.py:435
  28.0 3.9 %collective-permute-start.13 = (f32[64,128]{1,0:T(8,128)S(1)}, f32[64,128]{1,0:T(8,128)S(1)}, u32[]{:S(2)}, u32[]{:S(2)}) collective-permute-start(f32[64,128]{1,0:T(8,128)S(1)} %get-tuple-element.39), channel_id=1, source_target_pairs={{0,2},{1,3},{2,0},{3,1},{4,6},{5,7},{6,4},{7,5},{8,10},{9,11},{10,... | collective-permute-start | bytes 98312 | tf_op jit(solution)/shard_map/ppermute | solution.py:435
  29.2 3.4 %collective-permute-start.14 = (f32[64,128]{1,0:T(8,128)S(1)}, f32[64,128]{1,0:T(8,128)S(1)}, u32[]{:S(2)}, u32[]{:S(2)}) collective-permute-start(f32[64,128]{1,0:T(8,128)S(1)} %get-tuple-element.39), channel_id=1, source_target_pairs={{0,3},{1,2},{2,1},{3,0},{4,7},{5,6},{6,5},{7,4},{8,11},{9,10},{10,... | collective-permute-start | bytes 98312 | tf_op jit(solution)/shard_map/ppermute | solution.py:435

commit v4 on v3

--- a/solution.py
+++ b/solution.py
@@ -133,7 +133,7 @@
     return [pl.BlockSpec(memory_space=pltpu.VMEM)] * count
 
 
-def pallas(kernel, name, out_shape, in_specs, out_specs, scratch_shapes, work, **more):
+def pallas(kernel, name, out_shape, in_specs, out_specs, scratch_shapes, weight=0, **more):
     return pl.pallas_call(
         kernel,
         out_shape=out_shape,
@@ -142,7 +142,7 @@
         scratch_shapes=scratch_shapes,
         compiler_params=pltpu.CompilerParams(vmem_limit_bytes=24 << 20),
         cost_estimate=pl.CostEstimate(
-            flops=0, bytes_accessed=0, transcendentals=0
+            flops=weight, bytes_accessed=0, transcendentals=0
         ),
         name=name,
         **more,
@@ -180,7 +180,6 @@
         [pl.BlockSpec(memory_space=pltpu.HBM)] * 2,
         [pl.BlockSpec(memory_space=pl.ANY)] * 3,
         [pltpu.SemaphoreType.DMA((3,))],
-        10000,
     )(
         pltpu.with_memory_space_constraint(branch_x, pltpu.HBM),
         pltpu.with_memory_space_constraint(gate_weights, pltpu.HBM),
@@ -251,7 +250,6 @@
             pltpu.VMEM((tokens, HS), jnp.float32),
             pltpu.VMEM((2, tokens, HS), jnp.float32),
         ],
-        tokens * width,
     )(branch_x, edge, positions, weight, bias)
 
 
@@ -338,34 +336,53 @@
         in_vmem(4 + len(weights) + len(before)),
         in_vmem(4),
         [],
-        heads * tokens * HS,
+        5500000000 if before else 0,
     )(conv, masks, *params, *weights, *before)
 
 
-def natural_order(tokens):
+def lay_kernel(*refs):
+    state_out, prod_out = refs[-2:]
+    parts = [refs[at : at + 3] for at in range(0, len(refs) - 2, 3)]
+    heads, tokens = parts[0][0].shape[:2]
     span = tokens // 8
-    token = lax.broadcasted_iota(jnp.int32, (tokens, tokens), 0)
-    row = lax.broadcasted_iota(jnp.int32, (tokens, tokens), 1)
-    here = row == lax.rem(token, span) * 8 + lax.div(token, span)
-    return jnp.where(here, 1.0, 0.0).astype(jnp.bfloat16)
-
-
-def final_kernel(pairs, target_ref, *refs):
+    for slot, (state_ref, prod_ref, enter_ref) in enumerate(parts):
+        for head in range(heads):
+            enter_p, enter_s = enter_ref[head, 0], enter_ref[head, 1]
+            for step in range(span):
+                at = slice(step * 8, step * 8 + 8)
+                product = prod_ref[head, at, :]
+                natural = pl.ds(step, 8, stride=span)
+                state_out[slot * heads + head, natural, :] = state_ref[head, at, :] + product * enter_s
+                prod_out[slot * heads + head, natural, :] = product * enter_p
+
+
+def lay_out(parts):
+    heads, tokens = parts[0][0].shape[:2]
+    flat = [array for part in parts for array in part[:3]]
+    whole = jax.ShapeDtypeStruct((len(parts) * heads, tokens, HS), jnp.float32)
+    return pallas(
+        lay_kernel,
+        "lay_out",
+        [whole, whole],
+        in_vmem(len(flat)),
+        in_vmem(2),
+        [],
+    )(*flat)
+
+
+def final_kernel(pairs, target_ref, state_ref, prod_ref, *refs):
     devices = lax.axis_size("seq")
     here = lax.axis_index("seq")
-    ends, refs = refs[: devices - 1], refs[devices - 1 :]
-    parts = [refs[3 * slot : 3 * slot + 3] for slot in range(len(pairs))]
-    student_ref, loss_ref, ends_s, held, sem = refs[3 * len(pairs) :]
-    heads, tokens = parts[0][0].shape[:2]
-    span = tokens // 8
+    ends, (student_ref, loss_ref, ends_s, held, sem) = refs[: devices - 1], refs[devices - 1 :]
+    tokens = state_ref.shape[1]
+    heads = state_ref.shape[0] // len(pairs)
     width = heads * HS
     for apart in range(1, devices):
         ends_s[lax.bitwise_xor(here, apart)] = ends[apart - 1][...]
     squares = jnp.zeros((tokens, HS), jnp.float32)
     copies = []
     bases = []
-    order = natural_order(tokens)
-    for slot, (pair, (state_ref, prod_ref, enter_ref)) in enumerate(zip(pairs, parts)):
+    for slot, pair in enumerate(pairs):
         incoming = jnp.zeros((heads, HS), jnp.float32)
         row = 2 * heads * slot
         for place in range(devices - 1):
@@ -377,23 +394,12 @@
         bases.append(base)
         for head in range(heads):
             at_head = slot * heads + head
-            entering = enter_ref[head, 1] + enter_ref[head, 0] * incoming[head : head + 1]
-            rows = [
-                state_ref[head, step * 8 : step * 8 + 8, :]
-                + prod_ref[head, step * 8 : step * 8 + 8, :] * entering
-                for step in range(span)
-            ]
-            strided = jnp.concatenate(rows, axis=0).astype(jnp.bfloat16)
-            value = jnp.dot(order, strided, preferred_element_type=jnp.float32)
-            held[:, at_head * HS : (at_head + 1) * HS] = value.astype(jnp.bfloat16)
+            rounded = (
+                state_ref[at_head] + prod_ref[at_head] * incoming[head : head + 1]
+            ).astype(jnp.bfloat16)
+            student_ref[0, :, lanes_of(base + head)] = rounded
+            value = rounded.astype(jnp.float32)
             squares = squares + value * value
-        columns = pl.ds(pl.multiple_of(base * HS, width), width)
-        copies.append(
-            pltpu.make_async_copy(
-                held.at[:, pl.ds(slot * width, width)], student_ref.at[0, :, columns], sem.at[slot]
-            )
-        )
-        copies[-1].start()
     full = student_ref.shape[2]
     mean = jnp.sum(squares, axis=1, keepdims=True) * (1.0 / full)
     scale = jnp.broadcast_to(lax.rsqrt(mean + 1e-06), (tokens, HS))
@@ -401,7 +407,7 @@
     for slot, base in enumerate(bases):
         for head in range(heads):
             at_head = slot * heads + head
-            value = held[:, at_head * HS : (at_head + 1) * HS].astype(jnp.float32)
+            value = student_ref[0, :, lanes_of(base + head)].astype(jnp.float32)
             off = value * scale - target_ref[0, :, lanes_of(base + head)].astype(jnp.float32)
             total = total + off * off
     loss_ref[...] = jnp.sum(total.T, axis=0, keepdims=True) * (1.0 / full)
@@ -409,10 +415,9 @@
         copy.wait()
 
 
-def final(pairs, target, ends, parts):
-    heads, tokens = parts[0][0].shape[:2]
+def final(pairs, target, states, products, ends):
+    tokens = states.shape[1]
     full = HEADS * HS
-    flat = [array for part in parts for array in part[:3]]
     return pallas(
         functools.partial(final_kernel, pairs),
         "final",
@@ -420,15 +425,14 @@
             jax.ShapeDtypeStruct((1, tokens, full), jnp.bfloat16),
             jax.ShapeDtypeStruct((1, tokens), jnp.float32),
         ],
-        in_vmem(1 + len(ends) + len(flat)),
-        [pl.BlockSpec(memory_space=pltpu.HBM)] + in_vmem(1),
+        in_vmem(3 + len(ends)),
+        in_vmem(2),
         [
             pltpu.VMEM((len(ends) + 1,) + ends[0].shape, jnp.float32),
             pltpu.VMEM((tokens, full), jnp.bfloat16),
             pltpu.SemaphoreType.DMA((len(pairs),)),
         ],
-        tokens * full,
-    )(target, *ends, *flat)
+    )(target, states, products, *ends)
 
 
 def swap(value, axis, apart):
@@ -444,8 +448,8 @@
 ):
     tokens, width = branch_x.shape[1:]
     total = lax.axis_size("seq") * tokens
+    target = swap(teacher_held, "segment", 1)
     half, quarter, edge = cut(branch_x, gate_weights)
-    target = swap(teacher_held, "segment", 1)
     quarters = {pair: swap(quarter, "fsdp", pair) for pair in (2, 3)}
     half = swap(half, "fsdp", 1)
     edge = from_behind(edge, "seq", 1)
@@ -467,7 +471,8 @@
     parts.append(shard(conv, masks, params, 3, weights, total, before))
     end = parts[-1][3]
     ends = [swap(end, "seq", apart) for apart in (1, 2, 3)]
-    return final((0, 2, 1, 3), target, ends, parts)
+    states, products = lay_out(parts)
+    return final((0, 2, 1, 3), target, states, products, ends)
 
 
 def solution(mesh):

time: 35.1 us -> 34.5 us (0.983)
  waiting for transfers between devices: 10.5 us -> 6.01 us
  local copies, waits for them, and re-layouts: 0.03 us -> 2.23 us
  Pallas kernels: 7.86 us -> 8.78 us
  starting transfers between devices: 15.8 us -> 16.4 us
    ppermute x14, waiting for transfers between devices: 10.5 us -> 6.01 us  [swap(): lax.ppermute(value, axis, [(i, i ^ apart) for i in range(lax.axis_size(ax...]
    unnamed x14, local copies, waits for them, and re-layouts: 0.03 us -> 2.23 us
    pallas_call x0 -> x1, Pallas kernels: none -> 1.18 us  [lay_out(): pallas(lay_kernel, 'lay_out', [whole, whole], in_vmem(len(flat)), in_vmem...]
    ppermute x14, starting transfers between devices: 14.4 us -> 15.1 us  [swap(): lax.ppermute(value, axis, [(i, i ^ apart) for i in range(lax.axis_size(ax...]
    pallas_call x1, Pallas kernels: 2.45 us -> 2.09 us  [final(): pallas(functools.partial(final_kernel, pairs), 'final', [jax.ShapeDtypeSt...]
  transfers between devices with their start and end apart: 15 -> 15, of which waited for: 5 -> 5; matrix products, arithmetic and copies ran while one was open for 0% -> 0% of each run, Pallas kernels for 15% -> 16%
where the time goes in v4:
time: 34.5 us; the launch traced here: 34.2 us
  starting transfers between devices  16.4 us (48%)
  Pallas kernels  8.78 us (25%)
  waiting for transfers between devices  6.01 us (17%)
  local copies, waits for them, and re-layouts  2.23 us (6%)
  between operations  0.79 us (2%)
    ppermute x14, starting transfers between devices, swap(): lax.ppermute(value, axis, [(i, i ^ apart) for i in range(lax.axis_size(ax...  15.1 us
    ppermute x14, waiting for transfers between devices, swap(): lax.ppermute(value, axis, [(i, i ^ apart) for i in range(lax.axis_size(ax...  6.01 us
    pallas_call x4, Pallas kernels, shard(): pallas(functools.partial(shard_kernel, total, pair, counts), 'shard', [ja...  2.41 us
    unnamed x14, local copies, waits for them, and re-layouts  2.23 us
    pallas_call x1, Pallas kernels, final(): pallas(functools.partial(final_kernel, pairs), 'final', [jax.ShapeDtypeSt...  2.09 us
    pallas_call x1, Pallas kernels, conv_rows(): pallas(conv_kernel, 'conv_rows', [jax.ShapeDtypeStruct((heads, tokens, HS...  1.91 us
    ppermute x1, starting transfers between devices, from_behind(): lax.ppermute(value, axis, [(source, source + steps) for source in range(l...  1.29 us
    pallas_call x1, Pallas kernels, cut(): pallas(cut_kernel, 'cut', [jax.ShapeDtypeStruct((held // 2,) + rest, jnp....  1.19 us
  transfers between devices with their start and end apart: 15, of which 5 were waited for; matrix products, arithmetic and copies ran while one was open for 0% of the time, Pallas kernels for 16%

profile of v4, /device:TPU:0, one launch (start us, length us, event | category | flops | bytes accessed | tf_op | source)
XLA Modules:
  0.0 34.2 jit_solution(4002043119559987241)
XLA Ops:
  0.6 0.0 copy-start.1
  0.6 0.0 copy-start
  0.7 0.0 copy-start.3
  0.7 0.0 copy-start.2
  0.7 1.2 %cut.1 = (bf16[4,2,128,128]{3,2,1,0:T(8,128)(2,1)S(1)}, bf16[2,2,128,128]{3,2,1,0:T(8,128)(2,1)S(1)}, bf16[16,4096]{1,0:T(8,128)(2,1)S(1)}) custom-call(bf16[1,128,4096]{2,1,0:T(8,128)(2,1)} %x_ref.3, bf16[8,2,128,128]{3,2,1,0:T(8,128)(2,1)} %refs_0_.1), custom_call_target="tpu_custom_call" | custom-call | tf_op jit(solution)/shard_map/cut/pallas_call | solution.py:172
  1.9 4.1 %collective-permute-start.2 = (bf16[2,2,128,128]{3,2,1,0:T(8,128)(2,1)S(1)}, bf16[2,2,128,128]{3,2,1,0:T(8,128)(2,1)S(1)}, u32[]{:S(2)}, u32[]{:S(2)}) collective-permute-start(bf16[2,2,128,128]{3,2,1,0:T(8,128)(2,1)S(1)} %get-tuple-element.35), channel_id=1, source_target_pairs={{0,8},{4,12},{8,0},{12,4},{1,9},{5,13},{9,1},{13,5},{2,10},{6,14},... | collective-permute-start | bytes 393224 | tf_op jit(solution)/shard_map/ppermute | solution.py:439
  6.0 1.6 %collective-permute-start.6 = (bf16[4,2,128,128]{3,2,1,0:T(8,128)(2,1)S(1)}, bf16[4,2,128,128]{3,2,1,0:T(8,128)(2,1)S(1)}, u32[]{:S(2)}, u32[]{:S(2)}) collective-permute-start(bf16[4,2,128,128]{3,2,1,0:T(8,128)(2,1)S(1)} %get-tuple-element.41), channel_id=1, source_target_pairs={{0,4},{4,0},{8,12},{12,8},{1,5},{5,1},{9,13},{13,9},{2,6},{6,2},{1... | collective-permute-start | bytes 786440 | tf_op jit(solution)/shard_map/ppermute | solution.py:439
  7.5 1.5 %collective-permute-start = (bf16[1,128,4096]{2,1,0:T(8,128)(2,1)}, bf16[1,128,4096]{2,1,0:T(8,128)(2,1)S(1)}, u32[]{:S(2)}, u32[]{:S(2)}) collective-permute-start(bf16[1,128,4096]{2,1,0:T(8,128)(2,1)} %param.10), channel_id=1, source_target_pairs={{0,16},{16,0},{1,17},{17,1},{2,18},{18,2},{3,19},{19,3},{4,20},{20... | collective-permute-start | bytes 3145736 | tf_op jit(solution)/shard_map/ppermute | solution.py:439
  9.1 1.3 %collective-permute-start.1 = (bf16[16,4096]{1,0:T(8,128)(2,1)S(1)}, bf16[16,4096]{1,0:T(8,128)(2,1)S(1)}, u32[]{:S(2)}, u32[]{:S(2)}) collective-permute-start(bf16[16,4096]{1,0:T(8,128)(2,1)S(1)} %get-tuple-element.29), channel_id=1, source_target_pairs={{0,1},{1,2},{2,3},{4,5},{5,6},{6,7},{8,9},{9,10},{10,11},{12,13},{... | collective-permute-start | bytes 393224 | tf_op jit(solution)/shard_map/ppermute | solution.py:42
  10.4 0.3 collective-permute-start.8
  10.7 1.7 %collective-permute-done.2.refs_0_ = bf16[2,2,128,128]{3,2,1,0:T(8,128)(2,1)S(1)} collective-permute-done((bf16[2,2,128,128]{3,2,1,0:T(8,128)(2,1)S(1)}, bf16[2,2,128,128]{3,2,1,0:T(8,128)(2,1)S(1)}, u32[]{:S(2)}, u32[]{:S(2)}) %collective-permute-start.2) | collective-permute-done | bytes 131104 | tf_op jit(solution)/shard_map/ppermute | solution.py:439
  12.4 1.8 %collective-permute-start.3 = (bf16[2,2,128,128]{3,2,1,0:T(8,128)(2,1)S(1)}, bf16[2,2,128,128]{3,2,1,0:T(8,128)(2,1)S(1)}, u32[]{:S(2)}, u32[]{:S(2)}) collective-permute-start(bf16[2,2,128,128]{3,2,1,0:T(8,128)(2,1)S(1)} %collective-permute-done.2.refs_0_), channel_id=1, source_target_pairs={{0,2},{1,3},{2,0},{3,1},{4,6},{5,7},{6,4},{7,5},{8,10},{9,11},{10,... | collective-permute-start | bytes 393224 | tf_op jit(solution)/shard_map/ppermute | solution.py:439
  14.2 0.0 collective-permute-done.1.edge_ref
  14.2 0.0 copy-done
  14.2 0.8 %copy-done.4 = f32[4,4096]{1,0:T(4,128)S(1)} copy-done((f32[4,4096]{1,0:T(4,128)S(1)}, f32[4,4096]{1,0:T(4,128)}, u32[]{:S(2)}) %copy-start.4) | copy-done | bytes 65560
  15.0 0.7 %copy-done.5 = f32[4096]{0:T(1024)S(1)} copy-done((f32[4096]{0:T(1024)S(1)}, f32[4096]{0:T(1024)}, u32[]{:S(2)}) %copy-start.5) | copy-done | bytes 16408
  15.8 0.7 %copy-done.6 = s32[1,128]{1,0:T(1,128)S(1)} copy-done((s32[1,128]{1,0:T(1,128)S(1)}, s32[1,128]{1,0:T(1,128)}, u32[]{:S(2)}) %copy-start.6) | copy-done | bytes 536
  16.4 1.9 %conv_rows.1 = (bf16[32,128,128]{2,1,0:T(8,128)(2,1)S(1)}, f32[2,128,128]{2,1,0:T(8,128)S(1)}) custom-call(bf16[1,128,4096]{2,1,0:T(8,128)(2,1)S(1)} %copy-done, bf16[16,4096]{1,0:T(8,128)(2,1)S(1)} %collective-permute-done.1.edge_ref, s32[1,128]{1,0:T(1,128)S(1)} %copy-done.6, f32[4,4096]{1,0:T(4,128)S(1)} %copy-done.4, f32[1,4096]{1,0:T(1,128)S(1)} %bitcast.6), custom_call_target="tpu_custom_call" | custom-call | tf_op jit(solution)/shard_map/conv_rows/pallas_call | solution.py:239
  18.3 0.0 collective-permute-done.8.refs_0_
  18.3 2.7 %collective-permute-start.9 = (bf16[2,2,128,128]{3,2,1,0:T(8,128)(2,1)S(1)}, bf16[2,2,128,128]{3,2,1,0:T(8,128)(2,1)S(1)}, u32[]{:S(2)}, u32[]{:S(2)}) collective-permute-start(bf16[2,2,128,128]{3,2,1,0:T(8,128)(2,1)S(1)} %collective-permute-done.8.refs_0_), channel_id=1, source_target_pairs={{0,2},{1,3},{2,0},{3,1},{4,6},{5,7},{6,4},{7,5},{8,10},{9,11},{10,... | collective-permute-start | bytes 393224 | tf_op jit(solution)/shard_map/ppermute | solution.py:439
  21.0 0.0 copy-done.1
  21.0 0.0 copy-done.2
  21.1 0.6 %shard.4 = (f32[8,128,128]{2,1,0:T(8,128)S(1)}, f32[8,128,128]{2,1,0:T(8,128)S(1)}, f32[8,2,8,128]{3,2,1,0:T(8,128)S(1)}, f32[16,128]{1,0:T(8,128)S(1)}) custom-call(bf16[32,128,128]{2,1,0:T(8,128)(2,1)S(1)} %get-tuple-element.30.conv_ref, f32[2,128,128]{2,1,0:T(8,128)S(1)} %get-tuple-element.31.mask_ref, f32[2,4096]{1,0:T(2,128)S(1)} %copy-done.2, ...), custom_call_target="tpu_custom_call" | custom-call | tf_op jit(solution)/shard_map/shard/pallas_call | solution.py:327
  21.7 0.0 collective-permute-done.3.refs_2_
  21.7 0.0 collective-permute-done.6.refs_0_
  21.7 0.1 collective-permute-start.7
  21.8 0.5 %collective-permute-start.4 = (bf16[2,2,128,128]{3,2,1,0:T(8,128)(2,1)S(1)}, bf16[2,2,128,128]{3,2,1,0:T(8,128)(2,1)S(1)}, u32[]{:S(2)}, u32[]{:S(2)}) collective-permute-start(bf16[2,2,128,128]{3,2,1,0:T(8,128)(2,1)S(1)} %collective-permute-done.2.refs_0_), channel_id=1, source_target_pairs={{0,1},{1,0},{2,3},{3,2},{4,5},{5,4},{6,7},{7,6},{8,9},{9,8},{10,11... | collective-permute-start | bytes 393224 | tf_op jit(solution)/shard_map/ppermute | solution.py:439
  22.3 0.1 collective-permute-start.5
  22.3 2.0 %collective-permute-done.9.refs_2_ = bf16[2,2,128,128]{3,2,1,0:T(8,128)(2,1)S(1)} collective-permute-done((bf16[2,2,128,128]{3,2,1,0:T(8,128)(2,1)S(1)}, bf16[2,2,128,128]{3,2,1,0:T(8,128)(2,1)S(1)}, u32[]{:S(2)}, u32[]{:S(2)}) %collective-permute-start.9) | collective-permute-done | bytes 131104 | tf_op jit(solution)/shard_map/ppermute | solution.py:439
  24.3 0.0 collective-permute-start.10
  24.3 0.0 collective-permute-done.4.refs_1_
  24.3 0.5 %collective-permute-start.11 = (bf16[2,2,128,128]{3,2,1,0:T(8,128)(2,1)S(1)}, bf16[2,2,128,128]{3,2,1,0:T(8,128)(2,1)S(1)}, u32[]{:S(2)}, u32[]{:S(2)}) collective-permute-start(bf16[2,2,128,128]{3,2,1,0:T(8,128)(2,1)S(1)} %collective-permute-done.9.refs_2_), channel_id=1, source_target_pairs={{0,1},{1,0},{2,3},{3,2},{4,5},{5,4},{6,7},{7,6},{8,9},{9,8},{10,11... | collective-permute-start | bytes 393224 | tf_op jit(solution)/shard_map/ppermute | solution.py:439
  24.8 0.0 collective-permute-done.5.refs_3_
  24.9 0.6 %shard.5 = (f32[8,128,128]{2,1,0:T(8,128)S(1)}, f32[8,128,128]{2,1,0:T(8,128)S(1)}, f32[8,2,8,128]{3,2,1,0:T(8,128)S(1)}, f32[16,128]{1,0:T(8,128)S(1)}) custom-call(bf16[32,128,128]{2,1,0:T(8,128)(2,1)S(1)} %get-tuple-element.30.conv_ref, f32[2,128,128]{2,1,0:T(8,128)S(1)} %get-tuple-element.31.mask_ref, f32[2,4096]{1,0:T(2,128)S(1)} %copy-done.2, ...), custom_call_target="tpu_custom_call" | custom-call | tf_op jit(solution)/shard_map/shard/pallas_call | solution.py:327
  25.5 0.0 collective-permute-done.7.refs_1_
  25.5 0.6 %shard.6 = (f32[8,128,128]{2,1,0:T(8,128)S(1)}, f32[8,128,128]{2,1,0:T(8,128)S(1)}, f32[8,2,8,128]{3,2,1,0:T(8,128)S(1)}, f32[16,128]{1,0:T(8,128)S(1)}) custom-call(bf16[32,128,128]{2,1,0:T(8,128)(2,1)S(1)} %get-tuple-element.30.conv_ref, f32[2,128,128]{2,1,0:T(8,128)S(1)} %get-tuple-element.31.mask_ref, f32[2,4096]{1,0:T(2,128)S(1)} %copy-done.2, ...), custom_call_target="tpu_custom_call" | custom-call | tf_op jit(solution)/shard_map/shard/pallas_call | solution.py:327
  26.1 0.0 collective-permute-done.10.refs_1_
  26.1 0.0 collective-permute-done.11.refs_3_
  26.1 0.6 %shard.7 = (f32[8,128,128]{2,1,0:T(8,128)S(1)}, f32[8,128,128]{2,1,0:T(8,128)S(1)}, f32[8,2,8,128]{3,2,1,0:T(8,128)S(1)}, f32[64,128]{1,0:T(8,128)S(1)}) custom-call(bf16[32,128,128]{2,1,0:T(8,128)(2,1)S(1)} %get-tuple-element.30.conv_ref, f32[2,128,128]{2,1,0:T(8,128)S(1)} %get-tuple-element.31.mask_ref, f32[2,4096]{1,0:T(2,128)S(1)} %copy-done.2, ...), custom_call_target="tpu_custom_call" | custom-call | flops 5500000256 | tf_op jit(solution)/shard_map/shard/pallas_call | solution.py:327
  26.7 0.2 collective-permute-start.12
  26.9 1.7 %collective-permute-start.13 = (f32[64,128]{1,0:T(8,128)S(1)}, f32[64,128]{1,0:T(8,128)S(1)}, u32[]{:S(2)}, u32[]{:S(2)}) collective-permute-start(f32[64,128]{1,0:T(8,128)S(1)} %get-tuple-element.55), channel_id=1, source_target_pairs={{0,2},{1,3},{2,0},{3,1},{4,6},{5,7},{6,4},{7,5},{8,10},{9,11},{10,... | collective-permute-start | bytes 98312 | tf_op jit(solution)/shard_map/ppermute | solution.py:439
  28.5 0.1 collective-permute-start.14
  28.6 1.2 %lay_out.1 = (f32[32,128,128]{2,1,0:T(8,128)S(1)}, f32[32,128,128]{2,1,0:T(8,128)S(1)}) custom-call(f32[8,128,128]{2,1,0:T(8,128)S(1)} %get-tuple-element.32.refs_0_, f32[8,128,128]{2,1,0:T(8,128)S(1)} %get-tuple-element.33.refs_1_, f32[8,2,8,128]{3,2,1,0:T(8,128)S(1)} %get-tuple-element.34.refs_2_, f32[8,128,128]{2,1,0:T(8,128)S(1)} %get-tuple-element.38.refs_3_, ...), custom_call_target="tpu_custom_call" | custom-call | tf_op jit(solution)/shard_map/lay_out/pallas_call | solution.py:363
  29.8 0.0 collective-permute-done.12.refs_0_
  29.8 0.9 %collective-permute-done.13.refs_1_ = f32[64,128]{1,0:T(8,128)S(1)} collective-permute-done((f32[64,128]{1,0:T(8,128)S(1)}, f32[64,128]{1,0:T(8,128)S(1)}, u32[]{:S(2)}, u32[]{:S(2)}) %collective-permute-start.13) | collective-permute-done | bytes 32800 | tf_op jit(solution)/shard_map/ppermute | solution.py:439
  30.8 1.1 %collective-permute-done.14.refs_2_ = f32[64,128]{1,0:T(8,128)S(1)} collective-permute-done((f32[64,128]{1,0:T(8,128)S(1)}, f32[64,128]{1,0:T(8,128)S(1)}, u32[]{:S(2)}, u32[]{:S(2)}) %collective-permute-start.14) | collective-permute-done | bytes 32800 | tf_op jit(solution)/shard_map/ppermute | solution.py:439
  31.9 0.2 collective-permute-done.target_ref
  32.1 2.1 %final.1 = (bf16[1,128,4096]{2,1,0:T(8,128)(2,1)}, f32[1,128]{1,0:T(1,128)}) custom-call(bf16[1,128,4096]{2,1,0:T(8,128)(2,1)S(1)} %collective-permute-done.target_ref, f32[32,128,128]{2,1,0:T(8,128)S(1)} %get-tuple-element.53.state_ref, f32[32,128,128]{2,1,0:T(8,128)S(1)} %get-tuple-element.54.prod_ref, f32[64,128]{1,0:T(8,128)S(1)} %collective-permute-done.12.refs_0_, ...), custom_call_target="tpu_custom_call" | custom-call | tf_op jit(solution)/shard_map/final/pallas_call | solution.py:421
  (4 shorter events, 0.0 us)
Async XLA Ops:
  0.6 20.4 %copy-start.1 = (bf16[8,2,128,128]{3,2,1,0:T(8,128)(2,1)S(1)}, bf16[8,2,128,128]{3,2,1,0:T(8,128)(2,1)}, u32[]{:S(2)}) copy-start(bf16[8,2,128,128]{3,2,1,0:T(8,128)(2,1)} %refs_0_.1) | copy-start | bytes 1572868
  0.6 13.5 %copy-start = (bf16[1,128,4096]{2,1,0:T(8,128)(2,1)S(1)}, bf16[1,128,4096]{2,1,0:T(8,128)(2,1)}, u32[]{:S(2)}) copy-start(bf16[1,128,4096]{2,1,0:T(8,128)(2,1)} %x_ref.3) | copy-start | bytes 3145732
  0.7 20.4 %copy-start.3 = (f32[4096]{0:T(1024)S(1)}, f32[4096]{0:T(1024)}, u32[]{:S(2)}) copy-start(f32[4096]{0:T(1024)} %param.15) | copy-start | bytes 49156
  0.7 20.4 %copy-start.2 = (f32[2,4096]{1,0:T(2,128)S(1)}, f32[2,4096]{1,0:T(2,128)}, u32[]{:S(2)}) copy-start(f32[2,4096]{1,0:T(2,128)} %bias_ref.7) | copy-start | bytes 98308
  1.9 10.5 %collective-permute-start.2 = (bf16[2,2,128,128]{3,2,1,0:T(8,128)(2,1)S(1)}, bf16[2,2,128,128]{3,2,1,0:T(8,128)(2,1)S(1)}, u32[]{:S(2)}, u32[]{:S(2)}) collective-permute-start(bf16[2,2,128,128]{3,2,1,0:T(8,128)(2,1)S(1)} %get-tuple-element.35), channel_id=1, source_target_pairs={{0,8},{4,12},{8,0},{12,4},{1,9},{5,13},{9,1},{13,5},{2,10},{6,14},... | collective-permute-start | bytes 393224 | tf_op jit(solution)/shard_map/ppermute | solution.py:439
  6.0 15.7 %collective-permute-start.6 = (bf16[4,2,128,128]{3,2,1,0:T(8,128)(2,1)S(1)}, bf16[4,2,128,128]{3,2,1,0:T(8,128)(2,1)S(1)}, u32[]{:S(2)}, u32[]{:S(2)}) collective-permute-start(bf16[4,2,128,128]{3,2,1,0:T(8,128)(2,1)S(1)} %get-tuple-element.41), channel_id=1, source_target_pairs={{0,4},{4,0},{8,12},{12,8},{1,5},{5,1},{9,13},{13,9},{2,6},{6,2},{1... | collective-permute-start | bytes 786440 | tf_op jit(solution)/shard_map/ppermute | solution.py:439
  7.5 24.5 %collective-permute-start = (bf16[1,128,4096]{2,1,0:T(8,128)(2,1)}, bf16[1,128,4096]{2,1,0:T(8,128)(2,1)S(1)}, u32[]{:S(2)}, u32[]{:S(2)}) collective-permute-start(bf16[1,128,4096]{2,1,0:T(8,128)(2,1)} %param.10), channel_id=1, source_target_pairs={{0,16},{16,0},{1,17},{17,1},{2,18},{18,2},{3,19},{19,3},{4,20},{20... | collective-permute-start | bytes 3145736 | tf_op jit(solution)/shard_map/ppermute | solution.py:439
  9.1 5.1 %collective-permute-start.1 = (bf16[16,4096]{1,0:T(8,128)(2,1)S(1)}, bf16[16,4096]{1,0:T(8,128)(2,1)S(1)}, u32[]{:S(2)}, u32[]{:S(2)}) collective-permute-start(bf16[16,4096]{1,0:T(8,128)(2,1)S(1)} %get-tuple-element.29), channel_id=1, source_target_pairs={{0,1},{1,2},{2,3},{4,5},{5,6},{6,7},{8,9},{9,10},{10,11},{12,13},{... | collective-permute-start | bytes 393224 | tf_op jit(solution)/shard_map/ppermute | solution.py:42
  10.4 8.0 %collective-permute-start.8 = (bf16[2,2,128,128]{3,2,1,0:T(8,128)(2,1)S(1)}, bf16[2,2,128,128]{3,2,1,0:T(8,128)(2,1)S(1)}, u32[]{:S(2)}, u32[]{:S(2)}) collective-permute-start(bf16[2,2,128,128]{3,2,1,0:T(8,128)(2,1)S(1)} %get-tuple-element.35), channel_id=1, source_target_pairs={{0,12},{4,8},{8,4},{12,0},{1,13},{5,9},{9,5},{13,1},{2,14},{6,10},... | collective-permute-start | bytes 393224 | tf_op jit(solution)/shard_map/ppermute | solution.py:439
  12.4 9.3 %collective-permute-start.3 = (bf16[2,2,128,128]{3,2,1,0:T(8,128)(2,1)S(1)}, bf16[2,2,128,128]{3,2,1,0:T(8,128)(2,1)S(1)}, u32[]{:S(2)}, u32[]{:S(2)}) collective-permute-start(bf16[2,2,128,128]{3,2,1,0:T(8,128)(2,1)S(1)} %collective-permute-done.2.refs_0_), channel_id=1, source_target_pairs={{0,2},{1,3},{2,0},{3,1},{4,6},{5,7},{6,4},{7,5},{8,10},{9,11},{10,... | collective-permute-start | bytes 393224 | tf_op jit(solution)/shard_map/ppermute | solution.py:439
  14.2 0.8 %copy-start.4 = (f32[4,4096]{1,0:T(4,128)S(1)}, f32[4,4096]{1,0:T(4,128)}, u32[]{:S(2)}) copy-start(f32[4,4096]{1,0:T(4,128)} %w_ref.3) | copy-start | bytes 196612
  15.0 0.7 %copy-start.5 = (f32[4096]{0:T(1024)S(1)}, f32[4096]{0:T(1024)}, u32[]{:S(2)}) copy-start(f32[4096]{0:T(1024)} %param.14) | copy-start | bytes 49156
  15.7 0.7 %copy-start.6 = (s32[1,128]{1,0:T(1,128)S(1)}, s32[1,128]{1,0:T(1,128)}, u32[]{:S(2)}) copy-start(s32[1,128]{1,0:T(1,128)} %pos_ref.1) | copy-start | bytes 1540
  18.3 6.0 %collective-permute-start.9 = (bf16[2,2,128,128]{3,2,1,0:T(8,128)(2,1)S(1)}, bf16[2,2,128,128]{3,2,1,0:T(8,128)(2,1)S(1)}, u32[]{:S(2)}, u32[]{:S(2)}) collective-permute-start(bf16[2,2,128,128]{3,2,1,0:T(8,128)(2,1)S(1)} %collective-permute-done.8.refs_0_), channel_id=1, source_target_pairs={{0,2},{1,3},{2,0},{3,1},{4,6},{5,7},{6,4},{7,5},{8,10},{9,11},{10,... | collective-permute-start | bytes 393224 | tf_op jit(solution)/shard_map/ppermute | solution.py:439
  21.7 3.8 %collective-permute-start.7 = (bf16[4,2,128,128]{3,2,1,0:T(8,128)(2,1)S(1)}, bf16[4,2,128,128]{3,2,1,0:T(8,128)(2,1)S(1)}, u32[]{:S(2)}, u32[]{:S(2)}) collective-permute-start(bf16[4,2,128,128]{3,2,1,0:T(8,128)(2,1)S(1)} %collective-permute-done.6.refs_0_), channel_id=1, source_target_pairs={{0,1},{1,0},{2,3},{3,2},{4,5},{5,4},{6,7},{7,6},{8,9},{9,8},{10,11... | collective-permute-start | bytes 786440 | tf_op jit(solution)/shard_map/ppermute | solution.py:439
  21.8 2.6 %collective-permute-start.4 = (bf16[2,2,128,128]{3,2,1,0:T(8,128)(2,1)S(1)}, bf16[2,2,128,128]{3,2,1,0:T(8,128)(2,1)S(1)}, u32[]{:S(2)}, u32[]{:S(2)}) collective-permute-start(bf16[2,2,128,128]{3,2,1,0:T(8,128)(2,1)S(1)} %collective-permute-done.2.refs_0_), channel_id=1, source_target_pairs={{0,1},{1,0},{2,3},{3,2},{4,5},{5,4},{6,7},{7,6},{8,9},{9,8},{10,11... | collective-permute-start | bytes 393224 | tf_op jit(solution)/shard_map/ppermute | solution.py:439
  22.3 2.6 %collective-permute-start.5 = (bf16[2,2,128,128]{3,2,1,0:T(8,128)(2,1)S(1)}, bf16[2,2,128,128]{3,2,1,0:T(8,128)(2,1)S(1)}, u32[]{:S(2)}, u32[]{:S(2)}) collective-permute-start(bf16[2,2,128,128]{3,2,1,0:T(8,128)(2,1)S(1)} %collective-permute-done.3.refs_2_), channel_id=1, source_target_pairs={{0,1},{1,0},{2,3},{3,2},{4,5},{5,4},{6,7},{7,6},{8,9},{9,8},{10,11... | collective-permute-start | bytes 393224 | tf_op jit(solution)/shard_map/ppermute | solution.py:439
  24.3 1.7 %collective-permute-start.10 = (bf16[2,2,128,128]{3,2,1,0:T(8,128)(2,1)S(1)}, bf16[2,2,128,128]{3,2,1,0:T(8,128)(2,1)S(1)}, u32[]{:S(2)}, u32[]{:S(2)}) collective-permute-start(bf16[2,2,128,128]{3,2,1,0:T(8,128)(2,1)S(1)} %collective-permute-done.8.refs_0_), channel_id=1, source_target_pairs={{0,1},{1,0},{2,3},{3,2},{4,5},{5,4},{6,7},{7,6},{8,9},{9,8},{10,11... | collective-permute-start | bytes 393224 | tf_op jit(solution)/shard_map/ppermute | solution.py:439
  24.3 1.7 %collective-permute-start.11 = (bf16[2,2,128,128]{3,2,1,0:T(8,128)(2,1)S(1)}, bf16[2,2,128,128]{3,2,1,0:T(8,128)(2,1)S(1)}, u32[]{:S(2)}, u32[]{:S(2)}) collective-permute-start(bf16[2,2,128,128]{3,2,1,0:T(8,128)(2,1)S(1)} %collective-permute-done.9.refs_2_), channel_id=1, source_target_pairs={{0,1},{1,0},{2,3},{3,2},{4,5},{5,4},{6,7},{7,6},{8,9},{9,8},{10,11... | collective-permute-start | bytes 393224 | tf_op jit(solution)/shard_map/ppermute | solution.py:439
  26.7 3.1 %collective-permute-start.12 = (f32[64,128]{1,0:T(8,128)S(1)}, f32[64,128]{1,0:T(8,128)S(1)}, u32[]{:S(2)}, u32[]{:S(2)}) collective-permute-start(f32[64,128]{1,0:T(8,128)S(1)} %get-tuple-element.55), channel_id=1, source_target_pairs={{0,1},{1,0},{2,3},{3,2},{4,5},{5,4},{6,7},{7,6},{8,9},{9,8},{10,11... | collective-permute-start | bytes 98312 | tf_op jit(solution)/shard_map/ppermute | solution.py:439
  26.9 3.9 %collective-permute-start.13 = (f32[64,128]{1,0:T(8,128)S(1)}, f32[64,128]{1,0:T(8,128)S(1)}, u32[]{:S(2)}, u32[]{:S(2)}) collective-permute-start(f32[64,128]{1,0:T(8,128)S(1)} %get-tuple-element.55), channel_id=1, source_target_pairs={{0,2},{1,3},{2,0},{3,1},{4,6},{5,7},{6,4},{7,5},{8,10},{9,11},{10,... | collective-permute-start | bytes 98312 | tf_op jit(solution)/shard_map/ppermute | solution.py:439
  28.5 3.4 %collective-permute-start.14 = (f32[64,128]{1,0:T(8,128)S(1)}, f32[64,128]{1,0:T(8,128)S(1)}, u32[]{:S(2)}, u32[]{:S(2)}) collective-permute-start(f32[64,128]{1,0:T(8,128)S(1)} %get-tuple-element.55), channel_id=1, source_target_pairs={{0,3},{1,2},{2,1},{3,0},{4,7},{5,6},{6,5},{7,4},{8,11},{9,10},{10,... | collective-permute-start | bytes 98312 | tf_op jit(solution)/shard_map/ppermute | solution.py:439

commit v5 on v4

--- a/solution.py
+++ b/solution.py
@@ -149,7 +149,9 @@
     )
 
 
-def cut_kernel(x_ref, w_ref, half_ref, quarter_ref, edge_ref, sem):
+def cut_kernel(x_ref, w_ref, *refs):
+    small, refs = refs[: len(refs) // 2 - 2], refs[len(refs) // 2 - 2 :]
+    half_ref, quarter_ref, edge_ref, *near, sem = refs
     here = lax.axis_index("seq")
     tokens = x_ref.shape[1]
     halves, quarters = half_ref.shape[0], quarter_ref.shape[0]
@@ -160,13 +162,15 @@
         pltpu.make_async_copy(w_ref.at[pl.ds(here * quarters, quarters)], quarter_ref, sem.at[1]),
         pltpu.make_async_copy(x_ref.at[0, pl.ds(tokens - EDGE, EDGE), :], edge_ref, sem.at[2]),
     ]
+    for index, (source, target) in enumerate(zip(small, near)):
+        copies.append(pltpu.make_async_copy(source, target, sem.at[3 + index]))
     for copy in copies:
         copy.start()
     for copy in copies:
         copy.wait()
 
 
-def cut(branch_x, gate_weights):
+def cut(branch_x, gate_weights, *small):
     held = gate_weights.shape[0]
     rest = gate_weights.shape[1:]
     return pallas(
@@ -176,13 +180,16 @@
             jax.ShapeDtypeStruct((held // 2,) + rest, jnp.bfloat16),
             jax.ShapeDtypeStruct((held // 4,) + rest, jnp.bfloat16),
             jax.ShapeDtypeStruct((EDGE, branch_x.shape[2]), jnp.bfloat16),
-        ],
-        [pl.BlockSpec(memory_space=pltpu.HBM)] * 2,
-        [pl.BlockSpec(memory_space=pl.ANY)] * 3,
-        [pltpu.SemaphoreType.DMA((3,))],
+        ]
+        + [jax.ShapeDtypeStruct(value.shape, value.dtype) for value in small],
+        [pl.BlockSpec(memory_space=pltpu.HBM)] * (2 + len(small)),
+        [pl.BlockSpec(memory_space=pl.ANY)] * (3 + len(small)),
+        [pltpu.SemaphoreType.DMA((3 + len(small),))],
     )(
-        pltpu.with_memory_space_constraint(branch_x, pltpu.HBM),
-        pltpu.with_memory_space_constraint(gate_weights, pltpu.HBM),
+        *[
+            pltpu.with_memory_space_constraint(value, pltpu.HBM)
+            for value in (branch_x, gate_weights, *small)
+        ]
     )
 
 
@@ -370,18 +377,15 @@
     )(*flat)
 
 
-def final_kernel(pairs, target_ref, state_ref, prod_ref, *refs):
+def enter_kernel(pairs, state_ref, prod_ref, *refs):
     devices = lax.axis_size("seq")
     here = lax.axis_index("seq")
-    ends, (student_ref, loss_ref, ends_s, held, sem) = refs[: devices - 1], refs[devices - 1 :]
-    tokens = state_ref.shape[1]
+    ends, (rows_ref, scale_ref, ends_s) = refs[: devices - 1], refs[devices - 1 :]
+    tokens, full = rows_ref.shape
     heads = state_ref.shape[0] // len(pairs)
-    width = heads * HS
     for apart in range(1, devices):
         ends_s[lax.bitwise_xor(here, apart)] = ends[apart - 1][...]
     squares = jnp.zeros((tokens, HS), jnp.float32)
-    copies = []
-    bases = []
     for slot, pair in enumerate(pairs):
         incoming = jnp.zeros((heads, HS), jnp.float32)
         row = 2 * heads * slot
@@ -391,48 +395,62 @@
             )
             incoming = jnp.where(place < here, after, incoming)
         base = lax.bitwise_xor(lax.axis_index("fsdp"), pair) * heads
-        bases.append(base)
         for head in range(heads):
             at_head = slot * heads + head
             rounded = (
                 state_ref[at_head] + prod_ref[at_head] * incoming[head : head + 1]
             ).astype(jnp.bfloat16)
-            student_ref[0, :, lanes_of(base + head)] = rounded
+            rows_ref[:, lanes_of(base + head)] = rounded
             value = rounded.astype(jnp.float32)
             squares = squares + value * value
-    full = student_ref.shape[2]
     mean = jnp.sum(squares, axis=1, keepdims=True) * (1.0 / full)
-    scale = jnp.broadcast_to(lax.rsqrt(mean + 1e-06), (tokens, HS))
+    scale_ref[...] = jnp.broadcast_to(lax.rsqrt(mean + 1e-06), (tokens, HS))
+
+
+def enter(pairs, states, products, ends):
+    tokens = states.shape[1]
+    return pallas(
+        functools.partial(enter_kernel, pairs),
+        "enter",
+        [
+            jax.ShapeDtypeStruct((tokens, HEADS * HS), jnp.bfloat16),
+            jax.ShapeDtypeStruct((tokens, HS), jnp.float32),
+        ],
+        in_vmem(2 + len(ends)),
+        in_vmem(2),
+        [pltpu.VMEM((len(ends) + 1,) + ends[0].shape, jnp.float32)],
+    )(states, products, *ends)
+
+
+def loss_kernel(rows_ref, scale_ref, target_ref, student_ref, loss_ref, sem):
+    tokens, full = rows_ref.shape
+    copy = pltpu.make_async_copy(rows_ref, student_ref.at[0], sem)
+    copy.start()
+    scale = scale_ref[...]
     total = jnp.zeros((tokens, HS), jnp.float32)
-    for slot, base in enumerate(bases):
-        for head in range(heads):
-            at_head = slot * heads + head
-            value = student_ref[0, :, lanes_of(base + head)].astype(jnp.float32)
-            off = value * scale - target_ref[0, :, lanes_of(base + head)].astype(jnp.float32)
-            total = total + off * off
+    for start in range(0, full, HS):
+        lanes = slice(start, start + HS)
+        off = rows_ref[:, lanes].astype(jnp.float32) * scale - target_ref[0, :, lanes].astype(
+            jnp.float32
+        )
+        total = total + off * off
     loss_ref[...] = jnp.sum(total.T, axis=0, keepdims=True) * (1.0 / full)
-    for copy in copies:
-        copy.wait()
-
-
-def final(pairs, target, states, products, ends):
-    tokens = states.shape[1]
-    full = HEADS * HS
+    copy.wait()
+
+
+def losses(rows, scale, target):
+    tokens, full = rows.shape
     return pallas(
-        functools.partial(final_kernel, pairs),
-        "final",
+        loss_kernel,
+        "losses",
         [
             jax.ShapeDtypeStruct((1, tokens, full), jnp.bfloat16),
             jax.ShapeDtypeStruct((1, tokens), jnp.float32),
         ],
-        in_vmem(3 + len(ends)),
-        in_vmem(2),
-        [
-            pltpu.VMEM((len(ends) + 1,) + ends[0].shape, jnp.float32),
-            pltpu.VMEM((tokens, full), jnp.bfloat16),
-            pltpu.SemaphoreType.DMA((len(pairs),)),
-        ],
-    )(target, states, products, *ends)
+        in_vmem(3),
+        [pl.BlockSpec(memory_space=pltpu.HBM)] + in_vmem(1),
+        [pltpu.SemaphoreType.DMA],
+    )(rows, scale, target)
 
 
 def swap(value, axis, apart):
@@ -449,11 +467,13 @@
     tokens, width = branch_x.shape[1:]
     total = lax.axis_size("seq") * tokens
     target = swap(teacher_held, "segment", 1)
-    half, quarter, edge = cut(branch_x, gate_weights)
+    half, quarter, edge, *small = cut(
+        branch_x, gate_weights, positions, conv_weight, conv_bias.reshape(1, width)
+    )
     quarters = {pair: swap(quarter, "fsdp", pair) for pair in (2, 3)}
     half = swap(half, "fsdp", 1)
     edge = from_behind(edge, "seq", 1)
-    conv, masks = conv_rows(branch_x, edge, positions, conv_weight, conv_bias.reshape(1, width))
+    conv, masks = conv_rows(branch_x, edge, *small)
     params = (gate_bias, decay_rate.reshape(1, width))
     parts = [shard(conv, masks, params, 0, [gate_weights], total)]
     two = swap(quarters[2], "seq", 2)
@@ -472,7 +492,8 @@
     end = parts[-1][3]
     ends = [swap(end, "seq", apart) for apart in (1, 2, 3)]
     states, products = lay_out(parts)
-    return final((0, 2, 1, 3), target, states, products, ends)
+    rows, scale = enter((0, 2, 1, 3), states, products, ends)
+    return losses(rows, scale, target)
 
 
 def solution(mesh):

time: 34.5 us -> 33.8 us (0.980)
  local copies, waits for them, and re-layouts: 2.23 us -> 0.02 us
  waiting for transfers between devices: 6.01 us -> 7.99 us
  starting transfers between devices: 16.4 us -> 16 us
    unnamed x14 -> x8, local copies, waits for them, and re-layouts: 2.23 us -> 0.02 us
    ppermute x14, waiting for transfers between devices: 6.01 us -> 7.99 us  [swap(): lax.ppermute(value, axis, [(i, i ^ apart) for i in range(lax.axis_size(ax...]
    ppermute x14, starting transfers between devices: 15.1 us -> 14.7 us  [swap(): lax.ppermute(value, axis, [(i, i ^ apart) for i in range(lax.axis_size(ax...]
    pallas_call x1 -> x2, Pallas kernels: 2.09 us -> 2.1 us  [the longest x1 1.49 us: losses(): pallas(loss_kernel, 'losses', [jax.ShapeDtypeStruct((1, tokens, full), jn...]
  transfers between devices with their start and end apart: 15 -> 15, of which waited for: 5 -> 6; matrix products, arithmetic and copies ran while one was open for 0% -> 0% of each run, Pallas kernels for 16% -> 18%
where the time goes in v5:
time: 33.8 us; the launch traced here: 33.6 us
  starting transfers between devices  16 us (47%)
  Pallas kernels  8.88 us (26%)
  waiting for transfers between devices  7.99 us (24%)
  between operations  0.78 us (2%)
    ppermute x14, starting transfers between devices, swap(): lax.ppermute(value, axis, [(i, i ^ apart) for i in range(lax.axis_size(ax...  14.7 us
    ppermute x14, waiting for transfers between devices, swap(): lax.ppermute(value, axis, [(i, i ^ apart) for i in range(lax.axis_size(ax...  7.99 us
    pallas_call x4, Pallas kernels, shard(): pallas(functools.partial(shard_kernel, total, pair, counts), 'shard', [ja...  2.41 us
    pallas_call x1, Pallas kernels, conv_rows(): pallas(conv_kernel, 'conv_rows', [jax.ShapeDtypeStruct((heads, tokens, HS...  1.91 us
    pallas_call x1, Pallas kernels, losses(): pallas(loss_kernel, 'losses', [jax.ShapeDtypeStruct((1, tokens, full), jn...  1.49 us
    ppermute x1, starting transfers between devices, from_behind(): lax.ppermute(value, axis, [(source, source + steps) for source in range(l...  1.29 us
    pallas_call x1, Pallas kernels, cut(): pallas(cut_kernel, 'cut', [jax.ShapeDtypeStruct((held // 2,) + rest, jnp....  1.24 us
    pallas_call x1, Pallas kernels, lay_out(): pallas(lay_kernel, 'lay_out', [whole, whole], in_vmem(len(flat)), in_vmem...  1.22 us
  transfers between devices with their start and end apart: 15, of which 6 were waited for; matrix products, arithmetic and copies ran while one was open for 0% of the time, Pallas kernels for 18%

profile of v5, /device:TPU:0, one launch (start us, length us, event | category | flops | bytes accessed | tf_op | source)
XLA Modules:
  0.0 33.6 jit_solution(7199747219473308456)
XLA Ops:
  0.6 0.0 copy-start.1
  0.6 0.0 copy-start
  0.7 0.0 copy-start.3
  0.7 0.0 copy-start.2
  0.7 1.2 %cut.1 = (bf16[4,2,128,128]{3,2,1,0:T(8,128)(2,1)S(1)}, bf16[2,2,128,128]{3,2,1,0:T(8,128)(2,1)S(1)}, bf16[16,4096]{1,0:T(8,128)(2,1)S(1)}, s32[1,128]{1,0:T(1,1...) custom-call(bf16[1,128,4096]{2,1,0:T(8,128)(2,1)} %x_ref.3, bf16[8,2,128,128]{3,2,1,0:T(8,128)(2,1)} %refs_0_.3, ...), custom_call_target="tpu_custom_call" | custom-call | tf_op jit(solution)/shard_map/cut/pallas_call | solution.py:176
  1.9 4.1 %collective-permute-start.1 = (bf16[2,2,128,128]{3,2,1,0:T(8,128)(2,1)S(1)}, bf16[2,2,128,128]{3,2,1,0:T(8,128)(2,1)S(1)}, u32[]{:S(2)}, u32[]{:S(2)}) collective-permute-start(bf16[2,2,128,128]{3,2,1,0:T(8,128)(2,1)S(1)} %get-tuple-element.43), channel_id=1, source_target_pairs={{0,8},{4,12},{8,0},{12,4},{1,9},{5,13},{9,1},{13,5},{2,10},{6,14},... | collective-permute-start | bytes 393224 | tf_op jit(solution)/shard_map/ppermute | solution.py:457
  6.0 1.6 %collective-permute-start.5 = (bf16[4,2,128,128]{3,2,1,0:T(8,128)(2,1)S(1)}, bf16[4,2,128,128]{3,2,1,0:T(8,128)(2,1)S(1)}, u32[]{:S(2)}, u32[]{:S(2)}) collective-permute-start(bf16[4,2,128,128]{3,2,1,0:T(8,128)(2,1)S(1)} %get-tuple-element.49), channel_id=1, source_target_pairs={{0,4},{4,0},{8,12},{12,8},{1,5},{5,1},{9,13},{13,9},{2,6},{6,2},{1... | collective-permute-start | bytes 786440 | tf_op jit(solution)/shard_map/ppermute | solution.py:457
  7.6 1.5 %collective-permute-start.14 = (bf16[1,128,4096]{2,1,0:T(8,128)(2,1)}, bf16[1,128,4096]{2,1,0:T(8,128)(2,1)S(1)}, u32[]{:S(2)}, u32[]{:S(2)}) collective-permute-start(bf16[1,128,4096]{2,1,0:T(8,128)(2,1)} %param.10), channel_id=1, source_target_pairs={{0,16},{16,0},{1,17},{17,1},{2,18},{18,2},{3,19},{19,3},{4,20},{20... | collective-permute-start | bytes 3145736 | tf_op jit(solution)/shard_map/ppermute | solution.py:457
  9.1 1.3 %collective-permute-start = (bf16[16,4096]{1,0:T(8,128)(2,1)S(1)}, bf16[16,4096]{1,0:T(8,128)(2,1)S(1)}, u32[]{:S(2)}, u32[]{:S(2)}) collective-permute-start(bf16[16,4096]{1,0:T(8,128)(2,1)S(1)} %get-tuple-element.34), channel_id=1, source_target_pairs={{0,1},{1,2},{2,3},{4,5},{5,6},{6,7},{8,9},{9,10},{10,11},{12,13},{... | collective-permute-start | bytes 393224 | tf_op jit(solution)/shard_map/ppermute | solution.py:42
  10.4 0.3 collective-permute-start.7
  10.7 1.7 %collective-permute-done.1.refs_0_ = bf16[2,2,128,128]{3,2,1,0:T(8,128)(2,1)S(1)} collective-permute-done((bf16[2,2,128,128]{3,2,1,0:T(8,128)(2,1)S(1)}, bf16[2,2,128,128]{3,2,1,0:T(8,128)(2,1)S(1)}, u32[]{:S(2)}, u32[]{:S(2)}) %collective-permute-start.1) | collective-permute-done | bytes 131104 | tf_op jit(solution)/shard_map/ppermute | solution.py:457
  12.4 1.8 %collective-permute-start.2 = (bf16[2,2,128,128]{3,2,1,0:T(8,128)(2,1)S(1)}, bf16[2,2,128,128]{3,2,1,0:T(8,128)(2,1)S(1)}, u32[]{:S(2)}, u32[]{:S(2)}) collective-permute-start(bf16[2,2,128,128]{3,2,1,0:T(8,128)(2,1)S(1)} %collective-permute-done.1.refs_0_), channel_id=1, source_target_pairs={{0,2},{1,3},{2,0},{3,1},{4,6},{5,7},{6,4},{7,5},{8,10},{9,11},{10,... | collective-permute-start | bytes 393224 | tf_op jit(solution)/shard_map/ppermute | solution.py:457
  14.2 0.0 collective-permute-done.edge_ref
  14.2 0.0 copy-done
  14.2 1.9 %conv_rows.1 = (bf16[32,128,128]{2,1,0:T(8,128)(2,1)S(1)}, f32[2,128,128]{2,1,0:T(8,128)S(1)}) custom-call(bf16[1,128,4096]{2,1,0:T(8,128)(2,1)S(1)} %copy-done, bf16[16,4096]{1,0:T(8,128)(2,1)S(1)} %collective-permute-done.edge_ref, s32[1,128]{1,0:T(1,128)S(1)} %get-tuple-element.35.pos_ref, f32[4,4096]{1,0:T(4,128)S(1)} %get-tuple-element.36.w_ref, ...), custom_call_target="tpu_custom_call" | custom-call | tf_op jit(solution)/shard_map/conv_rows/pallas_call | solution.py:246
  16.1 2.1 %collective-permute-done.7.refs_0_ = bf16[2,2,128,128]{3,2,1,0:T(8,128)(2,1)S(1)} collective-permute-done((bf16[2,2,128,128]{3,2,1,0:T(8,128)(2,1)S(1)}, bf16[2,2,128,128]{3,2,1,0:T(8,128)(2,1)S(1)}, u32[]{:S(2)}, u32[]{:S(2)}) %collective-permute-start.7) | collective-permute-done | bytes 131104 | tf_op jit(solution)/shard_map/ppermute | solution.py:457
  18.2 2.3 %collective-permute-start.8 = (bf16[2,2,128,128]{3,2,1,0:T(8,128)(2,1)S(1)}, bf16[2,2,128,128]{3,2,1,0:T(8,128)(2,1)S(1)}, u32[]{:S(2)}, u32[]{:S(2)}) collective-permute-start(bf16[2,2,128,128]{3,2,1,0:T(8,128)(2,1)S(1)} %collective-permute-done.7.refs_0_), channel_id=1, source_target_pairs={{0,2},{1,3},{2,0},{3,1},{4,6},{5,7},{6,4},{7,5},{8,10},{9,11},{10,... | collective-permute-start | bytes 393224 | tf_op jit(solution)/shard_map/ppermute | solution.py:457
  20.5 0.0 copy-done.1
  20.5 0.0 copy-done.3
  20.5 0.0 copy-done.2
  20.5 0.6 %shard.4 = (f32[8,128,128]{2,1,0:T(8,128)S(1)}, f32[8,128,128]{2,1,0:T(8,128)S(1)}, f32[8,2,8,128]{3,2,1,0:T(8,128)S(1)}, f32[16,128]{1,0:T(8,128)S(1)}) custom-call(bf16[32,128,128]{2,1,0:T(8,128)(2,1)S(1)} %get-tuple-element.38.conv_ref, f32[2,128,128]{2,1,0:T(8,128)S(1)} %get-tuple-element.39.mask_ref, f32[2,4096]{1,0:T(2,128)S(1)} %copy-done.2, ...), custom_call_target="tpu_custom_call" | custom-call | tf_op jit(solution)/shard_map/shard/pallas_call | solution.py:334
  21.2 0.0 collective-permute-done.2.refs_2_
  21.2 0.0 collective-permute-done.5.refs_0_
  21.2 0.1 collective-permute-start.6
  21.3 0.5 %collective-permute-start.3 = (bf16[2,2,128,128]{3,2,1,0:T(8,128)(2,1)S(1)}, bf16[2,2,128,128]{3,2,1,0:T(8,128)(2,1)S(1)}, u32[]{:S(2)}, u32[]{:S(2)}) collective-permute-start(bf16[2,2,128,128]{3,2,1,0:T(8,128)(2,1)S(1)} %collective-permute-done.1.refs_0_), channel_id=1, source_target_pairs={{0,1},{1,0},{2,3},{3,2},{4,5},{5,4},{6,7},{7,6},{8,9},{9,8},{10,11... | collective-permute-start | bytes 393224 | tf_op jit(solution)/shard_map/ppermute | solution.py:457
  21.8 0.1 collective-permute-start.4
  21.8 2.5 %collective-permute-done.8.refs_2_ = bf16[2,2,128,128]{3,2,1,0:T(8,128)(2,1)S(1)} collective-permute-done((bf16[2,2,128,128]{3,2,1,0:T(8,128)(2,1)S(1)}, bf16[2,2,128,128]{3,2,1,0:T(8,128)(2,1)S(1)}, u32[]{:S(2)}, u32[]{:S(2)}) %collective-permute-start.8) | collective-permute-done | bytes 131104 | tf_op jit(solution)/shard_map/ppermute | solution.py:457
  24.4 0.0 collective-permute-start.9
  24.4 0.0 collective-permute-done.3.refs_1_
  24.4 0.5 %collective-permute-start.10 = (bf16[2,2,128,128]{3,2,1,0:T(8,128)(2,1)S(1)}, bf16[2,2,128,128]{3,2,1,0:T(8,128)(2,1)S(1)}, u32[]{:S(2)}, u32[]{:S(2)}) collective-permute-start(bf16[2,2,128,128]{3,2,1,0:T(8,128)(2,1)S(1)} %collective-permute-done.8.refs_2_), channel_id=1, source_target_pairs={{0,1},{1,0},{2,3},{3,2},{4,5},{5,4},{6,7},{7,6},{8,9},{9,8},{10,11... | collective-permute-start | bytes 393224 | tf_op jit(solution)/shard_map/ppermute | solution.py:457
  24.9 0.0 collective-permute-done.4.refs_3_
  24.9 0.6 %shard.5 = (f32[8,128,128]{2,1,0:T(8,128)S(1)}, f32[8,128,128]{2,1,0:T(8,128)S(1)}, f32[8,2,8,128]{3,2,1,0:T(8,128)S(1)}, f32[16,128]{1,0:T(8,128)S(1)}) custom-call(bf16[32,128,128]{2,1,0:T(8,128)(2,1)S(1)} %get-tuple-element.38.conv_ref, f32[2,128,128]{2,1,0:T(8,128)S(1)} %get-tuple-element.39.mask_ref, f32[2,4096]{1,0:T(2,128)S(1)} %copy-done.2, ...), custom_call_target="tpu_custom_call" | custom-call | tf_op jit(solution)/shard_map/shard/pallas_call | solution.py:334
  25.5 0.0 collective-permute-done.6.refs_1_
  25.5 0.6 %shard.6 = (f32[8,128,128]{2,1,0:T(8,128)S(1)}, f32[8,128,128]{2,1,0:T(8,128)S(1)}, f32[8,2,8,128]{3,2,1,0:T(8,128)S(1)}, f32[16,128]{1,0:T(8,128)S(1)}) custom-call(bf16[32,128,128]{2,1,0:T(8,128)(2,1)S(1)} %get-tuple-element.38.conv_ref, f32[2,128,128]{2,1,0:T(8,128)S(1)} %get-tuple-element.39.mask_ref, f32[2,4096]{1,0:T(2,128)S(1)} %copy-done.2, ...), custom_call_target="tpu_custom_call" | custom-call | tf_op jit(solution)/shard_map/shard/pallas_call | solution.py:334
  26.1 0.0 collective-permute-done.9.refs_1_
  26.1 0.0 collective-permute-done.10.refs_3_
  26.1 0.6 %shard.7 = (f32[8,128,128]{2,1,0:T(8,128)S(1)}, f32[8,128,128]{2,1,0:T(8,128)S(1)}, f32[8,2,8,128]{3,2,1,0:T(8,128)S(1)}, f32[64,128]{1,0:T(8,128)S(1)}) custom-call(bf16[32,128,128]{2,1,0:T(8,128)(2,1)S(1)} %get-tuple-element.38.conv_ref, f32[2,128,128]{2,1,0:T(8,128)S(1)} %get-tuple-element.39.mask_ref, f32[2,4096]{1,0:T(2,128)S(1)} %copy-done.2, ...), custom_call_target="tpu_custom_call" | custom-call | flops 5500000256 | tf_op jit(solution)/shard_map/shard/pallas_call | solution.py:334
  26.8 0.2 collective-permute-start.11
  26.9 1.1 %collective-permute-start.12 = (f32[64,128]{1,0:T(8,128)S(1)}, f32[64,128]{1,0:T(8,128)S(1)}, u32[]{:S(2)}, u32[]{:S(2)}) collective-permute-start(f32[64,128]{1,0:T(8,128)S(1)} %get-tuple-element.63), channel_id=1, source_target_pairs={{0,2},{1,3},{2,0},{3,1},{4,6},{5,7},{6,4},{7,5},{8,10},{9,11},{10,... | collective-permute-start | bytes 98312 | tf_op jit(solution)/shard_map/ppermute | solution.py:457
  28.0 0.7 %collective-permute-start.13 = (f32[64,128]{1,0:T(8,128)S(1)}, f32[64,128]{1,0:T(8,128)S(1)}, u32[]{:S(2)}, u32[]{:S(2)}) collective-permute-start(f32[64,128]{1,0:T(8,128)S(1)} %get-tuple-element.63), channel_id=1, source_target_pairs={{0,3},{1,2},{2,1},{3,0},{4,7},{5,6},{6,5},{7,4},{8,11},{9,10},{10,... | collective-permute-start | bytes 98312 | tf_op jit(solution)/shard_map/ppermute | solution.py:457
  28.7 1.2 %lay_out.1 = (f32[32,128,128]{2,1,0:T(8,128)S(1)}, f32[32,128,128]{2,1,0:T(8,128)S(1)}) custom-call(f32[8,128,128]{2,1,0:T(8,128)S(1)} %get-tuple-element.40.refs_0_, f32[8,128,128]{2,1,0:T(8,128)S(1)} %get-tuple-element.41.refs_1_, f32[8,2,8,128]{3,2,1,0:T(8,128)S(1)} %get-tuple-element.42.refs_2_, f32[8,128,128]{2,1,0:T(8,128)S(1)} %get-tuple-element.46.refs_3_, ...), custom_call_target="tpu_custom_call" | custom-call | tf_op jit(solution)/shard_map/lay_out/pallas_call | solution.py:370
  29.9 0.0 collective-permute-done.11.refs_0_
  29.9 0.9 %collective-permute-done.12.refs_1_ = f32[64,128]{1,0:T(8,128)S(1)} collective-permute-done((f32[64,128]{1,0:T(8,128)S(1)}, f32[64,128]{1,0:T(8,128)S(1)}, u32[]{:S(2)}, u32[]{:S(2)}) %collective-permute-start.12) | collective-permute-done | bytes 32800 | tf_op jit(solution)/shard_map/ppermute | solution.py:457
  30.8 0.6 %collective-permute-done.13.refs_2_ = f32[64,128]{1,0:T(8,128)S(1)} collective-permute-done((f32[64,128]{1,0:T(8,128)S(1)}, f32[64,128]{1,0:T(8,128)S(1)}, u32[]{:S(2)}, u32[]{:S(2)}) %collective-permute-start.13) | collective-permute-done | bytes 32800 | tf_op jit(solution)/shard_map/ppermute | solution.py:457
  31.4 0.6 %enter.1 = (bf16[128,4096]{1,0:T(8,128)(2,1)S(1)}, f32[128,128]{1,0:T(8,128)S(1)}) custom-call(f32[32,128,128]{2,1,0:T(8,128)S(1)} %get-tuple-element.61.state_ref, f32[32,128,128]{2,1,0:T(8,128)S(1)} %get-tuple-element.62.prod_ref, f32[64,128]{1,0:T(8,128)S(1)} %collective-permute-done.11.refs_0_, f32[64,128]{1,0:T(8,128)S(1)} %collective-permute-done.12.refs_1_, ...), custom_call_target="tpu_custom_call" | custom-call | tf_op jit(solution)/shard_map/enter/pallas_call | solution.py:412
  32.0 0.1 collective-permute-done.14.target_ref
  32.1 1.5 %losses.1 = (bf16[1,128,4096]{2,1,0:T(8,128)(2,1)}, f32[1,128]{1,0:T(1,128)}) custom-call(bf16[128,4096]{1,0:T(8,128)(2,1)S(1)} %get-tuple-element.64.rows_ref, f32[128,128]{1,0:T(8,128)S(1)} %get-tuple-element.65.scale_ref, bf16[1,128,4096]{2,1,0:T(8,128)(2,1)S(1)} %collective-permute-done.14.target_ref), custom_call_target="tpu_custom_call" | custom-call | tf_op jit(solution)/shard_map/losses/pallas_call | solution.py:443
Async XLA Ops:
  0.6 19.9 %copy-start.1 = (bf16[8,2,128,128]{3,2,1,0:T(8,128)(2,1)S(1)}, bf16[8,2,128,128]{3,2,1,0:T(8,128)(2,1)}, u32[]{:S(2)}) copy-start(bf16[8,2,128,128]{3,2,1,0:T(8,128)(2,1)} %refs_0_.3) | copy-start | bytes 1572868
  0.6 13.6 %copy-start = (bf16[1,128,4096]{2,1,0:T(8,128)(2,1)S(1)}, bf16[1,128,4096]{2,1,0:T(8,128)(2,1)}, u32[]{:S(2)}) copy-start(bf16[1,128,4096]{2,1,0:T(8,128)(2,1)} %x_ref.3) | copy-start | bytes 3145732
  0.7 19.9 %copy-start.3 = (f32[4096]{0:T(1024)S(1)}, f32[4096]{0:T(1024)}, u32[]{:S(2)}) copy-start(f32[4096]{0:T(1024)} %param.15) | copy-start | bytes 49156
  0.7 19.9 %copy-start.2 = (f32[2,4096]{1,0:T(2,128)S(1)}, f32[2,4096]{1,0:T(2,128)}, u32[]{:S(2)}) copy-start(f32[2,4096]{1,0:T(2,128)} %bias_ref.7) | copy-start | bytes 98308
  1.9 10.5 %collective-permute-start.1 = (bf16[2,2,128,128]{3,2,1,0:T(8,128)(2,1)S(1)}, bf16[2,2,128,128]{3,2,1,0:T(8,128)(2,1)S(1)}, u32[]{:S(2)}, u32[]{:S(2)}) collective-permute-start(bf16[2,2,128,128]{3,2,1,0:T(8,128)(2,1)S(1)} %get-tuple-element.43), channel_id=1, source_target_pairs={{0,8},{4,12},{8,0},{12,4},{1,9},{5,13},{9,1},{13,5},{2,10},{6,14},... | collective-permute-start | bytes 393224 | tf_op jit(solution)/shard_map/ppermute | solution.py:457
  6.0 15.1 %collective-permute-start.5 = (bf16[4,2,128,128]{3,2,1,0:T(8,128)(2,1)S(1)}, bf16[4,2,128,128]{3,2,1,0:T(8,128)(2,1)S(1)}, u32[]{:S(2)}, u32[]{:S(2)}) collective-permute-start(bf16[4,2,128,128]{3,2,1,0:T(8,128)(2,1)S(1)} %get-tuple-element.49), channel_id=1, source_target_pairs={{0,4},{4,0},{8,12},{12,8},{1,5},{5,1},{9,13},{13,9},{2,6},{6,2},{1... | collective-permute-start | bytes 786440 | tf_op jit(solution)/shard_map/ppermute | solution.py:457
  7.6 24.5 %collective-permute-start.14 = (bf16[1,128,4096]{2,1,0:T(8,128)(2,1)}, bf16[1,128,4096]{2,1,0:T(8,128)(2,1)S(1)}, u32[]{:S(2)}, u32[]{:S(2)}) collective-permute-start(bf16[1,128,4096]{2,1,0:T(8,128)(2,1)} %param.10), channel_id=1, source_target_pairs={{0,16},{16,0},{1,17},{17,1},{2,18},{18,2},{3,19},{19,3},{4,20},{20... | collective-permute-start | bytes 3145736 | tf_op jit(solution)/shard_map/ppermute | solution.py:457
  9.1 5.1 %collective-permute-start = (bf16[16,4096]{1,0:T(8,128)(2,1)S(1)}, bf16[16,4096]{1,0:T(8,128)(2,1)S(1)}, u32[]{:S(2)}, u32[]{:S(2)}) collective-permute-start(bf16[16,4096]{1,0:T(8,128)(2,1)S(1)} %get-tuple-element.34), channel_id=1, source_target_pairs={{0,1},{1,2},{2,3},{4,5},{5,6},{6,7},{8,9},{9,10},{10,11},{12,13},{... | collective-permute-start | bytes 393224 | tf_op jit(solution)/shard_map/ppermute | solution.py:42
  10.4 7.8 %collective-permute-start.7 = (bf16[2,2,128,128]{3,2,1,0:T(8,128)(2,1)S(1)}, bf16[2,2,128,128]{3,2,1,0:T(8,128)(2,1)S(1)}, u32[]{:S(2)}, u32[]{:S(2)}) collective-permute-start(bf16[2,2,128,128]{3,2,1,0:T(8,128)(2,1)S(1)} %get-tuple-element.43), channel_id=1, source_target_pairs={{0,12},{4,8},{8,4},{12,0},{1,13},{5,9},{9,5},{13,1},{2,14},{6,10},... | collective-permute-start | bytes 393224 | tf_op jit(solution)/shard_map/ppermute | solution.py:457
  12.4 8.7 %collective-permute-start.2 = (bf16[2,2,128,128]{3,2,1,0:T(8,128)(2,1)S(1)}, bf16[2,2,128,128]{3,2,1,0:T(8,128)(2,1)S(1)}, u32[]{:S(2)}, u32[]{:S(2)}) collective-permute-start(bf16[2,2,128,128]{3,2,1,0:T(8,128)(2,1)S(1)} %collective-permute-done.1.refs_0_), channel_id=1, source_target_pairs={{0,2},{1,3},{2,0},{3,1},{4,6},{5,7},{6,4},{7,5},{8,10},{9,11},{10,... | collective-permute-start | bytes 393224 | tf_op jit(solution)/shard_map/ppermute | solution.py:457
  18.2 6.1 %collective-permute-start.8 = (bf16[2,2,128,128]{3,2,1,0:T(8,128)(2,1)S(1)}, bf16[2,2,128,128]{3,2,1,0:T(8,128)(2,1)S(1)}, u32[]{:S(2)}, u32[]{:S(2)}) collective-permute-start(bf16[2,2,128,128]{3,2,1,0:T(8,128)(2,1)S(1)} %collective-permute-done.7.refs_0_), channel_id=1, source_target_pairs={{0,2},{1,3},{2,0},{3,1},{4,6},{5,7},{6,4},{7,5},{8,10},{9,11},{10,... | collective-permute-start | bytes 393224 | tf_op jit(solution)/shard_map/ppermute | solution.py:457
  21.2 4.3 %collective-permute-start.6 = (bf16[4,2,128,128]{3,2,1,0:T(8,128)(2,1)S(1)}, bf16[4,2,128,128]{3,2,1,0:T(8,128)(2,1)S(1)}, u32[]{:S(2)}, u32[]{:S(2)}) collective-permute-start(bf16[4,2,128,128]{3,2,1,0:T(8,128)(2,1)S(1)} %collective-permute-done.5.refs_0_), channel_id=1, source_target_pairs={{0,1},{1,0},{2,3},{3,2},{4,5},{5,4},{6,7},{7,6},{8,9},{9,8},{10,11... | collective-permute-start | bytes 786440 | tf_op jit(solution)/shard_map/ppermute | solution.py:457
  21.3 3.1 %collective-permute-start.3 = (bf16[2,2,128,128]{3,2,1,0:T(8,128)(2,1)S(1)}, bf16[2,2,128,128]{3,2,1,0:T(8,128)(2,1)S(1)}, u32[]{:S(2)}, u32[]{:S(2)}) collective-permute-start(bf16[2,2,128,128]{3,2,1,0:T(8,128)(2,1)S(1)} %collective-permute-done.1.refs_0_), channel_id=1, source_target_pairs={{0,1},{1,0},{2,3},{3,2},{4,5},{5,4},{6,7},{7,6},{8,9},{9,8},{10,11... | collective-permute-start | bytes 393224 | tf_op jit(solution)/shard_map/ppermute | solution.py:457
  21.8 3.1 %collective-permute-start.4 = (bf16[2,2,128,128]{3,2,1,0:T(8,128)(2,1)S(1)}, bf16[2,2,128,128]{3,2,1,0:T(8,128)(2,1)S(1)}, u32[]{:S(2)}, u32[]{:S(2)}) collective-permute-start(bf16[2,2,128,128]{3,2,1,0:T(8,128)(2,1)S(1)} %collective-permute-done.2.refs_2_), channel_id=1, source_target_pairs={{0,1},{1,0},{2,3},{3,2},{4,5},{5,4},{6,7},{7,6},{8,9},{9,8},{10,11... | collective-permute-start | bytes 393224 | tf_op jit(solution)/shard_map/ppermute | solution.py:457
  24.4 1.7 %collective-permute-start.9 = (bf16[2,2,128,128]{3,2,1,0:T(8,128)(2,1)S(1)}, bf16[2,2,128,128]{3,2,1,0:T(8,128)(2,1)S(1)}, u32[]{:S(2)}, u32[]{:S(2)}) collective-permute-start(bf16[2,2,128,128]{3,2,1,0:T(8,128)(2,1)S(1)} %collective-permute-done.7.refs_0_), channel_id=1, source_target_pairs={{0,1},{1,0},{2,3},{3,2},{4,5},{5,4},{6,7},{7,6},{8,9},{9,8},{10,11... | collective-permute-start | bytes 393224 | tf_op jit(solution)/shard_map/ppermute | solution.py:457
  24.4 1.8 %collective-permute-start.10 = (bf16[2,2,128,128]{3,2,1,0:T(8,128)(2,1)S(1)}, bf16[2,2,128,128]{3,2,1,0:T(8,128)(2,1)S(1)}, u32[]{:S(2)}, u32[]{:S(2)}) collective-permute-start(bf16[2,2,128,128]{3,2,1,0:T(8,128)(2,1)S(1)} %collective-permute-done.8.refs_2_), channel_id=1, source_target_pairs={{0,1},{1,0},{2,3},{3,2},{4,5},{5,4},{6,7},{7,6},{8,9},{9,8},{10,11... | collective-permute-start | bytes 393224 | tf_op jit(solution)/shard_map/ppermute | solution.py:457
  26.8 3.2 %collective-permute-start.11 = (f32[64,128]{1,0:T(8,128)S(1)}, f32[64,128]{1,0:T(8,128)S(1)}, u32[]{:S(2)}, u32[]{:S(2)}) collective-permute-start(f32[64,128]{1,0:T(8,128)S(1)} %get-tuple-element.63), channel_id=1, source_target_pairs={{0,1},{1,0},{2,3},{3,2},{4,5},{5,4},{6,7},{7,6},{8,9},{9,8},{10,11... | collective-permute-start | bytes 98312 | tf_op jit(solution)/shard_map/ppermute | solution.py:457
  26.9 3.9 %collective-permute-start.12 = (f32[64,128]{1,0:T(8,128)S(1)}, f32[64,128]{1,0:T(8,128)S(1)}, u32[]{:S(2)}, u32[]{:S(2)}) collective-permute-start(f32[64,128]{1,0:T(8,128)S(1)} %get-tuple-element.63), channel_id=1, source_target_pairs={{0,2},{1,3},{2,0},{3,1},{4,6},{5,7},{6,4},{7,5},{8,10},{9,11},{10,... | collective-permute-start | bytes 98312 | tf_op jit(solution)/shard_map/ppermute | solution.py:457
  28.0 3.4 %collective-permute-start.13 = (f32[64,128]{1,0:T(8,128)S(1)}, f32[64,128]{1,0:T(8,128)S(1)}, u32[]{:S(2)}, u32[]{:S(2)}) collective-permute-start(f32[64,128]{1,0:T(8,128)S(1)} %get-tuple-element.63), channel_id=1, source_target_pairs={{0,3},{1,2},{2,1},{3,0},{4,7},{5,6},{6,5},{7,4},{8,11},{9,10},{10,... | collective-permute-start | bytes 98312 | tf_op jit(solution)/shard_map/ppermute | solution.py:457

commit v6 on v4

--- a/solution.py
+++ b/solution.py
@@ -149,16 +149,39 @@
     )
 
 
-def cut_kernel(x_ref, w_ref, half_ref, quarter_ref, edge_ref, sem):
-    here = lax.axis_index("seq")
+def cut_kernel(w_ref, quarter_ref, sem):
+    quarters = quarter_ref.shape[0]
+    first = lax.axis_index("seq") * quarters
+    copy = pltpu.make_async_copy(w_ref.at[pl.ds(first, quarters)], quarter_ref, sem)
+    copy.start()
+    copy.wait()
+
+
+def cut(gate_weights):
+    return pallas(
+        cut_kernel,
+        "cut",
+        jax.ShapeDtypeStruct((gate_weights.shape[0] // 4,) + gate_weights.shape[1:], jnp.bfloat16),
+        [pl.BlockSpec(memory_space=pltpu.HBM)],
+        pl.BlockSpec(memory_space=pl.ANY),
+        [pltpu.SemaphoreType.DMA],
+    )(pltpu.with_memory_space_constraint(gate_weights, pltpu.HBM))
+
+
+def fetch_kernel(x_ref, w_ref, *refs):
+    small, refs = refs[: len(refs) // 2 - 1], refs[len(refs) // 2 - 1 :]
+    half_ref, edge_ref, *near, sem = refs
     tokens = x_ref.shape[1]
-    halves, quarters = half_ref.shape[0], quarter_ref.shape[0]
+    halves = half_ref.shape[0]
+    first = lax.rem(lax.axis_index("seq"), 2) * halves
+    pairs = [
+        (w_ref.at[pl.ds(first, halves)], half_ref),
+        (x_ref.at[0, pl.ds(tokens - EDGE, EDGE), :], edge_ref),
+        *zip(small, near),
+    ]
     copies = [
-        pltpu.make_async_copy(
-            w_ref.at[pl.ds(lax.rem(here, 2) * halves, halves)], half_ref, sem.at[0]
-        ),
-        pltpu.make_async_copy(w_ref.at[pl.ds(here * quarters, quarters)], quarter_ref, sem.at[1]),
-        pltpu.make_async_copy(x_ref.at[0, pl.ds(tokens - EDGE, EDGE), :], edge_ref, sem.at[2]),
+        pltpu.make_async_copy(source, target, sem.at[index])
+        for index, (source, target) in enumerate(pairs)
     ]
     for copy in copies:
         copy.start()
@@ -166,23 +189,25 @@
         copy.wait()
 
 
-def cut(branch_x, gate_weights):
+def fetch(branch_x, gate_weights, *small):
     held = gate_weights.shape[0]
-    rest = gate_weights.shape[1:]
     return pallas(
-        cut_kernel,
-        "cut",
+        fetch_kernel,
+        "fetch",
         [
-            jax.ShapeDtypeStruct((held // 2,) + rest, jnp.bfloat16),
-            jax.ShapeDtypeStruct((held // 4,) + rest, jnp.bfloat16),
+            jax.ShapeDtypeStruct((held // 2,) + gate_weights.shape[1:], jnp.bfloat16),
             jax.ShapeDtypeStruct((EDGE, branch_x.shape[2]), jnp.bfloat16),
-        ],
-        [pl.BlockSpec(memory_space=pltpu.HBM)] * 2,
-        [pl.BlockSpec(memory_space=pl.ANY)] * 3,
-        [pltpu.SemaphoreType.DMA((3,))],
+        ]
+        + [jax.ShapeDtypeStruct(value.shape, value.dtype) for value in small],
+        [pl.BlockSpec(memory_space=pltpu.HBM)] * (2 + len(small)),
+        [pl.BlockSpec(memory_space=pl.ANY)] * (2 + len(small)),
+        [pltpu.SemaphoreType.DMA((2 + len(small),))],
+        1500000000,
     )(
-        pltpu.with_memory_space_constraint(branch_x, pltpu.HBM),
-        pltpu.with_memory_space_constraint(gate_weights, pltpu.HBM),
+        *[
+            pltpu.with_memory_space_constraint(value, pltpu.HBM)
+            for value in (branch_x, gate_weights, *small)
+        ]
     )
 
 
@@ -336,7 +361,7 @@
         in_vmem(4 + len(weights) + len(before)),
         in_vmem(4),
         [],
-        5500000000 if before else 0,
+        5000000000 if before else 0,
     )(conv, masks, *params, *weights, *before)
 
 
@@ -370,18 +395,19 @@
     )(*flat)
 
 
+ROWS = 64
+
+
 def final_kernel(pairs, target_ref, state_ref, prod_ref, *refs):
     devices = lax.axis_size("seq")
     here = lax.axis_index("seq")
-    ends, (student_ref, loss_ref, ends_s, held, sem) = refs[: devices - 1], refs[devices - 1 :]
-    tokens = state_ref.shape[1]
+    ends, refs = refs[: devices - 1], refs[devices - 1 :]
+    student_ref, loss_ref, ends_s, rows, sem = refs
+    tokens, full = rows.shape
     heads = state_ref.shape[0] // len(pairs)
-    width = heads * HS
     for apart in range(1, devices):
         ends_s[lax.bitwise_xor(here, apart)] = ends[apart - 1][...]
-    squares = jnp.zeros((tokens, HS), jnp.float32)
-    copies = []
-    bases = []
+    places = []
     for slot, pair in enumerate(pairs):
         incoming = jnp.zeros((heads, HS), jnp.float32)
         row = 2 * heads * slot
@@ -391,25 +417,33 @@
             )
             incoming = jnp.where(place < here, after, incoming)
         base = lax.bitwise_xor(lax.axis_index("fsdp"), pair) * heads
-        bases.append(base)
         for head in range(heads):
-            at_head = slot * heads + head
-            rounded = (
-                state_ref[at_head] + prod_ref[at_head] * incoming[head : head + 1]
-            ).astype(jnp.bfloat16)
-            student_ref[0, :, lanes_of(base + head)] = rounded
+            places.append((slot * heads + head, lanes_of(base + head), incoming[head : head + 1]))
+    copies, totals = [], []
+    for block in range(0, tokens, ROWS):
+        at = pl.ds(block, ROWS)
+        squares = jnp.zeros((ROWS, HS), jnp.float32)
+        for index, lanes, entering in places:
+            rounded = (state_ref[index, at, :] + prod_ref[index, at, :] * entering).astype(
+                jnp.bfloat16
+            )
+            rows[at, lanes] = rounded
             value = rounded.astype(jnp.float32)
             squares = squares + value * value
-    full = student_ref.shape[2]
-    mean = jnp.sum(squares, axis=1, keepdims=True) * (1.0 / full)
-    scale = jnp.broadcast_to(lax.rsqrt(mean + 1e-06), (tokens, HS))
-    total = jnp.zeros((tokens, HS), jnp.float32)
-    for slot, base in enumerate(bases):
-        for head in range(heads):
-            at_head = slot * heads + head
-            value = student_ref[0, :, lanes_of(base + head)].astype(jnp.float32)
-            off = value * scale - target_ref[0, :, lanes_of(base + head)].astype(jnp.float32)
+        copies.append(
+            pltpu.make_async_copy(rows.at[at, :], student_ref.at[0, at, :], sem.at[len(copies)])
+        )
+        copies[-1].start()
+        mean = jnp.sum(squares, axis=1, keepdims=True) * (1.0 / full)
+        scale = jnp.broadcast_to(lax.rsqrt(mean + 1e-06), (ROWS, HS))
+        total = jnp.zeros((ROWS, HS), jnp.float32)
+        for start in range(0, full, HS):
+            lanes = slice(start, start + HS)
+            wanted = target_ref[0, at, lanes].astype(jnp.float32)
+            off = rows[at, lanes].astype(jnp.float32) * scale - wanted
             total = total + off * off
+        totals.append(total)
+    total = jnp.concatenate(totals, axis=0)
     loss_ref[...] = jnp.sum(total.T, axis=0, keepdims=True) * (1.0 / full)
     for copy in copies:
         copy.wait()
@@ -426,11 +460,11 @@
             jax.ShapeDtypeStruct((1, tokens), jnp.float32),
         ],
         in_vmem(3 + len(ends)),
-        in_vmem(2),
+        [pl.BlockSpec(memory_space=pltpu.HBM)] + in_vmem(1),
         [
             pltpu.VMEM((len(ends) + 1,) + ends[0].shape, jnp.float32),
             pltpu.VMEM((tokens, full), jnp.bfloat16),
-            pltpu.SemaphoreType.DMA((len(pairs),)),
+            pltpu.SemaphoreType.DMA((tokens // ROWS,)),
         ],
     )(target, states, products, *ends)
 
@@ -449,11 +483,14 @@
     tokens, width = branch_x.shape[1:]
     total = lax.axis_size("seq") * tokens
     target = swap(teacher_held, "segment", 1)
-    half, quarter, edge = cut(branch_x, gate_weights)
+    quarter = cut(gate_weights)
+    half, edge, *small = fetch(
+        branch_x, gate_weights, positions, conv_weight, conv_bias.reshape(1, width)
+    )
     quarters = {pair: swap(quarter, "fsdp", pair) for pair in (2, 3)}
     half = swap(half, "fsdp", 1)
     edge = from_behind(edge, "seq", 1)
-    conv, masks = conv_rows(branch_x, edge, positions, conv_weight, conv_bias.reshape(1, width))
+    conv, masks = conv_rows(branch_x, edge, *small)
     params = (gate_bias, decay_rate.reshape(1, width))
     parts = [shard(conv, masks, params, 0, [gate_weights], total)]
     two = swap(quarters[2], "seq", 2)

time: 34.5 us -> 33.6 us (0.974)
  local copies, waits for them, and re-layouts: 2.23 us -> 0.01 us
  waiting for transfers between devices: 6.01 us -> 7.68 us
  starting transfers between devices: 16.4 us -> 15.5 us
  Pallas kernels: 8.78 us -> 9.47 us
    unnamed x14 -> x8, local copies, waits for them, and re-layouts: 2.23 us -> 0.01 us
    ppermute x14, waiting for transfers between devices: 6.01 us -> 7.67 us  [swap(): lax.ppermute(value, axis, [(i, i ^ apart) for i in range(lax.axis_size(ax...]
    ppermute x14, starting transfers between devices: 15.1 us -> 14.2 us  [swap(): lax.ppermute(value, axis, [(i, i ^ apart) for i in range(lax.axis_size(ax...]
    pallas_call x1 -> x2, Pallas kernels: 1.19 us -> 2.09 us  [the longest x1 1.17 us: fetch(): pallas(fetch_kernel, 'fetch', [jax.ShapeDtypeStruct((held // 2,) + gate_w...]
  transfers between devices with their start and end apart: 15 -> 15, of which waited for: 5 -> 4; matrix products, arithmetic and copies ran while one was open for 0% -> 0% of each run, Pallas kernels for 16% -> 20%
where the time goes in v6:
time: 33.6 us; the launch traced here: 33.4 us
  starting transfers between devices  15.5 us (46%)
  Pallas kernels  9.47 us (28%)
  waiting for transfers between devices  7.68 us (23%)
  between operations  0.76 us (2%)
    ppermute x14, starting transfers between devices, swap(): lax.ppermute(value, axis, [(i, i ^ apart) for i in range(lax.axis_size(ax...  14.2 us
    ppermute x14, waiting for transfers between devices, swap(): lax.ppermute(value, axis, [(i, i ^ apart) for i in range(lax.axis_size(ax...  7.67 us
    pallas_call x4, Pallas kernels, shard(): pallas(functools.partial(shard_kernel, total, pair, counts), 'shard', [ja...  2.42 us
    pallas_call x1, Pallas kernels, conv_rows(): pallas(conv_kernel, 'conv_rows', [jax.ShapeDtypeStruct((heads, tokens, HS...  1.92 us
    pallas_call x1, Pallas kernels, final(): pallas(functools.partial(final_kernel, pairs), 'final', [jax.ShapeDtypeSt...  1.81 us
    ppermute x1, starting transfers between devices, from_behind(): lax.ppermute(value, axis, [(source, source + steps) for source in range(l...  1.29 us
    pallas_call x1, Pallas kernels, lay_out(): pallas(lay_kernel, 'lay_out', [whole, whole], in_vmem(len(flat)), in_vmem...  1.23 us
    pallas_call x1, Pallas kernels, fetch(): pallas(fetch_kernel, 'fetch', [jax.ShapeDtypeStruct((held // 2,) + gate_w...  1.17 us
  transfers between devices with their start and end apart: 15, of which 4 were waited for; matrix products, arithmetic and copies ran while one was open for 0% of the time, Pallas kernels for 20%

profile of v6, /device:TPU:0, one launch (start us, length us, event | category | flops | bytes accessed | tf_op | source)
XLA Modules:
  0.0 33.4 jit_solution(16665708402664824449)
XLA Ops:
  0.6 0.9 %cut.1 = bf16[2,2,128,128]{3,2,1,0:T(8,128)(2,1)S(1)} custom-call(bf16[8,2,128,128]{3,2,1,0:T(8,128)(2,1)} %w_ref.3), custom_call_target="tpu_custom_call" | custom-call | tf_op jit(solution)/shard_map/cut/pallas_call | solution.py:161
  1.6 4.1 %collective-permute-start.2 = (bf16[2,2,128,128]{3,2,1,0:T(8,128)(2,1)S(1)}, bf16[2,2,128,128]{3,2,1,0:T(8,128)(2,1)S(1)}, u32[]{:S(2)}, u32[]{:S(2)}) collective-permute-start(bf16[2,2,128,128]{3,2,1,0:T(8,128)(2,1)S(1)} %cut.1), channel_id=1, source_target_pairs={{0,8},{4,12},{8,0},{12,4},{1,9},{5,13},{9,1},{13,5},{2,10},{6,14},... | collective-permute-start | bytes 393224 | tf_op jit(solution)/shard_map/ppermute | solution.py:473
  5.7 1.5 %collective-permute-start = (bf16[1,128,4096]{2,1,0:T(8,128)(2,1)}, bf16[1,128,4096]{2,1,0:T(8,128)(2,1)S(1)}, u32[]{:S(2)}, u32[]{:S(2)}) collective-permute-start(bf16[1,128,4096]{2,1,0:T(8,128)(2,1)} %param.10), channel_id=1, source_target_pairs={{0,16},{16,0},{1,17},{17,1},{2,18},{18,2},{3,19},{19,3},{4,20},{20... | collective-permute-start | bytes 3145736 | tf_op jit(solution)/shard_map/ppermute | solution.py:473
  7.2 0.0 copy-start.1
  7.2 0.0 copy-start
  7.2 0.0 copy-start.2
  7.2 0.0 copy-start.3
  7.2 1.2 %fetch.1 = (bf16[4,2,128,128]{3,2,1,0:T(8,128)(2,1)S(1)}, bf16[16,4096]{1,0:T(8,128)(2,1)S(1)}, s32[1,128]{1,0:T(1,128)S(1)}, f32[4,4096]{1,0:T(4,128)S(1)}, f32[1,4096]{1,0:T(1,128)S(1)}) custom-call(bf16[1,128,4096]{2,1,0:T(8,128)(2,1)} %x_ref.3, bf16[8,2,128,128]{3,2,1,0:T(8,128)(2,1)} %w_ref.3, s32[1,128]{1,0:T(1,128)} %refs_0_.2, f32[4,4096]{1,0:T(4,128)} %refs_1_.1, ...), custom_call_target="tpu_custom_call" | custom-call | flops 1500000000 | tf_op jit(solution)/shard_map/fetch/pallas_call | solution.py:194
  8.4 1.6 %collective-permute-start.6 = (bf16[4,2,128,128]{3,2,1,0:T(8,128)(2,1)S(1)}, bf16[4,2,128,128]{3,2,1,0:T(8,128)(2,1)S(1)}, u32[]{:S(2)}, u32[]{:S(2)}) collective-permute-start(bf16[4,2,128,128]{3,2,1,0:T(8,128)(2,1)S(1)} %get-tuple-element.45), channel_id=1, source_target_pairs={{0,4},{4,0},{8,12},{12,8},{1,5},{5,1},{9,13},{13,9},{2,6},{6,2},{1... | collective-permute-start | bytes 786440 | tf_op jit(solution)/shard_map/ppermute | solution.py:473
  10.0 1.3 %collective-permute-start.1 = (bf16[16,4096]{1,0:T(8,128)(2,1)S(1)}, bf16[16,4096]{1,0:T(8,128)(2,1)S(1)}, u32[]{:S(2)}, u32[]{:S(2)}) collective-permute-start(bf16[16,4096]{1,0:T(8,128)(2,1)S(1)} %get-tuple-element.31), channel_id=1, source_target_pairs={{0,1},{1,2},{2,3},{4,5},{5,6},{6,7},{8,9},{9,10},{10,11},{12,13},{... | collective-permute-start | bytes 393224 | tf_op jit(solution)/shard_map/ppermute | solution.py:42
  11.3 0.3 collective-permute-start.8
  11.6 0.5 %collective-permute-done.2.refs_0_ = bf16[2,2,128,128]{3,2,1,0:T(8,128)(2,1)S(1)} collective-permute-done((bf16[2,2,128,128]{3,2,1,0:T(8,128)(2,1)S(1)}, bf16[2,2,128,128]{3,2,1,0:T(8,128)(2,1)S(1)}, u32[]{:S(2)}, u32[]{:S(2)}) %collective-permute-start.2) | collective-permute-done | bytes 131104 | tf_op jit(solution)/shard_map/ppermute | solution.py:473
  12.1 1.6 %collective-permute-start.3 = (bf16[2,2,128,128]{3,2,1,0:T(8,128)(2,1)S(1)}, bf16[2,2,128,128]{3,2,1,0:T(8,128)(2,1)S(1)}, u32[]{:S(2)}, u32[]{:S(2)}) collective-permute-start(bf16[2,2,128,128]{3,2,1,0:T(8,128)(2,1)S(1)} %collective-permute-done.2.refs_0_), channel_id=1, source_target_pairs={{0,2},{1,3},{2,0},{3,1},{4,6},{5,7},{6,4},{7,5},{8,10},{9,11},{10,... | collective-permute-start | bytes 393224 | tf_op jit(solution)/shard_map/ppermute | solution.py:473
  13.7 0.0 collective-permute-done.1.edge_ref
  13.7 0.0 copy-done.1
  13.7 1.9 %conv_rows.1 = (bf16[32,128,128]{2,1,0:T(8,128)(2,1)S(1)}, f32[2,128,128]{2,1,0:T(8,128)S(1)}) custom-call(bf16[1,128,4096]{2,1,0:T(8,128)(2,1)S(1)} %copy-done.1, bf16[16,4096]{1,0:T(8,128)(2,1)S(1)} %collective-permute-done.1.edge_ref, s32[1,128]{1,0:T(1,128)S(1)} %get-tuple-element.32.pos_ref, f32[4,4096]{1,0:T(4,128)S(1)} %get-tuple-element.33.w_ref, ...), custom_call_target="tpu_custom_call" | custom-call | tf_op jit(solution)/shard_map/conv_rows/pallas_call | solution.py:264
  15.6 2.8 %collective-permute-done.8.refs_0_ = bf16[2,2,128,128]{3,2,1,0:T(8,128)(2,1)S(1)} collective-permute-done((bf16[2,2,128,128]{3,2,1,0:T(8,128)(2,1)S(1)}, bf16[2,2,128,128]{3,2,1,0:T(8,128)(2,1)S(1)}, u32[]{:S(2)}, u32[]{:S(2)}) %collective-permute-start.8) | collective-permute-done | bytes 131104 | tf_op jit(solution)/shard_map/ppermute | solution.py:473
  18.5 1.9 %collective-permute-start.9 = (bf16[2,2,128,128]{3,2,1,0:T(8,128)(2,1)S(1)}, bf16[2,2,128,128]{3,2,1,0:T(8,128)(2,1)S(1)}, u32[]{:S(2)}, u32[]{:S(2)}) collective-permute-start(bf16[2,2,128,128]{3,2,1,0:T(8,128)(2,1)S(1)} %collective-permute-done.8.refs_0_), channel_id=1, source_target_pairs={{0,2},{1,3},{2,0},{3,1},{4,6},{5,7},{6,4},{7,5},{8,10},{9,11},{10,... | collective-permute-start | bytes 393224 | tf_op jit(solution)/shard_map/ppermute | solution.py:473
  20.4 0.0 copy-done
  20.4 0.0 copy-done.2
  20.4 0.0 copy-done.3
  20.4 0.6 %shard.4 = (f32[8,128,128]{2,1,0:T(8,128)S(1)}, f32[8,128,128]{2,1,0:T(8,128)S(1)}, f32[8,2,8,128]{3,2,1,0:T(8,128)S(1)}, f32[16,128]{1,0:T(8,128)S(1)}) custom-call(bf16[32,128,128]{2,1,0:T(8,128)(2,1)S(1)} %get-tuple-element.35.conv_ref, f32[2,128,128]{2,1,0:T(8,128)S(1)} %get-tuple-element.36.mask_ref, f32[2,4096]{1,0:T(2,128)S(1)} %copy-done.2, ...), custom_call_target="tpu_custom_call" | custom-call | tf_op jit(solution)/shard_map/shard/pallas_call | solution.py:352
  21.0 0.0 collective-permute-done.3.refs_2_
  21.0 0.0 collective-permute-done.6.refs_0_
  21.0 0.1 collective-permute-start.7
  21.1 0.5 %collective-permute-start.4 = (bf16[2,2,128,128]{3,2,1,0:T(8,128)(2,1)S(1)}, bf16[2,2,128,128]{3,2,1,0:T(8,128)(2,1)S(1)}, u32[]{:S(2)}, u32[]{:S(2)}) collective-permute-start(bf16[2,2,128,128]{3,2,1,0:T(8,128)(2,1)S(1)} %collective-permute-done.2.refs_0_), channel_id=1, source_target_pairs={{0,1},{1,0},{2,3},{3,2},{4,5},{5,4},{6,7},{7,6},{8,9},{9,8},{10,11... | collective-permute-start | bytes 393224 | tf_op jit(solution)/shard_map/ppermute | solution.py:473
  21.6 0.1 collective-permute-start.5
  21.7 3.1 %collective-permute-done.9.refs_2_ = bf16[2,2,128,128]{3,2,1,0:T(8,128)(2,1)S(1)} collective-permute-done((bf16[2,2,128,128]{3,2,1,0:T(8,128)(2,1)S(1)}, bf16[2,2,128,128]{3,2,1,0:T(8,128)(2,1)S(1)}, u32[]{:S(2)}, u32[]{:S(2)}) %collective-permute-start.9) | collective-permute-done | bytes 131104 | tf_op jit(solution)/shard_map/ppermute | solution.py:473
  24.7 0.2 collective-permute-start.10
  24.9 0.0 collective-permute-done.4.refs_1_
  24.9 0.3 collective-permute-start.11
  25.2 0.0 collective-permute-done.5.refs_3_
  25.2 0.6 %shard.5 = (f32[8,128,128]{2,1,0:T(8,128)S(1)}, f32[8,128,128]{2,1,0:T(8,128)S(1)}, f32[8,2,8,128]{3,2,1,0:T(8,128)S(1)}, f32[16,128]{1,0:T(8,128)S(1)}) custom-call(bf16[32,128,128]{2,1,0:T(8,128)(2,1)S(1)} %get-tuple-element.35.conv_ref, f32[2,128,128]{2,1,0:T(8,128)S(1)} %get-tuple-element.36.mask_ref, f32[2,4096]{1,0:T(2,128)S(1)} %copy-done.2, ...), custom_call_target="tpu_custom_call" | custom-call | tf_op jit(solution)/shard_map/shard/pallas_call | solution.py:352
  25.9 0.0 collective-permute-done.7.refs_1_
  25.9 0.6 %shard.6 = (f32[8,128,128]{2,1,0:T(8,128)S(1)}, f32[8,128,128]{2,1,0:T(8,128)S(1)}, f32[8,2,8,128]{3,2,1,0:T(8,128)S(1)}, f32[16,128]{1,0:T(8,128)S(1)}) custom-call(bf16[32,128,128]{2,1,0:T(8,128)(2,1)S(1)} %get-tuple-element.35.conv_ref, f32[2,128,128]{2,1,0:T(8,128)S(1)} %get-tuple-element.36.mask_ref, f32[2,4096]{1,0:T(2,128)S(1)} %copy-done.2, ...), custom_call_target="tpu_custom_call" | custom-call | tf_op jit(solution)/shard_map/shard/pallas_call | solution.py:352
  26.5 0.0 collective-permute-done.10.refs_1_
  26.5 0.0 collective-permute-done.11.refs_3_
  26.5 0.6 %shard.7 = (f32[8,128,128]{2,1,0:T(8,128)S(1)}, f32[8,128,128]{2,1,0:T(8,128)S(1)}, f32[8,2,8,128]{3,2,1,0:T(8,128)S(1)}, f32[64,128]{1,0:T(8,128)S(1)}) custom-call(bf16[32,128,128]{2,1,0:T(8,128)(2,1)S(1)} %get-tuple-element.35.conv_ref, f32[2,128,128]{2,1,0:T(8,128)S(1)} %get-tuple-element.36.mask_ref, f32[2,4096]{1,0:T(2,128)S(1)} %copy-done.2, ...), custom_call_target="tpu_custom_call" | custom-call | flops 5000000000 | tf_op jit(solution)/shard_map/shard/pallas_call | solution.py:352
  27.1 0.3 collective-permute-start.12
  27.4 0.5 %collective-permute-start.13 = (f32[64,128]{1,0:T(8,128)S(1)}, f32[64,128]{1,0:T(8,128)S(1)}, u32[]{:S(2)}, u32[]{:S(2)}) collective-permute-start(f32[64,128]{1,0:T(8,128)S(1)} %get-tuple-element.59), channel_id=1, source_target_pairs={{0,2},{1,3},{2,0},{3,1},{4,6},{5,7},{6,4},{7,5},{8,10},{9,11},{10,... | collective-permute-start | bytes 98312 | tf_op jit(solution)/shard_map/ppermute | solution.py:473
  27.9 1.2 %collective-permute-start.14 = (f32[64,128]{1,0:T(8,128)S(1)}, f32[64,128]{1,0:T(8,128)S(1)}, u32[]{:S(2)}, u32[]{:S(2)}) collective-permute-start(f32[64,128]{1,0:T(8,128)S(1)} %get-tuple-element.59), channel_id=1, source_target_pairs={{0,3},{1,2},{2,1},{3,0},{4,7},{5,6},{6,5},{7,4},{8,11},{9,10},{10,... | collective-permute-start | bytes 98312 | tf_op jit(solution)/shard_map/ppermute | solution.py:473
  29.0 1.2 %lay_out.1 = (f32[32,128,128]{2,1,0:T(8,128)S(1)}, f32[32,128,128]{2,1,0:T(8,128)S(1)}) custom-call(f32[8,128,128]{2,1,0:T(8,128)S(1)} %get-tuple-element.37.refs_0_, f32[8,128,128]{2,1,0:T(8,128)S(1)} %get-tuple-element.38.refs_1_, f32[8,2,8,128]{3,2,1,0:T(8,128)S(1)} %get-tuple-element.39.refs_2_, f32[8,128,128]{2,1,0:T(8,128)S(1)} %get-tuple-element.42.refs_3_, ...), custom_call_target="tpu_custom_call" | custom-call | tf_op jit(solution)/shard_map/lay_out/pallas_call | solution.py:388
  30.3 0.0 collective-permute-done.12.refs_0_
  30.3 1.3 %collective-permute-done.13.refs_1_ = f32[64,128]{1,0:T(8,128)S(1)} collective-permute-done((f32[64,128]{1,0:T(8,128)S(1)}, f32[64,128]{1,0:T(8,128)S(1)}, u32[]{:S(2)}, u32[]{:S(2)}) %collective-permute-start.13) | collective-permute-done | bytes 32800 | tf_op jit(solution)/shard_map/ppermute | solution.py:473
  31.6 0.0 collective-permute-done.14.refs_2_
  31.6 0.0 collective-permute-done.target_ref
  31.6 1.8 %final.1 = (bf16[1,128,4096]{2,1,0:T(8,128)(2,1)}, f32[1,128]{1,0:T(1,128)}) custom-call(bf16[1,128,4096]{2,1,0:T(8,128)(2,1)S(1)} %collective-permute-done.target_ref, f32[32,128,128]{2,1,0:T(8,128)S(1)} %get-tuple-element.57.state_ref, f32[32,128,128]{2,1,0:T(8,128)S(1)} %get-tuple-element.58.prod_ref, f32[64,128]{1,0:T(8,128)S(1)} %collective-permute-done.12.refs_0_, ...), custom_call_target="tpu_custom_call" | custom-call | tf_op jit(solution)/shard_map/final/pallas_call | solution.py:455
Async XLA Ops:
  1.6 10.5 %collective-permute-start.2 = (bf16[2,2,128,128]{3,2,1,0:T(8,128)(2,1)S(1)}, bf16[2,2,128,128]{3,2,1,0:T(8,128)(2,1)S(1)}, u32[]{:S(2)}, u32[]{:S(2)}) collective-permute-start(bf16[2,2,128,128]{3,2,1,0:T(8,128)(2,1)S(1)} %cut.1), channel_id=1, source_target_pairs={{0,8},{4,12},{8,0},{12,4},{1,9},{5,13},{9,1},{13,5},{2,10},{6,14},... | collective-permute-start | bytes 393224 | tf_op jit(solution)/shard_map/ppermute | solution.py:473
  5.7 25.9 %collective-permute-start = (bf16[1,128,4096]{2,1,0:T(8,128)(2,1)}, bf16[1,128,4096]{2,1,0:T(8,128)(2,1)S(1)}, u32[]{:S(2)}, u32[]{:S(2)}) collective-permute-start(bf16[1,128,4096]{2,1,0:T(8,128)(2,1)} %param.10), channel_id=1, source_target_pairs={{0,16},{16,0},{1,17},{17,1},{2,18},{18,2},{3,19},{19,3},{4,20},{20... | collective-permute-start | bytes 3145736 | tf_op jit(solution)/shard_map/ppermute | solution.py:473
  7.2 6.5 %copy-start.1 = (bf16[1,128,4096]{2,1,0:T(8,128)(2,1)S(1)}, bf16[1,128,4096]{2,1,0:T(8,128)(2,1)}, u32[]{:S(2)}) copy-start(bf16[1,128,4096]{2,1,0:T(8,128)(2,1)} %x_ref.3) | copy-start | bytes 3145732
  7.2 13.2 %copy-start = (bf16[8,2,128,128]{3,2,1,0:T(8,128)(2,1)S(1)}, bf16[8,2,128,128]{3,2,1,0:T(8,128)(2,1)}, u32[]{:S(2)}) copy-start(bf16[8,2,128,128]{3,2,1,0:T(8,128)(2,1)} %w_ref.3) | copy-start | bytes 1572868
  7.2 13.2 %copy-start.2 = (f32[2,4096]{1,0:T(2,128)S(1)}, f32[2,4096]{1,0:T(2,128)}, u32[]{:S(2)}) copy-start(f32[2,4096]{1,0:T(2,128)} %bias_ref.7) | copy-start | bytes 98308
  7.2 13.2 %copy-start.3 = (f32[4096]{0:T(1024)S(1)}, f32[4096]{0:T(1024)}, u32[]{:S(2)}) copy-start(f32[4096]{0:T(1024)} %param.15) | copy-start | bytes 49156
  8.4 12.6 %collective-permute-start.6 = (bf16[4,2,128,128]{3,2,1,0:T(8,128)(2,1)S(1)}, bf16[4,2,128,128]{3,2,1,0:T(8,128)(2,1)S(1)}, u32[]{:S(2)}, u32[]{:S(2)}) collective-permute-start(bf16[4,2,128,128]{3,2,1,0:T(8,128)(2,1)S(1)} %get-tuple-element.45), channel_id=1, source_target_pairs={{0,4},{4,0},{8,12},{12,8},{1,5},{5,1},{9,13},{13,9},{2,6},{6,2},{1... | collective-permute-start | bytes 786440 | tf_op jit(solution)/shard_map/ppermute | solution.py:473
  10.0 3.7 %collective-permute-start.1 = (bf16[16,4096]{1,0:T(8,128)(2,1)S(1)}, bf16[16,4096]{1,0:T(8,128)(2,1)S(1)}, u32[]{:S(2)}, u32[]{:S(2)}) collective-permute-start(bf16[16,4096]{1,0:T(8,128)(2,1)S(1)} %get-tuple-element.31), channel_id=1, source_target_pairs={{0,1},{1,2},{2,3},{4,5},{5,6},{6,7},{8,9},{9,10},{10,11},{12,13},{... | collective-permute-start | bytes 393224 | tf_op jit(solution)/shard_map/ppermute | solution.py:42
  11.3 7.2 %collective-permute-start.8 = (bf16[2,2,128,128]{3,2,1,0:T(8,128)(2,1)S(1)}, bf16[2,2,128,128]{3,2,1,0:T(8,128)(2,1)S(1)}, u32[]{:S(2)}, u32[]{:S(2)}) collective-permute-start(bf16[2,2,128,128]{3,2,1,0:T(8,128)(2,1)S(1)} %cut.1), channel_id=1, source_target_pairs={{0,12},{4,8},{8,4},{12,0},{1,13},{5,9},{9,5},{13,1},{2,14},{6,10},... | collective-permute-start | bytes 393224 | tf_op jit(solution)/shard_map/ppermute | solution.py:473
  12.1 8.9 %collective-permute-start.3 = (bf16[2,2,128,128]{3,2,1,0:T(8,128)(2,1)S(1)}, bf16[2,2,128,128]{3,2,1,0:T(8,128)(2,1)S(1)}, u32[]{:S(2)}, u32[]{:S(2)}) collective-permute-start(bf16[2,2,128,128]{3,2,1,0:T(8,128)(2,1)S(1)} %collective-permute-done.2.refs_0_), channel_id=1, source_target_pairs={{0,2},{1,3},{2,0},{3,1},{4,6},{5,7},{6,4},{7,5},{8,10},{9,11},{10,... | collective-permute-start | bytes 393224 | tf_op jit(solution)/shard_map/ppermute | solution.py:473
  18.5 6.3 %collective-permute-start.9 = (bf16[2,2,128,128]{3,2,1,0:T(8,128)(2,1)S(1)}, bf16[2,2,128,128]{3,2,1,0:T(8,128)(2,1)S(1)}, u32[]{:S(2)}, u32[]{:S(2)}) collective-permute-start(bf16[2,2,128,128]{3,2,1,0:T(8,128)(2,1)S(1)} %collective-permute-done.8.refs_0_), channel_id=1, source_target_pairs={{0,2},{1,3},{2,0},{3,1},{4,6},{5,7},{6,4},{7,5},{8,10},{9,11},{10,... | collective-permute-start | bytes 393224 | tf_op jit(solution)/shard_map/ppermute | solution.py:473
  21.0 4.9 %collective-permute-start.7 = (bf16[4,2,128,128]{3,2,1,0:T(8,128)(2,1)S(1)}, bf16[4,2,128,128]{3,2,1,0:T(8,128)(2,1)S(1)}, u32[]{:S(2)}, u32[]{:S(2)}) collective-permute-start(bf16[4,2,128,128]{3,2,1,0:T(8,128)(2,1)S(1)} %collective-permute-done.6.refs_0_), channel_id=1, source_target_pairs={{0,1},{1,0},{2,3},{3,2},{4,5},{5,4},{6,7},{7,6},{8,9},{9,8},{10,11... | collective-permute-start | bytes 786440 | tf_op jit(solution)/shard_map/ppermute | solution.py:473
  21.1 3.9 %collective-permute-start.4 = (bf16[2,2,128,128]{3,2,1,0:T(8,128)(2,1)S(1)}, bf16[2,2,128,128]{3,2,1,0:T(8,128)(2,1)S(1)}, u32[]{:S(2)}, u32[]{:S(2)}) collective-permute-start(bf16[2,2,128,128]{3,2,1,0:T(8,128)(2,1)S(1)} %collective-permute-done.2.refs_0_), channel_id=1, source_target_pairs={{0,1},{1,0},{2,3},{3,2},{4,5},{5,4},{6,7},{7,6},{8,9},{9,8},{10,11... | collective-permute-start | bytes 393224 | tf_op jit(solution)/shard_map/ppermute | solution.py:473
  21.6 3.7 %collective-permute-start.5 = (bf16[2,2,128,128]{3,2,1,0:T(8,128)(2,1)S(1)}, bf16[2,2,128,128]{3,2,1,0:T(8,128)(2,1)S(1)}, u32[]{:S(2)}, u32[]{:S(2)}) collective-permute-start(bf16[2,2,128,128]{3,2,1,0:T(8,128)(2,1)S(1)} %collective-permute-done.3.refs_2_), channel_id=1, source_target_pairs={{0,1},{1,0},{2,3},{3,2},{4,5},{5,4},{6,7},{7,6},{8,9},{9,8},{10,11... | collective-permute-start | bytes 393224 | tf_op jit(solution)/shard_map/ppermute | solution.py:473
  24.7 1.8 %collective-permute-start.10 = (bf16[2,2,128,128]{3,2,1,0:T(8,128)(2,1)S(1)}, bf16[2,2,128,128]{3,2,1,0:T(8,128)(2,1)S(1)}, u32[]{:S(2)}, u32[]{:S(2)}) collective-permute-start(bf16[2,2,128,128]{3,2,1,0:T(8,128)(2,1)S(1)} %collective-permute-done.8.refs_0_), channel_id=1, source_target_pairs={{0,1},{1,0},{2,3},{3,2},{4,5},{5,4},{6,7},{7,6},{8,9},{9,8},{10,11... | collective-permute-start | bytes 393224 | tf_op jit(solution)/shard_map/ppermute | solution.py:473
  24.9 1.5 %collective-permute-start.11 = (bf16[2,2,128,128]{3,2,1,0:T(8,128)(2,1)S(1)}, bf16[2,2,128,128]{3,2,1,0:T(8,128)(2,1)S(1)}, u32[]{:S(2)}, u32[]{:S(2)}) collective-permute-start(bf16[2,2,128,128]{3,2,1,0:T(8,128)(2,1)S(1)} %collective-permute-done.9.refs_2_), channel_id=1, source_target_pairs={{0,1},{1,0},{2,3},{3,2},{4,5},{5,4},{6,7},{7,6},{8,9},{9,8},{10,11... | collective-permute-start | bytes 393224 | tf_op jit(solution)/shard_map/ppermute | solution.py:473
  27.1 3.2 %collective-permute-start.12 = (f32[64,128]{1,0:T(8,128)S(1)}, f32[64,128]{1,0:T(8,128)S(1)}, u32[]{:S(2)}, u32[]{:S(2)}) collective-permute-start(f32[64,128]{1,0:T(8,128)S(1)} %get-tuple-element.59), channel_id=1, source_target_pairs={{0,1},{1,0},{2,3},{3,2},{4,5},{5,4},{6,7},{7,6},{8,9},{9,8},{10,11... | collective-permute-start | bytes 98312 | tf_op jit(solution)/shard_map/ppermute | solution.py:473
  27.4 4.2 %collective-permute-start.13 = (f32[64,128]{1,0:T(8,128)S(1)}, f32[64,128]{1,0:T(8,128)S(1)}, u32[]{:S(2)}, u32[]{:S(2)}) collective-permute-start(f32[64,128]{1,0:T(8,128)S(1)} %get-tuple-element.59), channel_id=1, source_target_pairs={{0,2},{1,3},{2,0},{3,1},{4,6},{5,7},{6,4},{7,5},{8,10},{9,11},{10,... | collective-permute-start | bytes 98312 | tf_op jit(solution)/shard_map/ppermute | solution.py:473
  27.9 3.7 %collective-permute-start.14 = (f32[64,128]{1,0:T(8,128)S(1)}, f32[64,128]{1,0:T(8,128)S(1)}, u32[]{:S(2)}, u32[]{:S(2)}) collective-permute-start(f32[64,128]{1,0:T(8,128)S(1)} %get-tuple-element.59), channel_id=1, source_target_pairs={{0,3},{1,2},{2,1},{3,0},{4,7},{5,6},{6,5},{7,4},{8,11},{9,10},{10,... | collective-permute-start | bytes 98312 | tf_op jit(solution)/shard_map/ppermute | solution.py:473

commit v7 on v6

--- a/solution.py
+++ b/solution.py
@@ -395,7 +395,7 @@
     )(*flat)
 
 
-ROWS = 64
+ROWS = 32
 
 
 def final_kernel(pairs, target_ref, state_ref, prod_ref, *refs):
@@ -419,7 +419,7 @@
         base = lax.bitwise_xor(lax.axis_index("fsdp"), pair) * heads
         for head in range(heads):
             places.append((slot * heads + head, lanes_of(base + head), incoming[head : head + 1]))
-    copies, totals = [], []
+    copies, scales, totals = [], [], []
     for block in range(0, tokens, ROWS):
         at = pl.ds(block, ROWS)
         squares = jnp.zeros((ROWS, HS), jnp.float32)
@@ -435,7 +435,9 @@
         )
         copies[-1].start()
         mean = jnp.sum(squares, axis=1, keepdims=True) * (1.0 / full)
-        scale = jnp.broadcast_to(lax.rsqrt(mean + 1e-06), (ROWS, HS))
+        scales.append(jnp.broadcast_to(lax.rsqrt(mean + 1e-06), (ROWS, HS)))
+    for block, scale in zip(range(0, tokens, ROWS), scales):
+        at = pl.ds(block, ROWS)
         total = jnp.zeros((ROWS, HS), jnp.float32)
         for start in range(0, full, HS):
             lanes = slice(start, start + HS)

time: 33.6 us -> 33.5 us (level)
  no operation moved by 1% of the time
where the time goes in v7:
time: 33.5 us; the launch traced here: 33.3 us
  starting transfers between devices  15.5 us (46%)
  Pallas kernels  9.36 us (28%)
  waiting for transfers between devices  7.68 us (23%)
  between operations  0.76 us (2%)
    ppermute x14, starting transfers between devices, swap(): lax.ppermute(value, axis, [(i, i ^ apart) for i in range(lax.axis_size(ax...  14.2 us
    ppermute x14, waiting for transfers between devices, swap(): lax.ppermute(value, axis, [(i, i ^ apart) for i in range(lax.axis_size(ax...  7.67 us
    pallas_call x4, Pallas kernels, shard(): pallas(functools.partial(shard_kernel, total, pair, counts), 'shard', [ja...  2.42 us
    pallas_call x1, Pallas kernels, conv_rows(): pallas(conv_kernel, 'conv_rows', [jax.ShapeDtypeStruct((heads, tokens, HS...  1.92 us
    pallas_call x1, Pallas kernels, final(): pallas(functools.partial(final_kernel, pairs), 'final', [jax.ShapeDtypeSt...  1.7 us
    ppermute x1, starting transfers between devices, from_behind(): lax.ppermute(value, axis, [(source, source + steps) for source in range(l...  1.29 us
    pallas_call x1, Pallas kernels, lay_out(): pallas(lay_kernel, 'lay_out', [whole, whole], in_vmem(len(flat)), in_vmem...  1.23 us
    pallas_call x1, Pallas kernels, fetch(): pallas(fetch_kernel, 'fetch', [jax.ShapeDtypeStruct((held // 2,) + gate_w...  1.17 us
  transfers between devices with their start and end apart: 15, of which 4 were waited for; matrix products, arithmetic and copies ran while one was open for 0% of the time, Pallas kernels for 20%

profile of v7, /device:TPU:0, one launch (start us, length us, event | category | flops | bytes accessed | tf_op | source)
XLA Modules:
  0.0 33.3 jit_solution(3081427100003022961)
XLA Ops:
  0.6 0.9 %cut.1 = bf16[2,2,128,128]{3,2,1,0:T(8,128)(2,1)S(1)} custom-call(bf16[8,2,128,128]{3,2,1,0:T(8,128)(2,1)} %w_ref.3), custom_call_target="tpu_custom_call" | custom-call | tf_op jit(solution)/shard_map/cut/pallas_call | solution.py:161
  1.6 4.1 %collective-permute-start.2 = (bf16[2,2,128,128]{3,2,1,0:T(8,128)(2,1)S(1)}, bf16[2,2,128,128]{3,2,1,0:T(8,128)(2,1)S(1)}, u32[]{:S(2)}, u32[]{:S(2)}) collective-permute-start(bf16[2,2,128,128]{3,2,1,0:T(8,128)(2,1)S(1)} %cut.1), channel_id=1, source_target_pairs={{0,8},{4,12},{8,0},{12,4},{1,9},{5,13},{9,1},{13,5},{2,10},{6,14},... | collective-permute-start | bytes 393224 | tf_op jit(solution)/shard_map/ppermute | solution.py:475
  5.7 1.5 %collective-permute-start = (bf16[1,128,4096]{2,1,0:T(8,128)(2,1)}, bf16[1,128,4096]{2,1,0:T(8,128)(2,1)S(1)}, u32[]{:S(2)}, u32[]{:S(2)}) collective-permute-start(bf16[1,128,4096]{2,1,0:T(8,128)(2,1)} %param.10), channel_id=1, source_target_pairs={{0,16},{16,0},{1,17},{17,1},{2,18},{18,2},{3,19},{19,3},{4,20},{20... | collective-permute-start | bytes 3145736 | tf_op jit(solution)/shard_map/ppermute | solution.py:475
  7.2 0.0 copy-start.1
  7.2 0.0 copy-start
  7.2 0.0 copy-start.2
  7.2 0.0 copy-start.3
  7.2 1.2 %fetch.1 = (bf16[4,2,128,128]{3,2,1,0:T(8,128)(2,1)S(1)}, bf16[16,4096]{1,0:T(8,128)(2,1)S(1)}, s32[1,128]{1,0:T(1,128)S(1)}, f32[4,4096]{1,0:T(4,128)S(1)}, f32[1,4096]{1,0:T(1,128)S(1)}) custom-call(bf16[1,128,4096]{2,1,0:T(8,128)(2,1)} %x_ref.3, bf16[8,2,128,128]{3,2,1,0:T(8,128)(2,1)} %w_ref.3, s32[1,128]{1,0:T(1,128)} %refs_0_.2, f32[4,4096]{1,0:T(4,128)} %refs_1_.1, ...), custom_call_target="tpu_custom_call" | custom-call | flops 1500000000 | tf_op jit(solution)/shard_map/fetch/pallas_call | solution.py:194
  8.4 1.6 %collective-permute-start.6 = (bf16[4,2,128,128]{3,2,1,0:T(8,128)(2,1)S(1)}, bf16[4,2,128,128]{3,2,1,0:T(8,128)(2,1)S(1)}, u32[]{:S(2)}, u32[]{:S(2)}) collective-permute-start(bf16[4,2,128,128]{3,2,1,0:T(8,128)(2,1)S(1)} %get-tuple-element.45), channel_id=1, source_target_pairs={{0,4},{4,0},{8,12},{12,8},{1,5},{5,1},{9,13},{13,9},{2,6},{6,2},{1... | collective-permute-start | bytes 786440 | tf_op jit(solution)/shard_map/ppermute | solution.py:475
  10.0 1.3 %collective-permute-start.1 = (bf16[16,4096]{1,0:T(8,128)(2,1)S(1)}, bf16[16,4096]{1,0:T(8,128)(2,1)S(1)}, u32[]{:S(2)}, u32[]{:S(2)}) collective-permute-start(bf16[16,4096]{1,0:T(8,128)(2,1)S(1)} %get-tuple-element.31), channel_id=1, source_target_pairs={{0,1},{1,2},{2,3},{4,5},{5,6},{6,7},{8,9},{9,10},{10,11},{12,13},{... | collective-permute-start | bytes 393224 | tf_op jit(solution)/shard_map/ppermute | solution.py:42
  11.3 0.3 collective-permute-start.8
  11.6 0.5 %collective-permute-done.2.refs_0_ = bf16[2,2,128,128]{3,2,1,0:T(8,128)(2,1)S(1)} collective-permute-done((bf16[2,2,128,128]{3,2,1,0:T(8,128)(2,1)S(1)}, bf16[2,2,128,128]{3,2,1,0:T(8,128)(2,1)S(1)}, u32[]{:S(2)}, u32[]{:S(2)}) %collective-permute-start.2) | collective-permute-done | bytes 131104 | tf_op jit(solution)/shard_map/ppermute | solution.py:475
  12.1 1.6 %collective-permute-start.3 = (bf16[2,2,128,128]{3,2,1,0:T(8,128)(2,1)S(1)}, bf16[2,2,128,128]{3,2,1,0:T(8,128)(2,1)S(1)}, u32[]{:S(2)}, u32[]{:S(2)}) collective-permute-start(bf16[2,2,128,128]{3,2,1,0:T(8,128)(2,1)S(1)} %collective-permute-done.2.refs_0_), channel_id=1, source_target_pairs={{0,2},{1,3},{2,0},{3,1},{4,6},{5,7},{6,4},{7,5},{8,10},{9,11},{10,... | collective-permute-start | bytes 393224 | tf_op jit(solution)/shard_map/ppermute | solution.py:475
  13.7 0.0 collective-permute-done.1.edge_ref
  13.7 0.0 copy-done.1
  13.7 1.9 %conv_rows.1 = (bf16[32,128,128]{2,1,0:T(8,128)(2,1)S(1)}, f32[2,128,128]{2,1,0:T(8,128)S(1)}) custom-call(bf16[1,128,4096]{2,1,0:T(8,128)(2,1)S(1)} %copy-done.1, bf16[16,4096]{1,0:T(8,128)(2,1)S(1)} %collective-permute-done.1.edge_ref, s32[1,128]{1,0:T(1,128)S(1)} %get-tuple-element.32.pos_ref, f32[4,4096]{1,0:T(4,128)S(1)} %get-tuple-element.33.w_ref, ...), custom_call_target="tpu_custom_call" | custom-call | tf_op jit(solution)/shard_map/conv_rows/pallas_call | solution.py:264
  15.6 2.8 %collective-permute-done.8.refs_0_ = bf16[2,2,128,128]{3,2,1,0:T(8,128)(2,1)S(1)} collective-permute-done((bf16[2,2,128,128]{3,2,1,0:T(8,128)(2,1)S(1)}, bf16[2,2,128,128]{3,2,1,0:T(8,128)(2,1)S(1)}, u32[]{:S(2)}, u32[]{:S(2)}) %collective-permute-start.8) | collective-permute-done | bytes 131104 | tf_op jit(solution)/shard_map/ppermute | solution.py:475
  18.5 1.9 %collective-permute-start.9 = (bf16[2,2,128,128]{3,2,1,0:T(8,128)(2,1)S(1)}, bf16[2,2,128,128]{3,2,1,0:T(8,128)(2,1)S(1)}, u32[]{:S(2)}, u32[]{:S(2)}) collective-permute-start(bf16[2,2,128,128]{3,2,1,0:T(8,128)(2,1)S(1)} %collective-permute-done.8.refs_0_), channel_id=1, source_target_pairs={{0,2},{1,3},{2,0},{3,1},{4,6},{5,7},{6,4},{7,5},{8,10},{9,11},{10,... | collective-permute-start | bytes 393224 | tf_op jit(solution)/shard_map/ppermute | solution.py:475
  20.4 0.0 copy-done
  20.4 0.0 copy-done.2
  20.4 0.0 copy-done.3
  20.4 0.6 %shard.4 = (f32[8,128,128]{2,1,0:T(8,128)S(1)}, f32[8,128,128]{2,1,0:T(8,128)S(1)}, f32[8,2,8,128]{3,2,1,0:T(8,128)S(1)}, f32[16,128]{1,0:T(8,128)S(1)}) custom-call(bf16[32,128,128]{2,1,0:T(8,128)(2,1)S(1)} %get-tuple-element.35.conv_ref, f32[2,128,128]{2,1,0:T(8,128)S(1)} %get-tuple-element.36.mask_ref, f32[2,4096]{1,0:T(2,128)S(1)} %copy-done.2, ...), custom_call_target="tpu_custom_call" | custom-call | tf_op jit(solution)/shard_map/shard/pallas_call | solution.py:352
  21.0 0.0 collective-permute-done.3.refs_2_
  21.0 0.0 collective-permute-done.6.refs_0_
  21.0 0.1 collective-permute-start.7
  21.1 0.5 %collective-permute-start.4 = (bf16[2,2,128,128]{3,2,1,0:T(8,128)(2,1)S(1)}, bf16[2,2,128,128]{3,2,1,0:T(8,128)(2,1)S(1)}, u32[]{:S(2)}, u32[]{:S(2)}) collective-permute-start(bf16[2,2,128,128]{3,2,1,0:T(8,128)(2,1)S(1)} %collective-permute-done.2.refs_0_), channel_id=1, source_target_pairs={{0,1},{1,0},{2,3},{3,2},{4,5},{5,4},{6,7},{7,6},{8,9},{9,8},{10,11... | collective-permute-start | bytes 393224 | tf_op jit(solution)/shard_map/ppermute | solution.py:475
  21.6 0.1 collective-permute-start.5
  21.7 3.1 %collective-permute-done.9.refs_2_ = bf16[2,2,128,128]{3,2,1,0:T(8,128)(2,1)S(1)} collective-permute-done((bf16[2,2,128,128]{3,2,1,0:T(8,128)(2,1)S(1)}, bf16[2,2,128,128]{3,2,1,0:T(8,128)(2,1)S(1)}, u32[]{:S(2)}, u32[]{:S(2)}) %collective-permute-start.9) | collective-permute-done | bytes 131104 | tf_op jit(solution)/shard_map/ppermute | solution.py:475
  24.7 0.2 collective-permute-start.10
  24.9 0.0 collective-permute-done.4.refs_1_
  24.9 0.3 collective-permute-start.11
  25.2 0.0 collective-permute-done.5.refs_3_
  25.2 0.6 %shard.5 = (f32[8,128,128]{2,1,0:T(8,128)S(1)}, f32[8,128,128]{2,1,0:T(8,128)S(1)}, f32[8,2,8,128]{3,2,1,0:T(8,128)S(1)}, f32[16,128]{1,0:T(8,128)S(1)}) custom-call(bf16[32,128,128]{2,1,0:T(8,128)(2,1)S(1)} %get-tuple-element.35.conv_ref, f32[2,128,128]{2,1,0:T(8,128)S(1)} %get-tuple-element.36.mask_ref, f32[2,4096]{1,0:T(2,128)S(1)} %copy-done.2, ...), custom_call_target="tpu_custom_call" | custom-call | tf_op jit(solution)/shard_map/shard/pallas_call | solution.py:352
  25.9 0.0 collective-permute-done.7.refs_1_
  25.9 0.6 %shard.6 = (f32[8,128,128]{2,1,0:T(8,128)S(1)}, f32[8,128,128]{2,1,0:T(8,128)S(1)}, f32[8,2,8,128]{3,2,1,0:T(8,128)S(1)}, f32[16,128]{1,0:T(8,128)S(1)}) custom-call(bf16[32,128,128]{2,1,0:T(8,128)(2,1)S(1)} %get-tuple-element.35.conv_ref, f32[2,128,128]{2,1,0:T(8,128)S(1)} %get-tuple-element.36.mask_ref, f32[2,4096]{1,0:T(2,128)S(1)} %copy-done.2, ...), custom_call_target="tpu_custom_call" | custom-call | tf_op jit(solution)/shard_map/shard/pallas_call | solution.py:352
  26.5 0.0 collective-permute-done.10.refs_1_
  26.5 0.0 collective-permute-done.11.refs_3_
  26.5 0.6 %shard.7 = (f32[8,128,128]{2,1,0:T(8,128)S(1)}, f32[8,128,128]{2,1,0:T(8,128)S(1)}, f32[8,2,8,128]{3,2,1,0:T(8,128)S(1)}, f32[64,128]{1,0:T(8,128)S(1)}) custom-call(bf16[32,128,128]{2,1,0:T(8,128)(2,1)S(1)} %get-tuple-element.35.conv_ref, f32[2,128,128]{2,1,0:T(8,128)S(1)} %get-tuple-element.36.mask_ref, f32[2,4096]{1,0:T(2,128)S(1)} %copy-done.2, ...), custom_call_target="tpu_custom_call" | custom-call | flops 5000000000 | tf_op jit(solution)/shard_map/shard/pallas_call | solution.py:352
  27.1 0.3 collective-permute-start.12
  27.4 0.5 %collective-permute-start.13 = (f32[64,128]{1,0:T(8,128)S(1)}, f32[64,128]{1,0:T(8,128)S(1)}, u32[]{:S(2)}, u32[]{:S(2)}) collective-permute-start(f32[64,128]{1,0:T(8,128)S(1)} %get-tuple-element.59), channel_id=1, source_target_pairs={{0,2},{1,3},{2,0},{3,1},{4,6},{5,7},{6,4},{7,5},{8,10},{9,11},{10,... | collective-permute-start | bytes 98312 | tf_op jit(solution)/shard_map/ppermute | solution.py:475
  27.9 1.2 %collective-permute-start.14 = (f32[64,128]{1,0:T(8,128)S(1)}, f32[64,128]{1,0:T(8,128)S(1)}, u32[]{:S(2)}, u32[]{:S(2)}) collective-permute-start(f32[64,128]{1,0:T(8,128)S(1)} %get-tuple-element.59), channel_id=1, source_target_pairs={{0,3},{1,2},{2,1},{3,0},{4,7},{5,6},{6,5},{7,4},{8,11},{9,10},{10,... | collective-permute-start | bytes 98312 | tf_op jit(solution)/shard_map/ppermute | solution.py:475
  29.0 1.2 %lay_out.1 = (f32[32,128,128]{2,1,0:T(8,128)S(1)}, f32[32,128,128]{2,1,0:T(8,128)S(1)}) custom-call(f32[8,128,128]{2,1,0:T(8,128)S(1)} %get-tuple-element.37.refs_0_, f32[8,128,128]{2,1,0:T(8,128)S(1)} %get-tuple-element.38.refs_1_, f32[8,2,8,128]{3,2,1,0:T(8,128)S(1)} %get-tuple-element.39.refs_2_, f32[8,128,128]{2,1,0:T(8,128)S(1)} %get-tuple-element.42.refs_3_, ...), custom_call_target="tpu_custom_call" | custom-call | tf_op jit(solution)/shard_map/lay_out/pallas_call | solution.py:388
  30.3 0.0 collective-permute-done.12.refs_0_
  30.3 1.3 %collective-permute-done.13.refs_1_ = f32[64,128]{1,0:T(8,128)S(1)} collective-permute-done((f32[64,128]{1,0:T(8,128)S(1)}, f32[64,128]{1,0:T(8,128)S(1)}, u32[]{:S(2)}, u32[]{:S(2)}) %collective-permute-start.13) | collective-permute-done | bytes 32800 | tf_op jit(solution)/shard_map/ppermute | solution.py:475
  31.6 0.0 collective-permute-done.14.refs_2_
  31.6 0.0 collective-permute-done.target_ref
  31.6 1.7 %final.1 = (bf16[1,128,4096]{2,1,0:T(8,128)(2,1)}, f32[1,128]{1,0:T(1,128)}) custom-call(bf16[1,128,4096]{2,1,0:T(8,128)(2,1)S(1)} %collective-permute-done.target_ref, f32[32,128,128]{2,1,0:T(8,128)S(1)} %get-tuple-element.57.state_ref, f32[32,128,128]{2,1,0:T(8,128)S(1)} %get-tuple-element.58.prod_ref, f32[64,128]{1,0:T(8,128)S(1)} %collective-permute-done.12.refs_0_, ...), custom_call_target="tpu_custom_call" | custom-call | tf_op jit(solution)/shard_map/final/pallas_call | solution.py:457
Async XLA Ops:
  1.6 10.5 %collective-permute-start.2 = (bf16[2,2,128,128]{3,2,1,0:T(8,128)(2,1)S(1)}, bf16[2,2,128,128]{3,2,1,0:T(8,128)(2,1)S(1)}, u32[]{:S(2)}, u32[]{:S(2)}) collective-permute-start(bf16[2,2,128,128]{3,2,1,0:T(8,128)(2,1)S(1)} %cut.1), channel_id=1, source_target_pairs={{0,8},{4,12},{8,0},{12,4},{1,9},{5,13},{9,1},{13,5},{2,10},{6,14},... | collective-permute-start | bytes 393224 | tf_op jit(solution)/shard_map/ppermute | solution.py:475
  5.7 25.9 %collective-permute-start = (bf16[1,128,4096]{2,1,0:T(8,128)(2,1)}, bf16[1,128,4096]{2,1,0:T(8,128)(2,1)S(1)}, u32[]{:S(2)}, u32[]{:S(2)}) collective-permute-start(bf16[1,128,4096]{2,1,0:T(8,128)(2,1)} %param.10), channel_id=1, source_target_pairs={{0,16},{16,0},{1,17},{17,1},{2,18},{18,2},{3,19},{19,3},{4,20},{20... | collective-permute-start | bytes 3145736 | tf_op jit(solution)/shard_map/ppermute | solution.py:475
  7.2 6.5 %copy-start.1 = (bf16[1,128,4096]{2,1,0:T(8,128)(2,1)S(1)}, bf16[1,128,4096]{2,1,0:T(8,128)(2,1)}, u32[]{:S(2)}) copy-start(bf16[1,128,4096]{2,1,0:T(8,128)(2,1)} %x_ref.3) | copy-start | bytes 3145732
  7.2 13.2 %copy-start = (bf16[8,2,128,128]{3,2,1,0:T(8,128)(2,1)S(1)}, bf16[8,2,128,128]{3,2,1,0:T(8,128)(2,1)}, u32[]{:S(2)}) copy-start(bf16[8,2,128,128]{3,2,1,0:T(8,128)(2,1)} %w_ref.3) | copy-start | bytes 1572868
  7.2 13.2 %copy-start.2 = (f32[2,4096]{1,0:T(2,128)S(1)}, f32[2,4096]{1,0:T(2,128)}, u32[]{:S(2)}) copy-start(f32[2,4096]{1,0:T(2,128)} %bias_ref.7) | copy-start | bytes 98308
  7.2 13.2 %copy-start.3 = (f32[4096]{0:T(1024)S(1)}, f32[4096]{0:T(1024)}, u32[]{:S(2)}) copy-start(f32[4096]{0:T(1024)} %param.15) | copy-start | bytes 49156
  8.4 12.6 %collective-permute-start.6 = (bf16[4,2,128,128]{3,2,1,0:T(8,128)(2,1)S(1)}, bf16[4,2,128,128]{3,2,1,0:T(8,128)(2,1)S(1)}, u32[]{:S(2)}, u32[]{:S(2)}) collective-permute-start(bf16[4,2,128,128]{3,2,1,0:T(8,128)(2,1)S(1)} %get-tuple-element.45), channel_id=1, source_target_pairs={{0,4},{4,0},{8,12},{12,8},{1,5},{5,1},{9,13},{13,9},{2,6},{6,2},{1... | collective-permute-start | bytes 786440 | tf_op jit(solution)/shard_map/ppermute | solution.py:475
  10.0 3.7 %collective-permute-start.1 = (bf16[16,4096]{1,0:T(8,128)(2,1)S(1)}, bf16[16,4096]{1,0:T(8,128)(2,1)S(1)}, u32[]{:S(2)}, u32[]{:S(2)}) collective-permute-start(bf16[16,4096]{1,0:T(8,128)(2,1)S(1)} %get-tuple-element.31), channel_id=1, source_target_pairs={{0,1},{1,2},{2,3},{4,5},{5,6},{6,7},{8,9},{9,10},{10,11},{12,13},{... | collective-permute-start | bytes 393224 | tf_op jit(solution)/shard_map/ppermute | solution.py:42
  11.3 7.2 %collective-permute-start.8 = (bf16[2,2,128,128]{3,2,1,0:T(8,128)(2,1)S(1)}, bf16[2,2,128,128]{3,2,1,0:T(8,128)(2,1)S(1)}, u32[]{:S(2)}, u32[]{:S(2)}) collective-permute-start(bf16[2,2,128,128]{3,2,1,0:T(8,128)(2,1)S(1)} %cut.1), channel_id=1, source_target_pairs={{0,12},{4,8},{8,4},{12,0},{1,13},{5,9},{9,5},{13,1},{2,14},{6,10},... | collective-permute-start | bytes 393224 | tf_op jit(solution)/shard_map/ppermute | solution.py:475
  12.1 8.9 %collective-permute-start.3 = (bf16[2,2,128,128]{3,2,1,0:T(8,128)(2,1)S(1)}, bf16[2,2,128,128]{3,2,1,0:T(8,128)(2,1)S(1)}, u32[]{:S(2)}, u32[]{:S(2)}) collective-permute-start(bf16[2,2,128,128]{3,2,1,0:T(8,128)(2,1)S(1)} %collective-permute-done.2.refs_0_), channel_id=1, source_target_pairs={{0,2},{1,3},{2,0},{3,1},{4,6},{5,7},{6,4},{7,5},{8,10},{9,11},{10,... | collective-permute-start | bytes 393224 | tf_op jit(solution)/shard_map/ppermute | solution.py:475
  18.5 6.3 %collective-permute-start.9 = (bf16[2,2,128,128]{3,2,1,0:T(8,128)(2,1)S(1)}, bf16[2,2,128,128]{3,2,1,0:T(8,128)(2,1)S(1)}, u32[]{:S(2)}, u32[]{:S(2)}) collective-permute-start(bf16[2,2,128,128]{3,2,1,0:T(8,128)(2,1)S(1)} %collective-permute-done.8.refs_0_), channel_id=1, source_target_pairs={{0,2},{1,3},{2,0},{3,1},{4,6},{5,7},{6,4},{7,5},{8,10},{9,11},{10,... | collective-permute-start | bytes 393224 | tf_op jit(solution)/shard_map/ppermute | solution.py:475
  21.0 4.9 %collective-permute-start.7 = (bf16[4,2,128,128]{3,2,1,0:T(8,128)(2,1)S(1)}, bf16[4,2,128,128]{3,2,1,0:T(8,128)(2,1)S(1)}, u32[]{:S(2)}, u32[]{:S(2)}) collective-permute-start(bf16[4,2,128,128]{3,2,1,0:T(8,128)(2,1)S(1)} %collective-permute-done.6.refs_0_), channel_id=1, source_target_pairs={{0,1},{1,0},{2,3},{3,2},{4,5},{5,4},{6,7},{7,6},{8,9},{9,8},{10,11... | collective-permute-start | bytes 786440 | tf_op jit(solution)/shard_map/ppermute | solution.py:475
  21.1 3.9 %collective-permute-start.4 = (bf16[2,2,128,128]{3,2,1,0:T(8,128)(2,1)S(1)}, bf16[2,2,128,128]{3,2,1,0:T(8,128)(2,1)S(1)}, u32[]{:S(2)}, u32[]{:S(2)}) collective-permute-start(bf16[2,2,128,128]{3,2,1,0:T(8,128)(2,1)S(1)} %collective-permute-done.2.refs_0_), channel_id=1, source_target_pairs={{0,1},{1,0},{2,3},{3,2},{4,5},{5,4},{6,7},{7,6},{8,9},{9,8},{10,11... | collective-permute-start | bytes 393224 | tf_op jit(solution)/shard_map/ppermute | solution.py:475
  21.6 3.7 %collective-permute-start.5 = (bf16[2,2,128,128]{3,2,1,0:T(8,128)(2,1)S(1)}, bf16[2,2,128,128]{3,2,1,0:T(8,128)(2,1)S(1)}, u32[]{:S(2)}, u32[]{:S(2)}) collective-permute-start(bf16[2,2,128,128]{3,2,1,0:T(8,128)(2,1)S(1)} %collective-permute-done.3.refs_2_), channel_id=1, source_target_pairs={{0,1},{1,0},{2,3},{3,2},{4,5},{5,4},{6,7},{7,6},{8,9},{9,8},{10,11... | collective-permute-start | bytes 393224 | tf_op jit(solution)/shard_map/ppermute | solution.py:475
  24.7 1.8 %collective-permute-start.10 = (bf16[2,2,128,128]{3,2,1,0:T(8,128)(2,1)S(1)}, bf16[2,2,128,128]{3,2,1,0:T(8,128)(2,1)S(1)}, u32[]{:S(2)}, u32[]{:S(2)}) collective-permute-start(bf16[2,2,128,128]{3,2,1,0:T(8,128)(2,1)S(1)} %collective-permute-done.8.refs_0_), channel_id=1, source_target_pairs={{0,1},{1,0},{2,3},{3,2},{4,5},{5,4},{6,7},{7,6},{8,9},{9,8},{10,11... | collective-permute-start | bytes 393224 | tf_op jit(solution)/shard_map/ppermute | solution.py:475
  24.9 1.5 %collective-permute-start.11 = (bf16[2,2,128,128]{3,2,1,0:T(8,128)(2,1)S(1)}, bf16[2,2,128,128]{3,2,1,0:T(8,128)(2,1)S(1)}, u32[]{:S(2)}, u32[]{:S(2)}) collective-permute-start(bf16[2,2,128,128]{3,2,1,0:T(8,128)(2,1)S(1)} %collective-permute-done.9.refs_2_), channel_id=1, source_target_pairs={{0,1},{1,0},{2,3},{3,2},{4,5},{5,4},{6,7},{7,6},{8,9},{9,8},{10,11... | collective-permute-start | bytes 393224 | tf_op jit(solution)/shard_map/ppermute | solution.py:475
  27.1 3.2 %collective-permute-start.12 = (f32[64,128]{1,0:T(8,128)S(1)}, f32[64,128]{1,0:T(8,128)S(1)}, u32[]{:S(2)}, u32[]{:S(2)}) collective-permute-start(f32[64,128]{1,0:T(8,128)S(1)} %get-tuple-element.59), channel_id=1, source_target_pairs={{0,1},{1,0},{2,3},{3,2},{4,5},{5,4},{6,7},{7,6},{8,9},{9,8},{10,11... | collective-permute-start | bytes 98312 | tf_op jit(solution)/shard_map/ppermute | solution.py:475
  27.4 4.2 %collective-permute-start.13 = (f32[64,128]{1,0:T(8,128)S(1)}, f32[64,128]{1,0:T(8,128)S(1)}, u32[]{:S(2)}, u32[]{:S(2)}) collective-permute-start(f32[64,128]{1,0:T(8,128)S(1)} %get-tuple-element.59), channel_id=1, source_target_pairs={{0,2},{1,3},{2,0},{3,1},{4,6},{5,7},{6,4},{7,5},{8,10},{9,11},{10,... | collective-permute-start | bytes 98312 | tf_op jit(solution)/shard_map/ppermute | solution.py:475
  27.9 3.7 %collective-permute-start.14 = (f32[64,128]{1,0:T(8,128)S(1)}, f32[64,128]{1,0:T(8,128)S(1)}, u32[]{:S(2)}, u32[]{:S(2)}) collective-permute-start(f32[64,128]{1,0:T(8,128)S(1)} %get-tuple-element.59), channel_id=1, source_target_pairs={{0,3},{1,2},{2,1},{3,0},{4,7},{5,6},{6,5},{7,4},{8,11},{9,10},{10,... | collective-permute-start | bytes 98312 | tf_op jit(solution)/shard_map/ppermute | solution.py:475

commit v8 on v7

--- a/solution.py
+++ b/solution.py
@@ -395,7 +395,7 @@
     )(*flat)
 
 
-ROWS = 32
+ROWS = 64
 
 
 def final_kernel(pairs, target_ref, state_ref, prod_ref, *refs):

time: 33.5 us -> 33.4 us (level)
  no operation moved by 1% of the time
where the time goes in v8:
time: 33.4 us; the launch traced here: 33.2 us
  starting transfers between devices  15.5 us (46%)
  Pallas kernels  9.34 us (28%)
  waiting for transfers between devices  7.68 us (23%)
  between operations  0.76 us (2%)
    ppermute x14, starting transfers between devices, swap(): lax.ppermute(value, axis, [(i, i ^ apart) for i in range(lax.axis_size(ax...  14.2 us
    ppermute x14, waiting for transfers between devices, swap(): lax.ppermute(value, axis, [(i, i ^ apart) for i in range(lax.axis_size(ax...  7.67 us
    pallas_call x4, Pallas kernels, shard(): pallas(functools.partial(shard_kernel, total, pair, counts), 'shard', [ja...  2.42 us
    pallas_call x1, Pallas kernels, conv_rows(): pallas(conv_kernel, 'conv_rows', [jax.ShapeDtypeStruct((heads, tokens, HS...  1.92 us
    pallas_call x1, Pallas kernels, final(): pallas(functools.partial(final_kernel, pairs), 'final', [jax.ShapeDtypeSt...  1.68 us
    ppermute x1, starting transfers between devices, from_behind(): lax.ppermute(value, axis, [(source, source + steps) for source in range(l...  1.29 us
    pallas_call x1, Pallas kernels, lay_out(): pallas(lay_kernel, 'lay_out', [whole, whole], in_vmem(len(flat)), in_vmem...  1.23 us
    pallas_call x1, Pallas kernels, fetch(): pallas(fetch_kernel, 'fetch', [jax.ShapeDtypeStruct((held // 2,) + gate_w...  1.17 us
  transfers between devices with their start and end apart: 15, of which 4 were waited for; matrix products, arithmetic and copies ran while one was open for 0% of the time, Pallas kernels for 20%

profile of v8, /device:TPU:0, one launch (start us, length us, event | category | flops | bytes accessed | tf_op | source)
XLA Modules:
  0.0 33.2 jit_solution(7264286288768952863)
XLA Ops:
  0.6 0.9 %cut.1 = bf16[2,2,128,128]{3,2,1,0:T(8,128)(2,1)S(1)} custom-call(bf16[8,2,128,128]{3,2,1,0:T(8,128)(2,1)} %w_ref.3), custom_call_target="tpu_custom_call" | custom-call | tf_op jit(solution)/shard_map/cut/pallas_call | solution.py:161
  1.6 4.1 %collective-permute-start.2 = (bf16[2,2,128,128]{3,2,1,0:T(8,128)(2,1)S(1)}, bf16[2,2,128,128]{3,2,1,0:T(8,128)(2,1)S(1)}, u32[]{:S(2)}, u32[]{:S(2)}) collective-permute-start(bf16[2,2,128,128]{3,2,1,0:T(8,128)(2,1)S(1)} %cut.1), channel_id=1, source_target_pairs={{0,8},{4,12},{8,0},{12,4},{1,9},{5,13},{9,1},{13,5},{2,10},{6,14},... | collective-permute-start | bytes 393224 | tf_op jit(solution)/shard_map/ppermute | solution.py:475
  5.7 1.5 %collective-permute-start = (bf16[1,128,4096]{2,1,0:T(8,128)(2,1)}, bf16[1,128,4096]{2,1,0:T(8,128)(2,1)S(1)}, u32[]{:S(2)}, u32[]{:S(2)}) collective-permute-start(bf16[1,128,4096]{2,1,0:T(8,128)(2,1)} %param.10), channel_id=1, source_target_pairs={{0,16},{16,0},{1,17},{17,1},{2,18},{18,2},{3,19},{19,3},{4,20},{20... | collective-permute-start | bytes 3145736 | tf_op jit(solution)/shard_map/ppermute | solution.py:475
  7.2 0.0 copy-start.1
  7.2 0.0 copy-start
  7.2 0.0 copy-start.2
  7.2 0.0 copy-start.3
  7.2 1.2 %fetch.1 = (bf16[4,2,128,128]{3,2,1,0:T(8,128)(2,1)S(1)}, bf16[16,4096]{1,0:T(8,128)(2,1)S(1)}, s32[1,128]{1,0:T(1,128)S(1)}, f32[4,4096]{1,0:T(4,128)S(1)}, f32[1,4096]{1,0:T(1,128)S(1)}) custom-call(bf16[1,128,4096]{2,1,0:T(8,128)(2,1)} %x_ref.3, bf16[8,2,128,128]{3,2,1,0:T(8,128)(2,1)} %w_ref.3, s32[1,128]{1,0:T(1,128)} %refs_0_.2, f32[4,4096]{1,0:T(4,128)} %refs_1_.1, ...), custom_call_target="tpu_custom_call" | custom-call | flops 1500000000 | tf_op jit(solution)/shard_map/fetch/pallas_call | solution.py:194
  8.4 1.6 %collective-permute-start.6 = (bf16[4,2,128,128]{3,2,1,0:T(8,128)(2,1)S(1)}, bf16[4,2,128,128]{3,2,1,0:T(8,128)(2,1)S(1)}, u32[]{:S(2)}, u32[]{:S(2)}) collective-permute-start(bf16[4,2,128,128]{3,2,1,0:T(8,128)(2,1)S(1)} %get-tuple-element.45), channel_id=1, source_target_pairs={{0,4},{4,0},{8,12},{12,8},{1,5},{5,1},{9,13},{13,9},{2,6},{6,2},{1... | collective-permute-start | bytes 786440 | tf_op jit(solution)/shard_map/ppermute | solution.py:475
  10.0 1.3 %collective-permute-start.1 = (bf16[16,4096]{1,0:T(8,128)(2,1)S(1)}, bf16[16,4096]{1,0:T(8,128)(2,1)S(1)}, u32[]{:S(2)}, u32[]{:S(2)}) collective-permute-start(bf16[16,4096]{1,0:T(8,128)(2,1)S(1)} %get-tuple-element.31), channel_id=1, source_target_pairs={{0,1},{1,2},{2,3},{4,5},{5,6},{6,7},{8,9},{9,10},{10,11},{12,13},{... | collective-permute-start | bytes 393224 | tf_op jit(solution)/shard_map/ppermute | solution.py:42
  11.3 0.3 collective-permute-start.8
  11.6 0.5 %collective-permute-done.2.refs_0_ = bf16[2,2,128,128]{3,2,1,0:T(8,128)(2,1)S(1)} collective-permute-done((bf16[2,2,128,128]{3,2,1,0:T(8,128)(2,1)S(1)}, bf16[2,2,128,128]{3,2,1,0:T(8,128)(2,1)S(1)}, u32[]{:S(2)}, u32[]{:S(2)}) %collective-permute-start.2) | collective-permute-done | bytes 131104 | tf_op jit(solution)/shard_map/ppermute | solution.py:475
  12.1 1.6 %collective-permute-start.3 = (bf16[2,2,128,128]{3,2,1,0:T(8,128)(2,1)S(1)}, bf16[2,2,128,128]{3,2,1,0:T(8,128)(2,1)S(1)}, u32[]{:S(2)}, u32[]{:S(2)}) collective-permute-start(bf16[2,2,128,128]{3,2,1,0:T(8,128)(2,1)S(1)} %collective-permute-done.2.refs_0_), channel_id=1, source_target_pairs={{0,2},{1,3},{2,0},{3,1},{4,6},{5,7},{6,4},{7,5},{8,10},{9,11},{10,... | collective-permute-start | bytes 393224 | tf_op jit(solution)/shard_map/ppermute | solution.py:475
  13.7 0.0 collective-permute-done.1.edge_ref
  13.7 0.0 copy-done.1
  13.7 1.9 %conv_rows.1 = (bf16[32,128,128]{2,1,0:T(8,128)(2,1)S(1)}, f32[2,128,128]{2,1,0:T(8,128)S(1)}) custom-call(bf16[1,128,4096]{2,1,0:T(8,128)(2,1)S(1)} %copy-done.1, bf16[16,4096]{1,0:T(8,128)(2,1)S(1)} %collective-permute-done.1.edge_ref, s32[1,128]{1,0:T(1,128)S(1)} %get-tuple-element.32.pos_ref, f32[4,4096]{1,0:T(4,128)S(1)} %get-tuple-element.33.w_ref, ...), custom_call_target="tpu_custom_call" | custom-call | tf_op jit(solution)/shard_map/conv_rows/pallas_call | solution.py:264
  15.6 2.8 %collective-permute-done.8.refs_0_ = bf16[2,2,128,128]{3,2,1,0:T(8,128)(2,1)S(1)} collective-permute-done((bf16[2,2,128,128]{3,2,1,0:T(8,128)(2,1)S(1)}, bf16[2,2,128,128]{3,2,1,0:T(8,128)(2,1)S(1)}, u32[]{:S(2)}, u32[]{:S(2)}) %collective-permute-start.8) | collective-permute-done | bytes 131104 | tf_op jit(solution)/shard_map/ppermute | solution.py:475
  18.5 1.9 %collective-permute-start.9 = (bf16[2,2,128,128]{3,2,1,0:T(8,128)(2,1)S(1)}, bf16[2,2,128,128]{3,2,1,0:T(8,128)(2,1)S(1)}, u32[]{:S(2)}, u32[]{:S(2)}) collective-permute-start(bf16[2,2,128,128]{3,2,1,0:T(8,128)(2,1)S(1)} %collective-permute-done.8.refs_0_), channel_id=1, source_target_pairs={{0,2},{1,3},{2,0},{3,1},{4,6},{5,7},{6,4},{7,5},{8,10},{9,11},{10,... | collective-permute-start | bytes 393224 | tf_op jit(solution)/shard_map/ppermute | solution.py:475
  20.4 0.0 copy-done
  20.4 0.0 copy-done.2
  20.4 0.0 copy-done.3
  20.4 0.6 %shard.4 = (f32[8,128,128]{2,1,0:T(8,128)S(1)}, f32[8,128,128]{2,1,0:T(8,128)S(1)}, f32[8,2,8,128]{3,2,1,0:T(8,128)S(1)}, f32[16,128]{1,0:T(8,128)S(1)}) custom-call(bf16[32,128,128]{2,1,0:T(8,128)(2,1)S(1)} %get-tuple-element.35.conv_ref, f32[2,128,128]{2,1,0:T(8,128)S(1)} %get-tuple-element.36.mask_ref, f32[2,4096]{1,0:T(2,128)S(1)} %copy-done.2, ...), custom_call_target="tpu_custom_call" | custom-call | tf_op jit(solution)/shard_map/shard/pallas_call | solution.py:352
  21.0 0.0 collective-permute-done.3.refs_2_
  21.0 0.0 collective-permute-done.6.refs_0_
  21.0 0.1 collective-permute-start.7
  21.1 0.5 %collective-permute-start.4 = (bf16[2,2,128,128]{3,2,1,0:T(8,128)(2,1)S(1)}, bf16[2,2,128,128]{3,2,1,0:T(8,128)(2,1)S(1)}, u32[]{:S(2)}, u32[]{:S(2)}) collective-permute-start(bf16[2,2,128,128]{3,2,1,0:T(8,128)(2,1)S(1)} %collective-permute-done.2.refs_0_), channel_id=1, source_target_pairs={{0,1},{1,0},{2,3},{3,2},{4,5},{5,4},{6,7},{7,6},{8,9},{9,8},{10,11... | collective-permute-start | bytes 393224 | tf_op jit(solution)/shard_map/ppermute | solution.py:475
  21.6 0.1 collective-permute-start.5
  21.7 3.1 %collective-permute-done.9.refs_2_ = bf16[2,2,128,128]{3,2,1,0:T(8,128)(2,1)S(1)} collective-permute-done((bf16[2,2,128,128]{3,2,1,0:T(8,128)(2,1)S(1)}, bf16[2,2,128,128]{3,2,1,0:T(8,128)(2,1)S(1)}, u32[]{:S(2)}, u32[]{:S(2)}) %collective-permute-start.9) | collective-permute-done | bytes 131104 | tf_op jit(solution)/shard_map/ppermute | solution.py:475
  24.7 0.2 collective-permute-start.10
  24.9 0.0 collective-permute-done.4.refs_1_
  24.9 0.3 collective-permute-start.11
  25.2 0.0 collective-permute-done.5.refs_3_
  25.2 0.6 %shard.5 = (f32[8,128,128]{2,1,0:T(8,128)S(1)}, f32[8,128,128]{2,1,0:T(8,128)S(1)}, f32[8,2,8,128]{3,2,1,0:T(8,128)S(1)}, f32[16,128]{1,0:T(8,128)S(1)}) custom-call(bf16[32,128,128]{2,1,0:T(8,128)(2,1)S(1)} %get-tuple-element.35.conv_ref, f32[2,128,128]{2,1,0:T(8,128)S(1)} %get-tuple-element.36.mask_ref, f32[2,4096]{1,0:T(2,128)S(1)} %copy-done.2, ...), custom_call_target="tpu_custom_call" | custom-call | tf_op jit(solution)/shard_map/shard/pallas_call | solution.py:352
  25.9 0.0 collective-permute-done.7.refs_1_
  25.9 0.6 %shard.6 = (f32[8,128,128]{2,1,0:T(8,128)S(1)}, f32[8,128,128]{2,1,0:T(8,128)S(1)}, f32[8,2,8,128]{3,2,1,0:T(8,128)S(1)}, f32[16,128]{1,0:T(8,128)S(1)}) custom-call(bf16[32,128,128]{2,1,0:T(8,128)(2,1)S(1)} %get-tuple-element.35.conv_ref, f32[2,128,128]{2,1,0:T(8,128)S(1)} %get-tuple-element.36.mask_ref, f32[2,4096]{1,0:T(2,128)S(1)} %copy-done.2, ...), custom_call_target="tpu_custom_call" | custom-call | tf_op jit(solution)/shard_map/shard/pallas_call | solution.py:352
  26.5 0.0 collective-permute-done.10.refs_1_
  26.5 0.0 collective-permute-done.11.refs_3_
  26.5 0.6 %shard.7 = (f32[8,128,128]{2,1,0:T(8,128)S(1)}, f32[8,128,128]{2,1,0:T(8,128)S(1)}, f32[8,2,8,128]{3,2,1,0:T(8,128)S(1)}, f32[64,128]{1,0:T(8,128)S(1)}) custom-call(bf16[32,128,128]{2,1,0:T(8,128)(2,1)S(1)} %get-tuple-element.35.conv_ref, f32[2,128,128]{2,1,0:T(8,128)S(1)} %get-tuple-element.36.mask_ref, f32[2,4096]{1,0:T(2,128)S(1)} %copy-done.2, ...), custom_call_target="tpu_custom_call" | custom-call | flops 5000000000 | tf_op jit(solution)/shard_map/shard/pallas_call | solution.py:352
  27.1 0.3 collective-permute-start.12
  27.4 0.5 %collective-permute-start.13 = (f32[64,128]{1,0:T(8,128)S(1)}, f32[64,128]{1,0:T(8,128)S(1)}, u32[]{:S(2)}, u32[]{:S(2)}) collective-permute-start(f32[64,128]{1,0:T(8,128)S(1)} %get-tuple-element.59), channel_id=1, source_target_pairs={{0,2},{1,3},{2,0},{3,1},{4,6},{5,7},{6,4},{7,5},{8,10},{9,11},{10,... | collective-permute-start | bytes 98312 | tf_op jit(solution)/shard_map/ppermute | solution.py:475
  27.9 1.2 %collective-permute-start.14 = (f32[64,128]{1,0:T(8,128)S(1)}, f32[64,128]{1,0:T(8,128)S(1)}, u32[]{:S(2)}, u32[]{:S(2)}) collective-permute-start(f32[64,128]{1,0:T(8,128)S(1)} %get-tuple-element.59), channel_id=1, source_target_pairs={{0,3},{1,2},{2,1},{3,0},{4,7},{5,6},{6,5},{7,4},{8,11},{9,10},{10,... | collective-permute-start | bytes 98312 | tf_op jit(solution)/shard_map/ppermute | solution.py:475
  29.0 1.2 %lay_out.1 = (f32[32,128,128]{2,1,0:T(8,128)S(1)}, f32[32,128,128]{2,1,0:T(8,128)S(1)}) custom-call(f32[8,128,128]{2,1,0:T(8,128)S(1)} %get-tuple-element.37.refs_0_, f32[8,128,128]{2,1,0:T(8,128)S(1)} %get-tuple-element.38.refs_1_, f32[8,2,8,128]{3,2,1,0:T(8,128)S(1)} %get-tuple-element.39.refs_2_, f32[8,128,128]{2,1,0:T(8,128)S(1)} %get-tuple-element.42.refs_3_, ...), custom_call_target="tpu_custom_call" | custom-call | tf_op jit(solution)/shard_map/lay_out/pallas_call | solution.py:388
  30.3 0.0 collective-permute-done.12.refs_0_
  30.3 1.3 %collective-permute-done.13.refs_1_ = f32[64,128]{1,0:T(8,128)S(1)} collective-permute-done((f32[64,128]{1,0:T(8,128)S(1)}, f32[64,128]{1,0:T(8,128)S(1)}, u32[]{:S(2)}, u32[]{:S(2)}) %collective-permute-start.13) | collective-permute-done | bytes 32800 | tf_op jit(solution)/shard_map/ppermute | solution.py:475
  31.6 0.0 collective-permute-done.14.refs_2_
  31.6 0.0 collective-permute-done.target_ref
  31.6 1.7 %final.1 = (bf16[1,128,4096]{2,1,0:T(8,128)(2,1)}, f32[1,128]{1,0:T(1,128)}) custom-call(bf16[1,128,4096]{2,1,0:T(8,128)(2,1)S(1)} %collective-permute-done.target_ref, f32[32,128,128]{2,1,0:T(8,128)S(1)} %get-tuple-element.57.state_ref, f32[32,128,128]{2,1,0:T(8,128)S(1)} %get-tuple-element.58.prod_ref, f32[64,128]{1,0:T(8,128)S(1)} %collective-permute-done.12.refs_0_, ...), custom_call_target="tpu_custom_call" | custom-call | tf_op jit(solution)/shard_map/final/pallas_call | solution.py:457
Async XLA Ops:
  1.6 10.5 %collective-permute-start.2 = (bf16[2,2,128,128]{3,2,1,0:T(8,128)(2,1)S(1)}, bf16[2,2,128,128]{3,2,1,0:T(8,128)(2,1)S(1)}, u32[]{:S(2)}, u32[]{:S(2)}) collective-permute-start(bf16[2,2,128,128]{3,2,1,0:T(8,128)(2,1)S(1)} %cut.1), channel_id=1, source_target_pairs={{0,8},{4,12},{8,0},{12,4},{1,9},{5,13},{9,1},{13,5},{2,10},{6,14},... | collective-permute-start | bytes 393224 | tf_op jit(solution)/shard_map/ppermute | solution.py:475
  5.7 25.9 %collective-permute-start = (bf16[1,128,4096]{2,1,0:T(8,128)(2,1)}, bf16[1,128,4096]{2,1,0:T(8,128)(2,1)S(1)}, u32[]{:S(2)}, u32[]{:S(2)}) collective-permute-start(bf16[1,128,4096]{2,1,0:T(8,128)(2,1)} %param.10), channel_id=1, source_target_pairs={{0,16},{16,0},{1,17},{17,1},{2,18},{18,2},{3,19},{19,3},{4,20},{20... | collective-permute-start | bytes 3145736 | tf_op jit(solution)/shard_map/ppermute | solution.py:475
  7.2 6.5 %copy-start.1 = (bf16[1,128,4096]{2,1,0:T(8,128)(2,1)S(1)}, bf16[1,128,4096]{2,1,0:T(8,128)(2,1)}, u32[]{:S(2)}) copy-start(bf16[1,128,4096]{2,1,0:T(8,128)(2,1)} %x_ref.3) | copy-start | bytes 3145732
  7.2 13.2 %copy-start = (bf16[8,2,128,128]{3,2,1,0:T(8,128)(2,1)S(1)}, bf16[8,2,128,128]{3,2,1,0:T(8,128)(2,1)}, u32[]{:S(2)}) copy-start(bf16[8,2,128,128]{3,2,1,0:T(8,128)(2,1)} %w_ref.3) | copy-start | bytes 1572868
  7.2 13.2 %copy-start.2 = (f32[2,4096]{1,0:T(2,128)S(1)}, f32[2,4096]{1,0:T(2,128)}, u32[]{:S(2)}) copy-start(f32[2,4096]{1,0:T(2,128)} %bias_ref.7) | copy-start | bytes 98308
  7.2 13.2 %copy-start.3 = (f32[4096]{0:T(1024)S(1)}, f32[4096]{0:T(1024)}, u32[]{:S(2)}) copy-start(f32[4096]{0:T(1024)} %param.15) | copy-start | bytes 49156
  8.4 12.6 %collective-permute-start.6 = (bf16[4,2,128,128]{3,2,1,0:T(8,128)(2,1)S(1)}, bf16[4,2,128,128]{3,2,1,0:T(8,128)(2,1)S(1)}, u32[]{:S(2)}, u32[]{:S(2)}) collective-permute-start(bf16[4,2,128,128]{3,2,1,0:T(8,128)(2,1)S(1)} %get-tuple-element.45), channel_id=1, source_target_pairs={{0,4},{4,0},{8,12},{12,8},{1,5},{5,1},{9,13},{13,9},{2,6},{6,2},{1... | collective-permute-start | bytes 786440 | tf_op jit(solution)/shard_map/ppermute | solution.py:475
  10.0 3.7 %collective-permute-start.1 = (bf16[16,4096]{1,0:T(8,128)(2,1)S(1)}, bf16[16,4096]{1,0:T(8,128)(2,1)S(1)}, u32[]{:S(2)}, u32[]{:S(2)}) collective-permute-start(bf16[16,4096]{1,0:T(8,128)(2,1)S(1)} %get-tuple-element.31), channel_id=1, source_target_pairs={{0,1},{1,2},{2,3},{4,5},{5,6},{6,7},{8,9},{9,10},{10,11},{12,13},{... | collective-permute-start | bytes 393224 | tf_op jit(solution)/shard_map/ppermute | solution.py:42
  11.3 7.2 %collective-permute-start.8 = (bf16[2,2,128,128]{3,2,1,0:T(8,128)(2,1)S(1)}, bf16[2,2,128,128]{3,2,1,0:T(8,128)(2,1)S(1)}, u32[]{:S(2)}, u32[]{:S(2)}) collective-permute-start(bf16[2,2,128,128]{3,2,1,0:T(8,128)(2,1)S(1)} %cut.1), channel_id=1, source_target_pairs={{0,12},{4,8},{8,4},{12,0},{1,13},{5,9},{9,5},{13,1},{2,14},{6,10},... | collective-permute-start | bytes 393224 | tf_op jit(solution)/shard_map/ppermute | solution.py:475
  12.1 8.9 %collective-permute-start.3 = (bf16[2,2,128,128]{3,2,1,0:T(8,128)(2,1)S(1)}, bf16[2,2,128,128]{3,2,1,0:T(8,128)(2,1)S(1)}, u32[]{:S(2)}, u32[]{:S(2)}) collective-permute-start(bf16[2,2,128,128]{3,2,1,0:T(8,128)(2,1)S(1)} %collective-permute-done.2.refs_0_), channel_id=1, source_target_pairs={{0,2},{1,3},{2,0},{3,1},{4,6},{5,7},{6,4},{7,5},{8,10},{9,11},{10,... | collective-permute-start | bytes 393224 | tf_op jit(solution)/shard_map/ppermute | solution.py:475
  18.5 6.3 %collective-permute-start.9 = (bf16[2,2,128,128]{3,2,1,0:T(8,128)(2,1)S(1)}, bf16[2,2,128,128]{3,2,1,0:T(8,128)(2,1)S(1)}, u32[]{:S(2)}, u32[]{:S(2)}) collective-permute-start(bf16[2,2,128,128]{3,2,1,0:T(8,128)(2,1)S(1)} %collective-permute-done.8.refs_0_), channel_id=1, source_target_pairs={{0,2},{1,3},{2,0},{3,1},{4,6},{5,7},{6,4},{7,5},{8,10},{9,11},{10,... | collective-permute-start | bytes 393224 | tf_op jit(solution)/shard_map/ppermute | solution.py:475
  21.0 4.9 %collective-permute-start.7 = (bf16[4,2,128,128]{3,2,1,0:T(8,128)(2,1)S(1)}, bf16[4,2,128,128]{3,2,1,0:T(8,128)(2,1)S(1)}, u32[]{:S(2)}, u32[]{:S(2)}) collective-permute-start(bf16[4,2,128,128]{3,2,1,0:T(8,128)(2,1)S(1)} %collective-permute-done.6.refs_0_), channel_id=1, source_target_pairs={{0,1},{1,0},{2,3},{3,2},{4,5},{5,4},{6,7},{7,6},{8,9},{9,8},{10,11... | collective-permute-start | bytes 786440 | tf_op jit(solution)/shard_map/ppermute | solution.py:475
  21.1 3.9 %collective-permute-start.4 = (bf16[2,2,128,128]{3,2,1,0:T(8,128)(2,1)S(1)}, bf16[2,2,128,128]{3,2,1,0:T(8,128)(2,1)S(1)}, u32[]{:S(2)}, u32[]{:S(2)}) collective-permute-start(bf16[2,2,128,128]{3,2,1,0:T(8,128)(2,1)S(1)} %collective-permute-done.2.refs_0_), channel_id=1, source_target_pairs={{0,1},{1,0},{2,3},{3,2},{4,5},{5,4},{6,7},{7,6},{8,9},{9,8},{10,11... | collective-permute-start | bytes 393224 | tf_op jit(solution)/shard_map/ppermute | solution.py:475
  21.6 3.7 %collective-permute-start.5 = (bf16[2,2,128,128]{3,2,1,0:T(8,128)(2,1)S(1)}, bf16[2,2,128,128]{3,2,1,0:T(8,128)(2,1)S(1)}, u32[]{:S(2)}, u32[]{:S(2)}) collective-permute-start(bf16[2,2,128,128]{3,2,1,0:T(8,128)(2,1)S(1)} %collective-permute-done.3.refs_2_), channel_id=1, source_target_pairs={{0,1},{1,0},{2,3},{3,2},{4,5},{5,4},{6,7},{7,6},{8,9},{9,8},{10,11... | collective-permute-start | bytes 393224 | tf_op jit(solution)/shard_map/ppermute | solution.py:475
  24.7 1.8 %collective-permute-start.10 = (bf16[2,2,128,128]{3,2,1,0:T(8,128)(2,1)S(1)}, bf16[2,2,128,128]{3,2,1,0:T(8,128)(2,1)S(1)}, u32[]{:S(2)}, u32[]{:S(2)}) collective-permute-start(bf16[2,2,128,128]{3,2,1,0:T(8,128)(2,1)S(1)} %collective-permute-done.8.refs_0_), channel_id=1, source_target_pairs={{0,1},{1,0},{2,3},{3,2},{4,5},{5,4},{6,7},{7,6},{8,9},{9,8},{10,11... | collective-permute-start | bytes 393224 | tf_op jit(solution)/shard_map/ppermute | solution.py:475
  24.9 1.5 %collective-permute-start.11 = (bf16[2,2,128,128]{3,2,1,0:T(8,128)(2,1)S(1)}, bf16[2,2,128,128]{3,2,1,0:T(8,128)(2,1)S(1)}, u32[]{:S(2)}, u32[]{:S(2)}) collective-permute-start(bf16[2,2,128,128]{3,2,1,0:T(8,128)(2,1)S(1)} %collective-permute-done.9.refs_2_), channel_id=1, source_target_pairs={{0,1},{1,0},{2,3},{3,2},{4,5},{5,4},{6,7},{7,6},{8,9},{9,8},{10,11... | collective-permute-start | bytes 393224 | tf_op jit(solution)/shard_map/ppermute | solution.py:475
  27.1 3.2 %collective-permute-start.12 = (f32[64,128]{1,0:T(8,128)S(1)}, f32[64,128]{1,0:T(8,128)S(1)}, u32[]{:S(2)}, u32[]{:S(2)}) collective-permute-start(f32[64,128]{1,0:T(8,128)S(1)} %get-tuple-element.59), channel_id=1, source_target_pairs={{0,1},{1,0},{2,3},{3,2},{4,5},{5,4},{6,7},{7,6},{8,9},{9,8},{10,11... | collective-permute-start | bytes 98312 | tf_op jit(solution)/shard_map/ppermute | solution.py:475
  27.4 4.2 %collective-permute-start.13 = (f32[64,128]{1,0:T(8,128)S(1)}, f32[64,128]{1,0:T(8,128)S(1)}, u32[]{:S(2)}, u32[]{:S(2)}) collective-permute-start(f32[64,128]{1,0:T(8,128)S(1)} %get-tuple-element.59), channel_id=1, source_target_pairs={{0,2},{1,3},{2,0},{3,1},{4,6},{5,7},{6,4},{7,5},{8,10},{9,11},{10,... | collective-permute-start | bytes 98312 | tf_op jit(solution)/shard_map/ppermute | solution.py:475
  27.9 3.7 %collective-permute-start.14 = (f32[64,128]{1,0:T(8,128)S(1)}, f32[64,128]{1,0:T(8,128)S(1)}, u32[]{:S(2)}, u32[]{:S(2)}) collective-permute-start(f32[64,128]{1,0:T(8,128)S(1)} %get-tuple-element.59), channel_id=1, source_target_pairs={{0,3},{1,2},{2,1},{3,0},{4,7},{5,6},{6,5},{7,4},{8,11},{9,10},{10,... | collective-permute-start | bytes 98312 | tf_op jit(solution)/shard_map/ppermute | solution.py:475
